TPU v7x, 32 devices: a whole 2x2x4 slice. The times are simulated.
32 devices in a mesh: expert: 8 (over z, y), dp: 4 (over x, core).
Axes of the slice: x: 2, y: 2, z: 4, core: 2. Of those that a mesh axis runs over, the one named last changes fastest.
Arguments:
- tokens: bfloat16 [1024, 3584], P('expert', 'dp'), may hold values from -6 to 6
- expert_ids: int32 [1024, 8], P('expert'), may hold values from 0 to 15, as said below
- gate_weights: float32 [1024, 8], P('expert'), may hold values from 0.05 to 0.5
- replica_plan: int32 [8], replicated, may hold values from 0 to 15, as said below
- w_gate: bfloat16 [16, 3584, 1024], P('expert', None, 'dp'), may hold values from -0.09375 to 0.09375
- w_up: bfloat16 [16, 3584, 1024], P('expert', None, 'dp'), may hold values from -0.09375 to 0.09375
- w_down: bfloat16 [16, 1024, 3584], P('expert', 'dp'), may hold values from -0.1875 to 0.1875
Outputs:
- mixed_out: bfloat16 [1024, 3584], P('expert', 'dp')
Inputs may be any that keep to these rules, and one draw needn't show every extreme that they name: `expert_ids`: each row names 8 different experts; one expert, which varies with the draw, is named by every row. `replica_plan`: entry j names one of the 2 experts owned by index (j + 4) % 8 of the expert axis, that is, an expert from k * 2 to k * 2 + 1 with that index k.
All inputs are finite; a program needn't handle non-finite values.
Results may differ from a plain program's by a relative error of at most 0.012.
Values may be sent and summed in bfloat16 or wider, within the bound.
No kernel may reach another device: no remote copies, remote signals or barrier semaphores. Data moves between devices by JAX's collectives and lax.ppermute only.
A program may use at most 128 MiB of HBM per device.

v0:
```python
import jax
import jax.numpy as jnp
from jax import lax
from jax.sharding import PartitionSpec as P

CAP = 8


def passed_along(value, axis, steps):
    count = lax.axis_size(axis)
    pairs = [(source, (source + steps) % count) for source in range(count)]
    return lax.ppermute(value, axis, pairs)


def expert_block(slot_rows, gate_piece, up_piece, down_piece):
    gate_value = jnp.dot(slot_rows, gate_piece, preferred_element_type=jnp.float32)
    up_value = jnp.dot(slot_rows, up_piece, preferred_element_type=jnp.float32)
    hidden = (jax.nn.silu(gate_value) * up_value).astype(jnp.bfloat16)
    return jnp.dot(hidden, down_piece, preferred_element_type=jnp.float32).astype(jnp.bfloat16)


def per_device(tokens, expert_ids, gate_weights, replica_plan, w_gate, w_up, w_down):
    owners = lax.axis_size("expert")
    own_index = lax.axis_index("expert")
    owned_count = w_gate.shape[0]
    host_slots = owned_count + 1
    experts = owned_count * owners
    tok_rows = tokens.shape[0]
    choose_count = expert_ids.shape[1]
    feature_share = tokens.shape[1]
    model_width = feature_share * lax.axis_size("dp")
    flat_ids = expert_ids.reshape(-1)
    assigned = flat_ids.shape[0]
    expert_range = jnp.arange(experts, dtype=jnp.int32)
    onehot = (flat_ids[:, None] == expert_range[None, :]).astype(jnp.int32)
    earlier = jnp.cumsum(onehot, axis=0) - onehot
    row_rank = jnp.sum(earlier * onehot, axis=1)
    hosted = (replica_plan[:, None] == expert_range[None, :]).astype(jnp.int32)
    copies = 1 + jnp.sum(hosted, axis=0)
    host_of = jnp.sum(jnp.arange(owners, dtype=jnp.int32)[:, None] * hosted, axis=0)
    my_copies = jnp.sum(onehot * copies[None, :], axis=1)
    my_host = jnp.sum(onehot * host_of[None, :], axis=1)
    copy_index = row_rank % my_copies
    position = row_rank // my_copies
    is_kept = position < CAP
    target = jnp.where(copy_index == 0, flat_ids // owned_count, my_host)
    target_slot = jnp.where(copy_index == 0, flat_ids % owned_count, owned_count)
    buffer_rows = owners * host_slots * CAP
    slot_place = jnp.where(
        is_kept, (target * host_slots + target_slot) * CAP + position, buffer_rows
    )
    token_of = jnp.arange(assigned, dtype=jnp.int32) // choose_count
    source = jnp.full((buffer_rows,), tok_rows, jnp.int32).at[slot_place].set(token_of, mode="drop")
    half_way = owners // 2
    receiver = (own_index + half_way) % owners
    local_pick = replica_plan[receiver] - own_index * owned_count
    outgoing_weights = (
        lax.dynamic_index_in_dim(w_gate, local_pick, 0, keepdims=False),
        lax.dynamic_index_in_dim(w_up, local_pick, 0, keepdims=False),
        lax.dynamic_index_in_dim(w_down, local_pick, 0, keepdims=False),
    )
    padded = jnp.concatenate([tokens, jnp.zeros((1, feature_share), jnp.bfloat16)], axis=0)
    outgoing = padded[source].reshape(owners, host_slots * CAP, feature_share)
    quarter = lax.all_to_all(outgoing, "expert", split_axis=0, concat_axis=0, tiled=True)
    arrived = lax.all_gather(quarter, "dp", axis=2, tiled=True)
    arrived = arrived.reshape(owners, host_slots, CAP, model_width)
    guest_gate, guest_up, guest_down = passed_along(
        (outgoing_weights[0], outgoing_weights[1], outgoing_weights[2]), "expert", half_way
    )
    results = []
    for slot_number in range(host_slots):
        slot_rows = arrived[:, slot_number].reshape(owners * CAP, model_width)
        if slot_number < owned_count:
            block_out = expert_block(
                slot_rows, w_gate[slot_number], w_up[slot_number], w_down[slot_number]
            )
        else:
            block_out = expert_block(slot_rows, guest_gate, guest_up, guest_down)
        results.append(block_out.reshape(owners, CAP, model_width))
    partials = jnp.stack(results, axis=1).reshape(owners, host_slots * CAP, model_width)
    weights_kept = jnp.where(is_kept, gate_weights.reshape(-1), 0.0)
    lookup = jnp.minimum(slot_place, buffer_rows - 1)
    returned = lax.all_to_all(partials, "expert", split_axis=0, concat_axis=0, tiled=True).reshape(
        buffer_rows, model_width
    )
    picked = returned[lookup].astype(jnp.float32) * weights_kept[:, None]
    combined = jnp.sum(picked.reshape(tok_rows, choose_count, model_width), axis=1)
    mixed_out = lax.psum_scatter(
        combined.astype(jnp.bfloat16), "dp", scatter_dimension=1, tiled=True
    )
    return mixed_out


def solution(mesh):
    in_specs = (
        P("expert", "dp"),
        P("expert", None),
        P("expert", None),
        P(),
        P("expert", None, "dp"),
        P("expert", None, "dp"),
        P("expert", "dp", None),
    )
    out_specs = P("expert", "dp")
    return jax.shard_map(
        per_device, mesh=mesh, in_specs=in_specs, out_specs=out_specs, check_vma=False
    )
```

profile of v0, /device:TPU:0, one launch (start us, length us, event | category | flops | bytes accessed | tf_op | source)
XLA Modules:
  0.0 372.9 jit_solution(8395977235913745759)
XLA Ops:
  7.6 4.5 %reduce-window.6 = s32[16,8,128]{2,1,0:T(8,128)S(1)} reduce-window(s32[16,8,128]{2,1,0:T(8,128)S(1)} %fusion.51, s32[]{:T(128)} %constant.92.clone.1), window={size=1x1x128 pad=0_0x0_0x127_0}, to_apply=%region_0.0 | reduce-window | flops 2080768 | bytes 131076 | tf_op jit(solution)/shard_map/reduce-window
  14.2 4.3 %scatter_custom_fusion = s32[192]{0:T(256)S(1)} fusion(s32[1024]{0:T(1024)S(1)} %bitcast.119, s32[1024]{0:T(1024)S(1)} %add_select_fusion.1, s32[]{:T(128)} %constant.91.clone.1), kind=kCustom, calls=%fused_computation.98 | custom fusion | bytes 772 | tf_op jit(solution)/shard_map/scatter | solution.py:53
  20.5 18.4 %all_to_all.10 = bf16[8,24,896]{2,1,0:T(8,128)(2,1)} all-to-all(bf16[8,24,896]{2,1,0:T(8,128)(2,1)S(1)} %bitcast.105), channel_id=1, replica_groups=mesh['expert'=8,'dp'=4] {'expert'}, dimensions={0} | all-to-all | bytes 688128 | tf_op jit(solution)/shard_map/all_to_all | solution.py:64
  40.2 3.1 dynamic-slice_bitcast_fusion.1
  44.0 1.4 dynamic-slice_bitcast_fusion.2
  45.4 2.1 collective-permute-start
  47.6 1.3 dynamic-slice_bitcast_fusion
  49.7 6.4 %all-gather.2.cloned.1.call-done = bf16[8,24,3584]{2,1,0:T(8,128)(2,1)} async-done(((bf16[8,24,896]{2,1,0:T(8,128)(2,1)}), bf16[8,24,3584]{2,1,0:T(8,128)(2,1)}) %all-gather.2.cloned.1.call-update) | async-done | bytes 1376272 | tf_op jit(solution)/shard_map/all_gather | solution.py:65
  56.1 2.2 fusion.12
  58.3 1.9 fusion.7
  60.2 142.2 %collective-permute-done.1 = bf16[3584,256]{1,0:T(8,128)(2,1)} collective-permute-done((bf16[3584,256]{1,0:T(8,128)(2,1)}, bf16[3584,256]{1,0:T(8,128)(2,1)}, u32[]{:S(2)}, u32[]{:S(2)}) %collective-permute-start.1) | collective-permute-done | bytes 1835040 | tf_op jit(solution)/shard_map/ppermute | solution.py:12
  202.4 1.9 fusion.36
  204.3 4.1 %fusion.1 = bf16[8,1,8,3584]{3,2,1,0:T(8,128)(2,1)} fusion(bf16[2,256,3584]{2,1,0:T(8,128)(2,1)} %param.13, bf16[2,3584,256]{2,1,0:T(8,128)(2,1)} %param.12, bf16[8,3,8,3584]{3,2,1,0:T(8,128)(2,1)S(1)} %bitcast.110, f32[64,256]{1,0:T(8,128)S(1)} %fusion.12), kind=kOutput, calls=%fused_computation.8 | convolution fusion | flops 235208704 | bytes 4653056 | tf_op jit(solution)/shard_map/dot_general | solution.py:19
  208.4 4.1 %fusion.2 = bf16[8,1,8,3584]{3,2,1,0:T(8,128)(2,1)} fusion(bf16[2,256,3584]{2,1,0:T(8,128)(2,1)} %param.13, bf16[2,3584,256]{2,1,0:T(8,128)(2,1)} %param.12, bf16[8,3,8,3584]{3,2,1,0:T(8,128)(2,1)S(1)} %bitcast.111, f32[64,256]{1,0:T(8,128)S(1)} %fusion.7), kind=kOutput, calls=%fused_computation.9 | convolution fusion | flops 235208704 | bytes 4653056 | tf_op jit(solution)/shard_map/dot_general | solution.py:19
  212.5 29.1 %collective-permute-done = bf16[3584,256]{1,0:T(8,128)(2,1)S(1)} collective-permute-done((bf16[3584,256]{1,0:T(8,128)(2,1)}, bf16[3584,256]{1,0:T(8,128)(2,1)S(1)}, u32[]{:S(2)}, u32[]{:S(2)}) %collective-permute-start) | collective-permute-done | bytes 1835040 | tf_op jit(solution)/shard_map/ppermute | solution.py:12
  241.6 38.9 %collective-permute-done.2 = bf16[256,3584]{1,0:T(8,128)(2,1)} collective-permute-done((bf16[256,3584]{1,0:T(8,128)(2,1)}, bf16[256,3584]{1,0:T(8,128)(2,1)}, u32[]{:S(2)}, u32[]{:S(2)}) %collective-permute-start.2) | collective-permute-done | bytes 1835040 | tf_op jit(solution)/shard_map/ppermute | solution.py:12
  280.5 2.9 fusion.3
  284.7 4.9 %all-to-all-start.1 = ((bf16[8,24,3584]{2,1,0:T(8,128)(2,1)}), bf16[8,24,3584]{2,1,0:T(8,128)(2,1)S(1)}, u32[]{:S(2)}, u32[]{:S(2)}) async-start(bf16[8,24,3584]{2,1,0:T(8,128)(2,1)} %maximum_bitcast_fusion), calls=%async_computation.1 | async-start | bytes 2752512 | tf_op jit(solution)/shard_map/all_to_all | solution.py:83
  290.5 32.0 %all-to-all-done.1 = bf16[8,24,3584]{2,1,0:T(8,128)(2,1)S(1)} async-done(((bf16[8,24,3584]{2,1,0:T(8,128)(2,1)}), bf16[8,24,3584]{2,1,0:T(8,128)(2,1)S(1)}, u32[]{:S(2)}, u32[]{:S(2)}) %all-to-all-start.1) | async-done | bytes 1376288 | tf_op jit(solution)/shard_map/all_to_all | solution.py:83
  322.6 7.3 %gather_fusion.1 = bf16[1024,3584]{1,0:T(8,128)(2,1)} fusion(bf16[192,3584]{1,0:T(8,128)(2,1)S(1)} %bitcast.103, s32[1024]{0:T(1024)S(1)} %broadcast_clamp_fusion), kind=kCustom, calls=%fused_computation.1 | custom fusion | bytes 14684160 | tf_op jit(solution)/shard_map/gather | solution.py:86
  329.9 9.8 %fusion = bf16[128,3584]{1,0:T(8,128)(2,1)S(1)} fusion(bf16[1024,3584]{1,0:T(8,128)(2,1)} %gather_fusion.1, f32[128,8]{1,0:T(8,128)S(1)} %copy.55), kind=kLoop, calls=%fused_computation.4 | loop fusion | flops 10551296 | bytes 8261632 | tf_op jit(solution)/shard_map/reduce_sum | solution.py:87
  339.7 1.3 copy.56
  341.0 23.3 %reduce-scatter.4.cloned.1.call-done = bf16[896,128]{1,0:T(8,128)(2,1)} async-done(((bf16[3584,128]{1,0:T(8,128)(2,1)}), bf16[896,128]{1,0:T(8,128)(2,1)}) %reduce-scatter.4.cloned.1.call-update) | async-done | bytes 229392
  364.3 1.8 copy.57
  (52 shorter events, 9.4 us)
Async XLA Ops:
  6.5 49.6 %all-gather.2.cloned.1.call-start = ((), (), s32[]{:S(2)}) async-start(), calls=%async_computation.3 | async-start | bytes 1720320 | tf_op jit(solution)/shard_map/all_gather | solution.py:65
  19.5 19.5 %copy-start.6 = (s32[8]{0:T(128)S(1)}, s32[8]{0:T(128)}, u32[]{:S(2)}) copy-start(s32[8]{0:T(128)} %param.10) | copy-start | bytes 100
  40.2 3.9 %copy-start = (bf16[2,3584,256]{2,1,0:T(8,128)(2,1)S(1)}, bf16[2,3584,256]{2,1,0:T(8,128)(2,1)}, u32[]{:S(2)}) copy-start(bf16[2,3584,256]{2,1,0:T(8,128)(2,1)} %param.11) | copy-start | bytes 11010052
  43.3 4.3 %copy-start.1 = (bf16[2,256,3584]{2,1,0:T(8,128)(2,1)S(1)}, bf16[2,256,3584]{2,1,0:T(8,128)(2,1)}, u32[]{:S(2)}) copy-start(bf16[2,256,3584]{2,1,0:T(8,128)(2,1)} %param.13) | copy-start | bytes 11010052
  43.3 159.2 %collective-permute-start.1 = (bf16[3584,256]{1,0:T(8,128)(2,1)}, bf16[3584,256]{1,0:T(8,128)(2,1)}, u32[]{:S(2)}, u32[]{:S(2)}) collective-permute-start(bf16[3584,256]{1,0:T(8,128)(2,1)} %dynamic-slice_bitcast_fusion.1), channel_id=1, source_target_pairs={{0,16},{4,20},{8,24},{12,28},{16,0},{20,4},{24,8},{28,12},{1,17},{... | collective-permute-start | bytes 5505032 | tf_op jit(solution)/shard_map/ppermute | solution.py:12
  45.4 196.2 %collective-permute-start = (bf16[3584,256]{1,0:T(8,128)(2,1)}, bf16[3584,256]{1,0:T(8,128)(2,1)S(1)}, u32[]{:S(2)}, u32[]{:S(2)}) collective-permute-start(bf16[3584,256]{1,0:T(8,128)(2,1)} %dynamic-slice_bitcast_fusion.2), channel_id=1, source_target_pairs={{0,16},{4,20},{8,24},{12,28},{16,0},{20,4},{24,8},{28,12},{1,17},{... | collective-permute-start | bytes 5505032 | tf_op jit(solution)/shard_map/ppermute | solution.py:12
  48.9 231.6 %collective-permute-start.2 = (bf16[256,3584]{1,0:T(8,128)(2,1)}, bf16[256,3584]{1,0:T(8,128)(2,1)}, u32[]{:S(2)}, u32[]{:S(2)}) collective-permute-start(bf16[256,3584]{1,0:T(8,128)(2,1)} %dynamic-slice_bitcast_fusion), channel_id=1, source_target_pairs={{0,16},{4,20},{8,24},{12,28},{16,0},{20,4},{24,8},{28,12},{1,17},{... | collective-permute-start | bytes 5505032 | tf_op jit(solution)/shard_map/ppermute | solution.py:12
  56.1 2.2 copy-start.2
  212.5 70.9 %copy-start.3 = (bf16[8,1,8,3584]{3,2,1,0:T(8,128)(2,1)S(1)}, bf16[8,1,8,3584]{3,2,1,0:T(8,128)(2,1)}, u32[]{:S(2)}) copy-start(bf16[8,1,8,3584]{3,2,1,0:T(8,128)(2,1)} %fusion.1) | copy-start | bytes 1376260
  212.5 70.9 %copy-start.4 = (bf16[8,1,8,3584]{3,2,1,0:T(8,128)(2,1)S(1)}, bf16[8,1,8,3584]{3,2,1,0:T(8,128)(2,1)}, u32[]{:S(2)}) copy-start(bf16[8,1,8,3584]{3,2,1,0:T(8,128)(2,1)} %fusion.2) | copy-start | bytes 1376260
  284.7 5.7 %copy-start.5 = (f32[128,8]{0,1:T(8,128)S(1)}, f32[128,8]{0,1:T(8,128)}, u32[]{:S(2)}) copy-start(f32[128,8]{0,1:T(8,128)} %param.9) | copy-start | bytes 12292
  284.7 37.9 %all-to-all-start.1 = ((bf16[8,24,3584]{2,1,0:T(8,128)(2,1)}), bf16[8,24,3584]{2,1,0:T(8,128)(2,1)S(1)}, u32[]{:S(2)}, u32[]{:S(2)}) async-start(bf16[8,24,3584]{2,1,0:T(8,128)(2,1)} %maximum_bitcast_fusion), calls=%async_computation.1 | async-start | bytes 2752512 | tf_op jit(solution)/shard_map/all_to_all | solution.py:83
  289.6 74.7 %reduce-scatter.4.cloned.1.call-start = ((), (), s32[]{:S(2)}) async-start(), calls=%async_computation.4 | async-start | bytes 1146880
Sparse Core Ops, SparseCore 0:
  39.0 17.0 all-gather.1
  341.1 23.0 reduce-scatter.3
where the time goes:
time: 373 us
  waiting for transfers between devices  272 us (73%)
  local copies, waits for them, and re-layouts  24.8 us (7%)
  blocking collectives  18.4 us (5%)
  other arithmetic  17.6 us (5%)
  matrix products  17.2 us (5%)
  between operations  14.3 us (4%)
  starting transfers between devices  8.82 us (2%)
    ppermute x3, waiting for transfers between devices, passed_along(): return lax.ppermute(value, axis, pairs)  210 us
    all_to_all x1, waiting for transfers between devices, per_device(): lax.all_to_all(partials, 'expert', split_axis=0, concat_axis=0, tiled=True)  32 us
    unnamed x3, waiting for transfers between devices  23.3 us
    all_to_all x1, blocking collectives, per_device(): lax.all_to_all(outgoing, 'expert', split_axis=0, concat_axis=0, tiled=True)  18.4 us
    dot_general x3, matrix products, expert_block(): jnp.dot(hidden, down_piece, preferred_element_type=jnp.float32)  11.1 us
    reduce_sum x1, other arithmetic, per_device(): jnp.sum(picked.reshape(tok_rows, choose_count, model_width), axis=1)  9.8 us
  transfers between devices with their start and end apart: 6, of which 6 were waited for; matrix products, arithmetic and copies ran while one was open for 6% of the time, Pallas kernels for 0%

commit v1 on v0

v1 whole, which is shorter than its diff:
```python
import functools

import jax
import jax.numpy as jnp
from jax import lax
from jax.experimental import pallas as pl
from jax.experimental.pallas import tpu as pltpu
from jax.sharding import PartitionSpec as P

CAP = 8
F32 = jnp.float32
BF16 = jnp.bfloat16
VMEM = pl.BlockSpec(memory_space=pltpu.VMEM)
SMEM = pl.BlockSpec(memory_space=pltpu.SMEM)
LIMIT = 40 * 2**20


def dot(left, right):
    return jnp.dot(left, right, preferred_element_type=F32)


def dot_rows(left, right, precision=None):
    return lax.dot_general(
        left, right, (((0,), (0,)), ((), ())), precision=precision, preferred_element_type=F32
    )


def route_kernel(owned, plan, ids, gates, tokens, outgoing, mix_high, mix_low):
    tok_rows, choices = ids.shape
    share = tokens.shape[1]
    owners = plan.shape[0]
    experts = owners * owned
    row = lax.broadcasted_iota(jnp.int32, (tok_rows, tok_rows), 0)
    col = lax.broadcasted_iota(jnp.int32, (tok_rows, tok_rows), 1)
    same = (row == col).astype(F32)
    earlier = (row < col).astype(BF16)
    ids_t = dot_rows(ids[...].astype(F32).astype(BF16), same.astype(BF16)).astype(jnp.int32)
    gates_t = dot_rows(gates[...], same, lax.Precision.HIGHEST)
    expert = lax.broadcasted_iota(jnp.int32, (experts, tok_rows), 0)
    named = jnp.zeros((experts, tok_rows), F32)
    weight = jnp.zeros((experts, tok_rows), F32)
    for choice in range(choices):
        hit = expert == ids_t[choice : choice + 1, :]
        named = named + hit.astype(F32)
        weight = weight + jnp.where(hit, gates_t[choice : choice + 1, :], 0.0)
    rank = dot(named.astype(BF16), earlier)
    owner = expert // owned
    within = expert - owner * owned
    hot = jnp.zeros((experts, tok_rows), jnp.int32)
    for host in range(owners):
        source = (host + owners // 2) % owners
        hot = jnp.where(owner == source, plan[host] - source * owned, hot)
    limit = jnp.where(within == hot, 2 * CAP, CAP)
    start = jnp.where(within == hot, 0, CAP * (1 + within + (within < hot).astype(jnp.int32)))
    rank = rank.astype(jnp.int32)
    place = jnp.where((named > 0.0) & (rank < limit), start + rank, -1)
    slot = lax.broadcasted_iota(jnp.int32, (CAP, tok_rows), 0)
    for chunk in range(owned + 1):
        picks, mixes = [], []
        for index in range(owners):
            pick = jnp.zeros((CAP, tok_rows), F32)
            mix = jnp.zeros((CAP, tok_rows), F32)
            for number in range(index * owned, (index + 1) * owned):
                match = place[number : number + 1, :] == slot + chunk * CAP
                pick = pick + match.astype(F32)
                mix = mix + jnp.where(match, weight[number : number + 1, :], 0.0)
            picks.append(pick)
            mixes.append(mix)
        pick = jnp.concatenate(picks, axis=0).astype(BF16)
        mix = jnp.concatenate(mixes, axis=0)
        outgoing[:, chunk * share : (chunk + 1) * share] = dot(pick, tokens[...]).astype(BF16)
        high = mix.astype(BF16)
        mix_high[chunk] = high
        mix_low[chunk] = (mix - high.astype(F32)).astype(BF16)


def groups_of(owned):
    return [(0, 1)] + [(number + 1,) for number in range(1, owned)]


def chunk_rows(block, chunks, share):
    return jnp.concatenate(
        [block[:, chunk * share : (chunk + 1) * share] for chunk in chunks], axis=0
    )


def projections(order, features, blocks, gate, up, group, chunks):
    share = blocks[0].shape[1] // (gate.shape[0] + 1)
    pick = order[group]
    gate_value = up_value = None
    for number, block in enumerate(blocks):
        rows = chunk_rows(block, chunks, share)
        place = pl.ds(pl.multiple_of(features[number] * share, share), share)
        gate_part = dot(rows, gate[pick, place, :])
        up_part = dot(rows, up[pick, place, :])
        gate_value = gate_part if gate_value is None else gate_value + gate_part
        up_value = up_part if up_value is None else up_value + up_part
    return gate_value, up_value


def near_kernel(count, order, features, *refs):
    blocks, (gate, up, gate_out, up_out) = refs[:count], refs[count:]
    lines = blocks[0].shape[0]
    for group, chunks in enumerate(groups_of(gate.shape[0])):
        gate_value, up_value = projections(order, features, blocks, gate, up, group, chunks)
        place = slice(chunks[0] * lines, (chunks[-1] + 1) * lines)
        gate_out[place, :] = gate_value
        up_out[place, :] = up_value


def down_parts(order, features, hidden, down, outs, lines):
    owned = down.shape[0]
    share = outs[0].shape[1] // (owned + 1)
    for number, out in enumerate(outs):
        place = pl.ds(pl.multiple_of(features[number] * share, share), share)
        for group, chunks in enumerate(groups_of(owned)):
            rows = hidden[chunks[0] * lines : (chunks[-1] + 1) * lines, :]
            value = dot(rows, down[order[group], :, place]).astype(out.dtype)
            for spot, chunk in enumerate(chunks):
                out[:, chunk * share : (chunk + 1) * share] = value[spot * lines : (spot + 1) * lines]


def far_kernel(count, order, features, *refs):
    blocks, (gate_in, up_in, gate, up, down, hidden, *outs) = refs[:count], refs[count:]
    lines = blocks[0].shape[0]
    for group, chunks in enumerate(groups_of(gate.shape[0])):
        gate_value, up_value = projections(order, features, blocks, gate, up, group, chunks)
        place = slice(chunks[0] * lines, (chunks[-1] + 1) * lines)
        gate_value = gate_value + gate_in[place, :]
        up_value = up_value + up_in[place, :]
        hidden[place, :] = (jax.nn.silu(gate_value) * up_value).astype(BF16)
    down_parts(order, features, hidden, down, outs, lines)


def own_kernel(order, features, hidden, down, *outs):
    down_parts(order, features, hidden, down, outs, outs[0].shape[0])


def mix_kernel(returned, mix_high, mix_low, out):
    chunks = mix_high.shape[0]
    share = out.shape[1]
    total = jnp.zeros(out.shape, F32)
    for chunk in range(chunks):
        rows = returned[:, chunk * share : (chunk + 1) * share]
        total = total + dot_rows(mix_high[chunk], rows) + dot_rows(mix_low[chunk], rows)
    out[...] = total.astype(out.dtype)


def call(kernel, outs, specs, *args, flops=0):
    moved = sum(a.size * a.dtype.itemsize for a in (*args, *outs))
    return pl.pallas_call(
        kernel,
        out_shape=outs,
        in_specs=specs,
        out_specs=[VMEM] * len(outs),
        compiler_params=pltpu.CompilerParams(vmem_limit_bytes=LIMIT),
        cost_estimate=pl.CostEstimate(flops=flops, bytes_accessed=moved, transcendentals=0),
    )(*args)


def swapped(value, axis, mask):
    count = lax.axis_size(axis)
    return lax.ppermute(value, axis, [(source, source ^ mask) for source in range(count)])


def per_device(tokens, expert_ids, gate_weights, replica_plan, w_gate, w_up, w_down):
    owners = lax.axis_size("expert")
    own_index = lax.axis_index("expert")
    parts = lax.axis_size("dp")
    own_part = lax.axis_index("dp")
    owned, model_width, hidden_share = w_gate.shape
    tok_rows, share = tokens.shape
    chunks = owned + 1
    lines = owners * CAP
    wide = chunks * share
    shape = jax.ShapeDtypeStruct

    outgoing, mix_high, mix_low = call(
        functools.partial(route_kernel, owned),
        [
            shape((lines, wide), BF16),
            shape((chunks, lines, tok_rows), BF16),
            shape((chunks, lines, tok_rows), BF16),
        ],
        [SMEM, VMEM, VMEM, VMEM],
        replica_plan, expert_ids, gate_weights, tokens,
    )

    def exchanged(value):
        value = value.reshape(owners, CAP, wide)
        value = lax.all_to_all(value, "expert", split_axis=0, concat_axis=0, tiled=True)
        return value.reshape(lines, wide)

    hot = replica_plan[(own_index + owners // 2) % owners] - own_index * owned
    rest = jnp.arange(owned - 1, dtype=jnp.int32)
    order = jnp.concatenate([hot[None], rest + (rest >= hot)])

    blocks = {0: exchanged(outgoing)}
    mask = parts // 2
    while mask:
        for have in list(blocks):
            blocks[have ^ mask] = swapped(blocks[have], "dp", mask)
        mask //= 2
    near = [m for m in range(parts) if m < parts // 2]
    far = [m for m in range(parts) if m >= parts // 2]
    near_features = jnp.stack([own_part ^ m for m in near]).astype(jnp.int32)
    far_features = jnp.stack([own_part ^ m for m in far]).astype(jnp.int32)
    sums = [shape((chunks * lines, hidden_share), F32)] * 2
    near_flops = 4 * len(near) * chunks * lines * share * hidden_share
    gate_sum, up_sum = call(
        functools.partial(near_kernel, len(near)),
        sums,
        [SMEM, SMEM] + [VMEM] * (len(near) + 2),
        order, near_features, *[blocks[m] for m in near], w_gate, w_up,
        flops=near_flops,
    )
    hidden, *far_outs = call(
        functools.partial(far_kernel, len(far)),
        [shape((chunks * lines, hidden_share), BF16)] + [shape((lines, wide), BF16)] * len(far),
        [SMEM, SMEM] + [VMEM] * (len(far) + 5),
        order, far_features, *[blocks[m] for m in far], gate_sum, up_sum, w_gate, w_up, w_down,
        flops=near_flops * 3 // 2,
    )

    def reduced(found):
        mask = 1
        while mask < parts // 2:
            for m in [m for m in found if m & mask]:
                arrived = swapped(found.pop(m), "dp", mask)
                found[m ^ mask] = found[m ^ mask].astype(F32) + arrived.astype(F32)
            mask *= 2
        return found

    (top, far_sum), = reduced(dict(zip(far, far_outs))).items()
    crossed = swapped(far_sum.astype(BF16), "dp", top)
    near_outs = call(
        own_kernel,
        [shape((lines, wide), BF16)] * len(near),
        [SMEM, SMEM, VMEM, VMEM],
        order, near_features, hidden, w_down,
        flops=near_flops // 2,
    )
    near_sum = reduced(dict(zip(near, near_outs)))[0]
    returned = exchanged((near_sum.astype(F32) + crossed.astype(F32)).astype(BF16))
    (mixed_out,) = call(
        mix_kernel,
        [shape((tok_rows, share), BF16)],
        [VMEM] * 3,
        returned, mix_high, mix_low,
    )
    return mixed_out


def solution(mesh):
    in_specs = (
        P("expert", "dp"),
        P("expert", None),
        P("expert", None),
        P(),
        P("expert", None, "dp"),
        P("expert", None, "dp"),
        P("expert", "dp", None),
    )
    out_specs = P("expert", "dp")
    return jax.shard_map(
        per_device, mesh=mesh, in_specs=in_specs, out_specs=out_specs, check_vma=False
    )
```

time: 373 us -> 73.1 us (0.20)
  waiting for transfers between devices: 272 us -> 15.1 us
  other arithmetic: 17.6 us -> 0.38 us
  matrix products: 17.2 us -> 0 us
  blocking collectives: 18.4 us -> 34.2 us
  between operations: 14.3 us -> 0.72 us
  local copies, waits for them, and re-layouts: 24.8 us -> 12.4 us
  Pallas kernels: 0 us -> 6.26 us
  starting transfers between devices: 8.82 us -> 3.7 us
    ppermute x3 -> x6, waiting for transfers between devices: 210 us -> 15.1 us  [swapped(): lax.ppermute(value, axis, [(source, source ^ mask) for source in range(co...]
    all_to_all x1 -> x0, waiting for transfers between devices: 32 us -> none  [per_device(): lax.all_to_all(partials, 'expert', split_axis=0, concat_axis=0, tiled=True)]
    unnamed x3 -> x0, waiting for transfers between devices: 23.3 us -> none
    dot_general x6 -> x0, matrix products: 17.2 us -> none  [the longest x3 11.1 us: expert_block(): jnp.dot(hidden, down_piece, preferred_element_type=jnp.float32)]
    all_to_all x1 -> x2, blocking collectives: 18.4 us -> 34.2 us  [exchanged(): lax.all_to_all(value, 'expert', split_axis=0, concat_axis=0, tiled=True)]
    reduce_sum x3 -> x0, other arithmetic: 10.6 us -> none  [the longest x1 9.8 us: per_device(): jnp.sum(picked.reshape(tok_rows, choose_count, model_width), axis=1)]
    gather x2 -> x0, local copies, waits for them, and re-layouts: 8.37 us -> none  [the longest x1 7.33 us: per_device(): picked = returned[lookup].astype(jnp.float32) * weights_kept[:, None]]
    unnamed x17 -> x16, local copies, waits for them, and re-layouts: 3.87 us -> 11.1 us
  transfers between devices with their start and end apart: 6 -> 6, of which waited for: 6 -> 3; matrix products, arithmetic and copies ran while one was open for 6% -> 2% of each run, Pallas kernels for 0% -> 3%
where the time goes in v1:
time: 73.1 us; the launch traced here: 72.7 us
  blocking collectives  34.2 us (47%)
  waiting for transfers between devices  15.1 us (21%)
  local copies, waits for them, and re-layouts  12.4 us (17%)
  Pallas kernels  6.26 us (9%)
  starting transfers between devices  3.7 us (5%)
    all_to_all x2, blocking collectives, exchanged(): lax.all_to_all(value, 'expert', split_axis=0, concat_axis=0, tiled=True)  34.2 us
    ppermute x6, waiting for transfers between devices, swapped(): lax.ppermute(value, axis, [(source, source ^ mask) for source in range(co...  15.1 us
    unnamed x16, local copies, waits for them, and re-layouts  11.1 us
    pallas_call x5, Pallas kernels, call(): pl.pallas_call(kernel, out_shape=outs, in_specs=specs, out_specs=[VMEM] *...  6.26 us
    ppermute x6, starting transfers between devices, swapped(): lax.ppermute(value, axis, [(source, source ^ mask) for source in range(co...  3.7 us
  transfers between devices with their start and end apart: 6, of which 3 were waited for; matrix products, arithmetic and copies ran while one was open for 2% of the time, Pallas kernels for 3%

profile of v1, /device:TPU:0, one launch (start us, length us, event | category | flops | bytes accessed | tf_op | source)
XLA Modules:
  0.0 72.7 jit_solution(11039443024364750995)
XLA Ops:
  0.0 0.8 %copy.8.ids = s32[128,8]{1,0:T(8,128)S(1)} copy(s32[128,8]{0,1:T(8,128)} %param.8) | data formatting | bytes 8192 | tf_op args[1]
  0.8 0.8 %copy.9.gates = f32[128,8]{1,0:T(8,128)S(1)} copy(f32[128,8]{0,1:T(8,128)} %param.9) | data formatting | bytes 8192 | tf_op args[2]
  1.6 0.9 %copy-done.5 = bf16[128,896]{1,0:T(8,128)(2,1)S(1)} copy-done((bf16[128,896]{1,0:T(8,128)(2,1)S(1)}, bf16[128,896]{1,0:T(8,128)(2,1)}, u32[]{:S(2)}) %copy-start.5) | copy-done | bytes 229400
  2.5 0.7 copy-done.6
  3.2 1.1 %shard_map.73 = (bf16[64,2688]{1,0:T(8,128)(2,1)S(1)}, bf16[3,64,128]{2,1,0:T(8,128)(2,1)S(1)}, bf16[3,64,128]{2,1,0:T(8,128)(2,1)S(1)}) custom-call(s32[8]{0:T(128)S(1)} %copy-done.6, s32[128,8]{1,0:T(8,128)S(1)} %copy.8.ids, f32[128,8]{1,0:T(8,128)S(1)} %copy.9.gates, bf16[128,896]{1,0:T(8,128)(2,1)S(1)} %copy-done.5), custom_call_target="tpu_custom_call" | custom-call | bytes 679968 | tf_op jit(solution)/shard_map/pallas_call | solution.py:151
  4.3 18.3 %all_to_all.10 = bf16[8,8,2688]{2,1,0:T(8,128)(2,1)S(1)} all-to-all(bf16[8,8,2688]{2,1,0:T(8,128)(2,1)S(1)} %bitcast.15), channel_id=1, replica_groups=mesh['expert'=8,'dp'=4] {'expert'}, dimensions={0} | all-to-all | bytes 688128 | tf_op jit(solution)/shard_map/all_to_all | solution.py:191
  22.6 1.5 %collective-permute-start = (bf16[64,2688]{1,0:T(8,128)(2,1)S(1)}, bf16[64,2688]{1,0:T(8,128)(2,1)S(1)}, u32[]{:S(2)}, u32[]{:S(2)}) collective-permute-start(bf16[64,2688]{1,0:T(8,128)(2,1)S(1)} %bitcast.11), channel_id=1, source_target_pairs={{0,2},{1,3},{2,0},{3,1},{4,6},{5,7},{6,4},{7,5},{8,10},{9,11},{10,... | collective-permute-start | bytes 1032200 | tf_op jit(solution)/shard_map/ppermute | solution.py:163
  24.1 6.0 %collective-permute-done.refs_0_ = bf16[64,2688]{1,0:T(8,128)(2,1)S(1)} collective-permute-done((bf16[64,2688]{1,0:T(8,128)(2,1)S(1)}, bf16[64,2688]{1,0:T(8,128)(2,1)S(1)}, u32[]{:S(2)}, u32[]{:S(2)}) %collective-permute-start) | collective-permute-done | bytes 344096 | tf_op jit(solution)/shard_map/ppermute | solution.py:163
  30.1 1.2 %dynamic_slice.3 = s32[1]{0:T(128)} dynamic-slice(s32[8]{0:T(128)} %plan.1, s32[]{:T(128)S(6)} %select_n.11), dynamic_slice_sizes={1} | dynamic-slice | bytes 12 | tf_op jit(solution)/shard_map/dynamic_slice | solution.py:194
  32.1 2.0 %copy-done = bf16[2,3584,256]{2,1,0:T(8,128)(2,1)S(1)} copy-done((bf16[2,3584,256]{2,1,0:T(8,128)(2,1)S(1)}, bf16[2,3584,256]{2,1,0:T(8,128)(2,1)}, u32[]{:S(2)}) %copy-start) | copy-done | bytes 3670040
  34.2 2.0 %copy-done.2 = bf16[2,3584,256]{2,1,0:T(8,128)(2,1)S(1)} copy-done((bf16[2,3584,256]{2,1,0:T(8,128)(2,1)S(1)}, bf16[2,3584,256]{2,1,0:T(8,128)(2,1)}, u32[]{:S(2)}) %copy-start.2) | copy-done | bytes 3670040
  36.2 1.3 %shard_map.74 = (f32[192,256]{1,0:T(8,128)S(1)}, f32[192,256]{1,0:T(8,128)S(1)}) custom-call(s32[2]{0:T(128)S(1)} %get-tuple-element.25.order, s32[2]{0:T(128)S(1)} %get-tuple-element.26.features, bf16[64,2688]{1,0:T(8,128)(2,1)S(1)} %bitcast.13, bf16[64,2688]{1,0:T(8,128)(2,1)S(1)} %collective-permute-done.2.refs_1_, bf16[2,3584,256]{2,1,0:T(8,128)(2,1)S(1)} %copy-done, ...), custom_call_target="tpu_custom_call" | custom-call | flops 352321536 | bytes 8421392 | tf_op jit(solution)/shard_map/pallas_call | solution.py:151
  37.5 0.7 copy-done.1
  38.2 1.1 %copy-done.3 = bf16[2,3584,256]{2,1,0:T(8,128)(2,1)S(1)} copy-done((bf16[2,3584,256]{2,1,0:T(8,128)(2,1)S(1)}, bf16[2,3584,256]{2,1,0:T(8,128)(2,1)}, u32[]{:S(2)}) %copy-start.3) | copy-done | bytes 3670040
  39.3 2.0 %copy-done.4 = bf16[2,256,3584]{2,1,0:T(8,128)(2,1)S(1)} copy-done((bf16[2,256,3584]{2,1,0:T(8,128)(2,1)S(1)}, bf16[2,256,3584]{2,1,0:T(8,128)(2,1)}, u32[]{:S(2)}) %copy-start.4) | copy-done | bytes 3670040
  41.4 1.6 %shard_map.75 = (bf16[192,256]{1,0:T(8,128)(2,1)S(1)}, bf16[64,2688]{1,0:T(8,128)(2,1)S(1)}, bf16[64,2688]{1,0:T(8,128)(2,1)S(1)}) custom-call(s32[2]{0:T(128)S(1)} %get-tuple-element.25.order, s32[2]{0:T(128)S(1)} %pad_add_fusion.2.features, bf16[64,2688]{1,0:T(8,128)(2,1)S(1)} %collective-permute-done.refs_0_, ...), custom_call_target="tpu_custom_call" | custom-call | flops 528482304 | bytes 12877840 | tf_op jit(solution)/shard_map/pallas_call | solution.py:151
  43.0 0.6 collective-permute-start.4
  43.6 1.0 %shard_map.76 = (bf16[64,2688]{1,0:T(8,128)(2,1)S(1)}, bf16[64,2688]{1,0:T(8,128)(2,1)S(1)}) custom-call(s32[2]{0:T(128)S(1)} %get-tuple-element.25.order, s32[2]{0:T(128)S(1)} %get-tuple-element.26.features, bf16[192,256]{1,0:T(8,128)(2,1)S(1)} %get-tuple-element.18.hidden, bf16[2,256,3584]{2,1,0:T(8,128)(2,1)S(1)} %copy-done.4), custom_call_target="tpu_custom_call" | custom-call | flops 176160768 | bytes 4456464 | tf_op jit(solution)/shard_map/pallas_call | solution.py:151
  44.6 0.2 collective-permute-done.4
  45.0 1.6 %collective-permute-start.5 = (bf16[64,2688]{1,0:T(8,128)(2,1)S(1)}, bf16[64,2688]{1,0:T(8,128)(2,1)S(1)}, u32[]{:S(2)}, u32[]{:S(2)}) collective-permute-start(bf16[64,2688]{1,0:T(8,128)(2,1)S(1)} %add_convert_fusion.1), channel_id=1, source_target_pairs={{0,2},{1,3},{2,0},{3,1},{4,6},{5,7},{6,4},{7,5},{8,10},{9,11},{10,... | collective-permute-start | bytes 1032200 | tf_op jit(solution)/shard_map/ppermute | solution.py:163
  46.5 8.8 %collective-permute-done.5 = bf16[64,2688]{1,0:T(8,128)(2,1)S(1)} collective-permute-done((bf16[64,2688]{1,0:T(8,128)(2,1)S(1)}, bf16[64,2688]{1,0:T(8,128)(2,1)S(1)}, u32[]{:S(2)}, u32[]{:S(2)}) %collective-permute-start.5) | collective-permute-done | bytes 344096 | tf_op jit(solution)/shard_map/ppermute | solution.py:163
  55.4 0.1 fusion
  55.5 16.0 %all_to_all.11 = bf16[8,8,2688]{2,1,0:T(8,128)(2,1)S(1)} all-to-all(bf16[8,8,2688]{2,1,0:T(8,128)(2,1)S(1)} %fusion), channel_id=1, replica_groups=mesh['expert'=8,'dp'=4] {'expert'}, dimensions={0} | all-to-all | bytes 688128 | tf_op jit(solution)/shard_map/all_to_all | solution.py:191
  71.5 1.2 %shard_map.77 = bf16[128,896]{1,0:T(8,128)(2,1)} custom-call(bf16[64,2688]{1,0:T(8,128)(2,1)S(1)} %bitcast.14, bf16[3,64,128]{2,1,0:T(8,128)(2,1)S(1)} %get-tuple-element.23.mix_high, bf16[3,64,128]{2,1,0:T(8,128)(2,1)S(1)} %get-tuple-element.24.mix_low), custom_call_target="tpu_custom_call" | custom-call | bytes 671744 | tf_op jit(solution)/shard_map/pallas_call | solution.py:151
  (16 shorter events, 0.3 us)
Async XLA Ops:
  1.6 0.9 %copy-start.5 = (bf16[128,896]{1,0:T(8,128)(2,1)S(1)}, bf16[128,896]{1,0:T(8,128)(2,1)}, u32[]{:S(2)}) copy-start(bf16[128,896]{1,0:T(8,128)(2,1)} %tokens.1) | copy-start | bytes 688132
  2.5 0.7 copy-start.6
  22.6 7.5 %collective-permute-start = (bf16[64,2688]{1,0:T(8,128)(2,1)S(1)}, bf16[64,2688]{1,0:T(8,128)(2,1)S(1)}, u32[]{:S(2)}, u32[]{:S(2)}) collective-permute-start(bf16[64,2688]{1,0:T(8,128)(2,1)S(1)} %bitcast.11), channel_id=1, source_target_pairs={{0,2},{1,3},{2,0},{3,1},{4,6},{5,7},{6,4},{7,5},{8,10},{9,11},{10,... | collective-permute-start | bytes 1032200 | tf_op jit(solution)/shard_map/ppermute | solution.py:163
  24.1 8.1 %collective-permute-start.2 = (bf16[64,2688]{1,0:T(8,128)(2,1)S(1)}, bf16[64,2688]{1,0:T(8,128)(2,1)S(1)}, u32[]{:S(2)}, u32[]{:S(2)}) collective-permute-start(bf16[64,2688]{1,0:T(8,128)(2,1)S(1)} %bitcast.12), channel_id=1, source_target_pairs={{0,1},{1,0},{2,3},{3,2},{4,5},{5,4},{6,7},{7,6},{8,9},{9,8},{10,11... | collective-permute-start | bytes 1032200 | tf_op jit(solution)/shard_map/ppermute | solution.py:163
  30.1 7.5 %collective-permute-start.1 = (bf16[64,2688]{1,0:T(8,128)(2,1)S(1)}, bf16[64,2688]{1,0:T(8,128)(2,1)S(1)}, u32[]{:S(2)}, u32[]{:S(2)}) collective-permute-start(bf16[64,2688]{1,0:T(8,128)(2,1)S(1)} %collective-permute-done.refs_0_), channel_id=1, source_target_pairs={{0,1},{1,0},{2,3},{3,2},{4,5},{5,4},{6,7},{7,6},{8,9},{9,8},{10,11... | collective-permute-start | bytes 1032200 | tf_op jit(solution)/shard_map/ppermute | solution.py:163
  32.1 2.0 %copy-start = (bf16[2,3584,256]{2,1,0:T(8,128)(2,1)S(1)}, bf16[2,3584,256]{2,1,0:T(8,128)(2,1)}, u32[]{:S(2)}) copy-start(bf16[2,3584,256]{2,1,0:T(8,128)(2,1)} %refs_4_.1) | copy-start | bytes 11010052
  34.1 2.0 %copy-start.2 = (bf16[2,3584,256]{2,1,0:T(8,128)(2,1)S(1)}, bf16[2,3584,256]{2,1,0:T(8,128)(2,1)}, u32[]{:S(2)}) copy-start(bf16[2,3584,256]{2,1,0:T(8,128)(2,1)} %refs_5_.1) | copy-start | bytes 11010052
  36.2 2.0 %copy-start.1 = (bf16[2,3584,256]{2,1,0:T(8,128)(2,1)S(1)}, bf16[2,3584,256]{2,1,0:T(8,128)(2,1)}, u32[]{:S(2)}) copy-start(bf16[2,3584,256]{2,1,0:T(8,128)(2,1)} %refs_4_.1) | copy-start | bytes 11010052
  36.2 3.2 %copy-start.3 = (bf16[2,3584,256]{2,1,0:T(8,128)(2,1)S(1)}, bf16[2,3584,256]{2,1,0:T(8,128)(2,1)}, u32[]{:S(2)}) copy-start(bf16[2,3584,256]{2,1,0:T(8,128)(2,1)} %refs_5_.1) | copy-start | bytes 11010052
  39.3 2.0 %copy-start.4 = (bf16[2,256,3584]{2,1,0:T(8,128)(2,1)S(1)}, bf16[2,256,3584]{2,1,0:T(8,128)(2,1)}, u32[]{:S(2)}) copy-start(bf16[2,256,3584]{2,1,0:T(8,128)(2,1)} %down.1) | copy-start | bytes 11010052
  43.0 1.8 %collective-permute-start.4 = (bf16[64,2688]{1,0:T(8,128)(2,1)S(1)}, bf16[64,2688]{1,0:T(8,128)(2,1)S(1)}, u32[]{:S(2)}, u32[]{:S(2)}) collective-permute-start(bf16[64,2688]{1,0:T(8,128)(2,1)S(1)} %get-tuple-element.22), channel_id=1, source_target_pairs={{0,1},{1,0},{2,3},{3,2},{4,5},{5,4},{6,7},{7,6},{8,9},{9,8},{10,11... | collective-permute-start | bytes 1032200 | tf_op jit(solution)/shard_map/ppermute | solution.py:163
  44.6 2.0 %collective-permute-start.3 = (bf16[64,2688]{1,0:T(8,128)(2,1)S(1)}, bf16[64,2688]{1,0:T(8,128)(2,1)S(1)}, u32[]{:S(2)}, u32[]{:S(2)}) collective-permute-start(bf16[64,2688]{1,0:T(8,128)(2,1)S(1)} %get-tuple-element.20), channel_id=1, source_target_pairs={{0,1},{1,0},{2,3},{3,2},{4,5},{5,4},{6,7},{7,6},{8,9},{9,8},{10,11... | collective-permute-start | bytes 1032200 | tf_op jit(solution)/shard_map/ppermute | solution.py:163
  45.0 10.4 %collective-permute-start.5 = (bf16[64,2688]{1,0:T(8,128)(2,1)S(1)}, bf16[64,2688]{1,0:T(8,128)(2,1)S(1)}, u32[]{:S(2)}, u32[]{:S(2)}) collective-permute-start(bf16[64,2688]{1,0:T(8,128)(2,1)S(1)} %add_convert_fusion.1), channel_id=1, source_target_pairs={{0,2},{1,3},{2,0},{3,1},{4,6},{5,7},{6,4},{7,5},{8,10},{9,11},{10,... | collective-permute-start | bytes 1032200 | tf_op jit(solution)/shard_map/ppermute | solution.py:163

commit v2 on v1

v2 whole, which is shorter than its diff:
```python
import functools

import jax
import jax.numpy as jnp
from jax import lax
from jax.experimental import pallas as pl
from jax.experimental.pallas import tpu as pltpu
from jax.sharding import PartitionSpec as P

CAP = 8
F32 = jnp.float32
BF16 = jnp.bfloat16
VMEM = pl.BlockSpec(memory_space=pltpu.VMEM)
HBM = pl.BlockSpec(memory_space=pltpu.HBM)
LIMIT = 20 * 2**20


def dot(left, right):
    return jnp.dot(left, right, preferred_element_type=F32)


def dot_rows(left, right):
    return lax.dot_general(left, right, (((0,), (0,)), ((), ())), preferred_element_type=F32)


def copied(pairs, sems):
    copies = [pltpu.make_async_copy(*pair, sems.at[n]) for n, pair in enumerate(pairs)]
    for copy in copies:
        copy.start()
    return copies


def route_kernel(
    owned, plan_hbm, ids_hbm, gates_hbm, tokens_hbm, outgoing, mix_high, mix_low,
    plan, ids, gates, tokens, sems,
):
    copies = copied(
        [(plan_hbm, plan), (ids_hbm, ids), (gates_hbm, gates), (tokens_hbm, tokens)], sems
    )
    choices, tok_rows = ids.shape
    share = tokens.shape[1]
    owners = plan.shape[0]
    experts = owners * owned
    row = lax.broadcasted_iota(jnp.int32, (tok_rows, tok_rows), 0)
    col = lax.broadcasted_iota(jnp.int32, (tok_rows, tok_rows), 1)
    earlier = (row < col).astype(F32).astype(BF16)
    expert = lax.broadcasted_iota(jnp.int32, (experts, tok_rows), 0)
    owner = expert // owned
    within = expert - owner * owned
    named = jnp.zeros((experts, tok_rows), F32)
    weight = jnp.zeros((experts, tok_rows), F32)
    hot = jnp.zeros((experts, tok_rows), jnp.int32)
    copies[0].wait()
    for host in range(owners):
        source = (host + owners // 2) % owners
        hot = jnp.where(owner == source, plan[host] - source * owned, hot)
    copies[1].wait()
    copies[2].wait()
    for choice in range(choices):
        hit = expert == ids[choice : choice + 1, :]
        named = named + hit.astype(F32)
        weight = weight + jnp.where(hit, gates[choice : choice + 1, :], 0.0)
    rank = dot(named.astype(BF16), earlier)
    limit = jnp.where(within == hot, 2 * CAP, CAP)
    start = jnp.where(within == hot, 0, CAP * (1 + within + (within < hot).astype(jnp.int32)))
    rank = rank.astype(jnp.int32)
    place = jnp.where((named > 0.0) & (rank < limit), start + rank, -1)
    slot = lax.broadcasted_iota(jnp.int32, (CAP, tok_rows), 0)
    for chunk in range(owned + 1):
        picks, mixes = [], []
        for index in range(owners):
            pick = jnp.zeros((CAP, tok_rows), F32)
            mix = jnp.zeros((CAP, tok_rows), F32)
            for number in range(index * owned, (index + 1) * owned):
                match = place[number : number + 1, :] == slot + chunk * CAP
                pick = pick + match.astype(F32)
                mix = mix + jnp.where(match, weight[number : number + 1, :], 0.0)
            picks.append(pick)
            mixes.append(mix)
        pick = jnp.concatenate(picks, axis=0).astype(BF16)
        mix = jnp.concatenate(mixes, axis=0)
        if chunk == 0:
            copies[3].wait()
        outgoing[:, chunk * share : (chunk + 1) * share] = dot(pick, tokens[...]).astype(BF16)
        high = mix.astype(BF16)
        mix_high[chunk] = high
        mix_low[chunk] = (mix - high.astype(F32)).astype(BF16)


def groups_of(owned):
    return [(0, 1)] + [(number + 1,) for number in range(1, owned)]


def chunk_rows(block, chunks, share):
    return jnp.concatenate(
        [block[:, chunk * share : (chunk + 1) * share] for chunk in chunks], axis=0
    )


def projections(blocks, weights, group, chunks):
    share = blocks[0].shape[1] // (weights.shape[0] + 1)
    value = None
    for number, block in enumerate(blocks):
        rows = chunk_rows(block, chunks, share)
        part = dot(rows, weights[group, number * share : (number + 1) * share, :])
        value = part if value is None else value + part
    return value


def near_kernel(
    near, far, plan_hbm, gate_hbm, up_hbm, down_hbm, *refs
):
    blocks, refs = refs[: len(near)], refs[len(near) :]
    gate_out, up_out, gate_far, up_far, down, plan, gate, up, plan_sem, sems = refs
    owned = gate_hbm.shape[0]
    share = blocks[0].shape[1] // (owned + 1)
    lines = blocks[0].shape[0]
    owners = plan.shape[0]
    own_index, own_part = lax.axis_index("expert"), lax.axis_index("dp")
    (plan_copy,) = copied([(plan_hbm, plan)], plan_sem)
    plan_copy.wait()
    hot = plan[lax.rem(own_index + owners // 2, owners)] - own_index * owned
    order = [hot] + [n + (n >= hot).astype(jnp.int32) for n in range(owned - 1)]

    def features(m):
        return pl.ds(pl.multiple_of((own_part ^ m) * share, share), share)

    pairs = []
    for wanted, (gate_to, up_to) in ((near, (gate, up)), (far, (gate_far, up_far))):
        for group, pick in enumerate(order):
            for number, m in enumerate(wanted):
                place = slice(number * share, (number + 1) * share)
                pairs.append((gate_hbm.at[pick, features(m), :], gate_to.at[group, place, :]))
                pairs.append((up_hbm.at[pick, features(m), :], up_to.at[group, place, :]))
    for m in far + near:
        for group, pick in enumerate(order):
            place = slice(m * share, (m + 1) * share)
            pairs.append((down_hbm.at[pick, :, features(m)], down.at[group, :, place]))
    copies = copied(pairs, sems)
    for group, chunks in enumerate(groups_of(owned)):
        count = 2 * len(near)
        for copy in copies[group * count : (group + 1) * count]:
            copy.wait()
        place = slice(chunks[0] * lines, (chunks[-1] + 1) * lines)
        gate_out[place, :] = projections(blocks, gate, group, chunks)
        up_out[place, :] = projections(blocks, up, group, chunks)
    for copy in copies[2 * len(near) * owned :]:
        copy.wait()


def down_parts(numbers, hidden, down, outs, lines):
    owned = down.shape[0]
    share = outs[0].shape[1] // (owned + 1)
    for m, out in zip(numbers, outs):
        for group, chunks in enumerate(groups_of(owned)):
            rows = hidden[chunks[0] * lines : (chunks[-1] + 1) * lines, :]
            value = dot(rows, down[group, :, m * share : (m + 1) * share]).astype(out.dtype)
            for spot, chunk in enumerate(chunks):
                out[:, chunk * share : (chunk + 1) * share] = value[spot * lines : (spot + 1) * lines]


def far_kernel(far, *refs):
    blocks, (gate_in, up_in, gate, up, down, hidden, *outs) = refs[: len(far)], refs[len(far) :]
    lines = blocks[0].shape[0]
    for group, chunks in enumerate(groups_of(gate.shape[0])):
        place = slice(chunks[0] * lines, (chunks[-1] + 1) * lines)
        gate_value = projections(blocks, gate, group, chunks) + gate_in[place, :]
        up_value = projections(blocks, up, group, chunks) + up_in[place, :]
        hidden[place, :] = (jax.nn.silu(gate_value) * up_value).astype(BF16)
    down_parts(far, hidden, down, outs, lines)


def own_kernel(near, hidden, down, *outs):
    down_parts(near, hidden, down, outs, outs[0].shape[0])


def mix_kernel(returned, mix_high, mix_low, out):
    chunks = mix_high.shape[0]
    share = out.shape[1]
    total = jnp.zeros(out.shape, F32)
    for chunk in range(chunks):
        rows = returned[:, chunk * share : (chunk + 1) * share]
        total = total + dot_rows(mix_high[chunk], rows) + dot_rows(mix_low[chunk], rows)
    out[...] = total.astype(out.dtype)


def call(kernel, outs, specs, *args, scratch=(), flops=0):
    moved = sum(a.size * a.dtype.itemsize for a in (*args, *outs))
    return pl.pallas_call(
        kernel,
        out_shape=outs,
        in_specs=specs,
        out_specs=[VMEM] * len(outs),
        scratch_shapes=list(scratch),
        compiler_params=pltpu.CompilerParams(vmem_limit_bytes=LIMIT),
        cost_estimate=pl.CostEstimate(flops=flops, bytes_accessed=moved, transcendentals=0),
    )(*args)


def swapped(value, axis, mask):
    count = lax.axis_size(axis)
    return lax.ppermute(value, axis, [(source, source ^ mask) for source in range(count)])


def per_device(tokens, expert_ids, gate_weights, replica_plan, w_gate, w_up, w_down):
    owners = lax.axis_size("expert")
    parts = lax.axis_size("dp")
    owned, model_width, hidden_share = w_gate.shape
    tok_rows, share = tokens.shape
    choices = expert_ids.shape[1]
    chunks = owned + 1
    lines = owners * CAP
    wide = chunks * share
    shape = jax.ShapeDtypeStruct
    plan_memory = pltpu.SMEM((owners,), jnp.int32)

    outgoing, mix_high, mix_low = call(
        functools.partial(route_kernel, owned),
        [
            shape((lines, wide), BF16),
            shape((chunks, lines, tok_rows), BF16),
            shape((chunks, lines, tok_rows), BF16),
        ],
        [HBM] * 4,
        replica_plan, expert_ids.T, gate_weights.T, tokens,
        scratch=[
            plan_memory,
            pltpu.VMEM((choices, tok_rows), jnp.int32),
            pltpu.VMEM((choices, tok_rows), F32),
            pltpu.VMEM((tok_rows, share), BF16),
            pltpu.SemaphoreType.DMA((4,)),
        ],
    )

    def exchanged(value):
        value = value.reshape(owners, CAP, wide)
        value = lax.all_to_all(value, "expert", split_axis=0, concat_axis=0, tiled=True)
        return value.reshape(lines, wide)

    near = [m for m in range(parts) if m < parts // 2]
    far = [m for m in range(parts) if m >= parts // 2]

    def spread(blocks, mask):
        while mask:
            for have in list(blocks):
                blocks[have ^ mask] = swapped(blocks[have], "dp", mask)
            mask //= 2
        return blocks

    arrived = exchanged(outgoing)
    top = parts // 2
    crossed = swapped(arrived, "dp", top)
    blocks = spread({0: arrived}, top // 2)
    half = (owned, len(near) * share, hidden_share)
    near_flops = 4 * len(near) * chunks * lines * share * hidden_share
    halves = call(
        functools.partial(near_kernel, near, far),
        [
            shape((chunks * lines, hidden_share), F32),
            shape((chunks * lines, hidden_share), F32),
            shape(half, BF16),
            shape(half, BF16),
            shape(w_down.shape, BF16),
        ],
        [HBM] * 4 + [VMEM] * len(near),
        replica_plan, w_gate, w_up, w_down, *[blocks[m] for m in near],
        scratch=[
            plan_memory,
            pltpu.VMEM(half, BF16),
            pltpu.VMEM(half, BF16),
            pltpu.SemaphoreType.DMA((1,)),
            pltpu.SemaphoreType.DMA((6 * len(near) * owned,)),
        ],
        flops=near_flops,
    )
    crossed, *halves = lax.optimization_barrier((crossed, *halves))
    gate_sum, up_sum, gate_far, up_far, down = halves
    blocks |= spread({top: crossed}, top // 2)
    hidden, *far_outs = call(
        functools.partial(far_kernel, far),
        [shape((chunks * lines, hidden_share), BF16)] + [shape((lines, wide), BF16)] * len(far),
        [VMEM] * (len(far) + 5),
        *[blocks[m] for m in far], *halves,
        flops=near_flops * 3 // 2,
    )

    def reduced(found):
        mask = 1
        while mask < parts // 2:
            for m in [m for m in found if m & mask]:
                arrived = swapped(found.pop(m), "dp", mask)
                found[m ^ mask] = found[m ^ mask].astype(F32) + arrived.astype(F32)
            mask *= 2
        return found

    far_sum = reduced(dict(zip(far, far_outs)))[top]
    crossed = swapped(far_sum.astype(BF16), "dp", top)
    near_outs = call(
        functools.partial(own_kernel, near),
        [shape((lines, wide), BF16)] * len(near),
        [VMEM, VMEM],
        hidden, down,
        flops=near_flops // 2,
    )
    near_sum = reduced(dict(zip(near, near_outs)))[0]
    returned = exchanged((near_sum.astype(F32) + crossed.astype(F32)).astype(BF16))
    (mixed_out,) = call(
        mix_kernel,
        [shape((tok_rows, share), BF16)],
        [VMEM] * 3,
        returned, mix_high, mix_low,
    )
    return mixed_out


def solution(mesh):
    in_specs = (
        P("expert", "dp"),
        P("expert", None),
        P("expert", None),
        P(),
        P("expert", None, "dp"),
        P("expert", None, "dp"),
        P("expert", "dp", None),
    )
    out_specs = P("expert", "dp")
    return jax.shard_map(
        per_device, mesh=mesh, in_specs=in_specs, out_specs=out_specs, check_vma=False
    )
```

time: 73.1 us -> 66.5 us (0.910)
  waiting for transfers between devices: 15.1 us -> 10.9 us
  Pallas kernels: 6.26 us -> 10.1 us
  local copies, waits for them, and re-layouts: 12.4 us -> 9.08 us
  blocking collectives: 34.2 us -> 31.9 us
    ppermute x6, waiting for transfers between devices: 15.1 us -> 10.9 us  [swapped(): lax.ppermute(value, axis, [(source, source ^ mask) for source in range(co...]
    pallas_call x5, Pallas kernels: 6.26 us -> 10.1 us  [call(): pl.pallas_call(kernel, out_shape=outs, in_specs=specs, out_specs=[VMEM] *...]
    all_to_all x2, blocking collectives: 34.2 us -> 31.9 us  [exchanged(): lax.all_to_all(value, 'expert', split_axis=0, concat_axis=0, tiled=True)]
    unnamed x16 -> x14, local copies, waits for them, and re-layouts: 11.1 us -> 9.08 us
    dynamic_slice x1 -> x0, local copies, waits for them, and re-layouts: 1.24 us -> none  [per_device(): hot = replica_plan[(own_index + owners // 2) % owners] - own_index * owned]
  transfers between devices with their start and end apart: 6 -> 6, of which waited for: 3 -> 4; matrix products, arithmetic and copies ran while one was open for 2% -> 0% of each run, Pallas kernels for 3% -> 10%
where the time goes in v2:
time: 66.5 us; the launch traced here: 66.1 us
  blocking collectives  31.9 us (48%)
  waiting for transfers between devices  10.9 us (16%)
  Pallas kernels  10.1 us (15%)
  local copies, waits for them, and re-layouts  9.08 us (14%)
  starting transfers between devices  3.9 us (6%)
    all_to_all x2, blocking collectives, exchanged(): lax.all_to_all(value, 'expert', split_axis=0, concat_axis=0, tiled=True)  31.9 us
    ppermute x6, waiting for transfers between devices, swapped(): lax.ppermute(value, axis, [(source, source ^ mask) for source in range(co...  10.9 us
    pallas_call x5, Pallas kernels, call(): pl.pallas_call(kernel, out_shape=outs, in_specs=specs, out_specs=[VMEM] *...  10.1 us
    unnamed x14, local copies, waits for them, and re-layouts  9.08 us
    ppermute x6, starting transfers between devices, swapped(): lax.ppermute(value, axis, [(source, source ^ mask) for source in range(co...  3.9 us
  transfers between devices with their start and end apart: 6, of which 4 were waited for; matrix products, arithmetic and copies ran while one was open for 0% of the time, Pallas kernels for 10%

profile of v2, /device:TPU:0, one launch (start us, length us, event | category | flops | bytes accessed | tf_op | source)
XLA Modules:
  0.0 66.1 jit_solution(15724751535351428678)
XLA Ops:
  0.0 0.9 %copy-done.3 = bf16[128,896]{1,0:T(8,128)(2,1)S(1)} copy-done((bf16[128,896]{1,0:T(8,128)(2,1)S(1)}, bf16[128,896]{1,0:T(8,128)(2,1)}, u32[]{:S(2)}) %copy-start.3) | copy-done | bytes 229400
  0.9 0.7 %copy-done.4 = s32[128,8]{0,1:T(8,128)S(1)} copy-done((s32[128,8]{0,1:T(8,128)S(1)}, s32[128,8]{0,1:T(8,128)}, u32[]{:S(2)}) %copy-start.4) | copy-done | bytes 4120
  1.6 0.7 %copy-done.5 = f32[128,8]{0,1:T(8,128)S(1)} copy-done((f32[128,8]{0,1:T(8,128)S(1)}, f32[128,8]{0,1:T(8,128)}, u32[]{:S(2)}) %copy-start.5) | copy-done | bytes 4120
  2.3 0.7 copy-done.6
  3.0 1.0 %shard_map.73 = (bf16[64,2688]{1,0:T(8,128)(2,1)S(1)}, bf16[3,64,128]{2,1,0:T(8,128)(2,1)S(1)}, bf16[3,64,128]{2,1,0:T(8,128)(2,1)S(1)}) custom-call(s32[8]{0:T(128)S(1)} %copy-done.6, s32[8,128]{1,0:T(8,128)S(1)} %bitcast.12, f32[8,128]{1,0:T(8,128)S(1)} %bitcast.13, bf16[128,896]{1,0:T(8,128)(2,1)S(1)} %copy-done.3), custom_call_target="tpu_custom_call" | custom-call | bytes 679968 | tf_op jit(solution)/shard_map/pallas_call | solution.py:189
  4.0 18.3 %all_to_all.10 = bf16[8,8,2688]{2,1,0:T(8,128)(2,1)S(1)} all-to-all(bf16[8,8,2688]{2,1,0:T(8,128)(2,1)S(1)} %bitcast.11), channel_id=1, replica_groups=mesh['expert'=8,'dp'=4] {'expert'}, dimensions={0} | all-to-all | bytes 688128 | tf_op jit(solution)/shard_map/all_to_all | solution.py:237
  22.3 1.5 %collective-permute-start = (bf16[64,2688]{1,0:T(8,128)(2,1)S(1)}, bf16[64,2688]{1,0:T(8,128)(2,1)S(1)}, u32[]{:S(2)}, u32[]{:S(2)}) collective-permute-start(bf16[64,2688]{1,0:T(8,128)(2,1)S(1)} %bitcast.8), channel_id=1, source_target_pairs={{0,2},{1,3},{2,0},{3,1},{4,6},{5,7},{6,4},{7,5},{8,10},{9,11},{10,... | collective-permute-start | bytes 1032200 | tf_op jit(solution)/shard_map/ppermute | solution.py:202
  23.8 0.2 collective-permute-done.1.refs_1_
  23.9 2.0 %copy-done = bf16[2,3584,256]{2,1,0:T(8,128)(2,1)S(1)} copy-done((bf16[2,3584,256]{2,1,0:T(8,128)(2,1)S(1)}, bf16[2,3584,256]{2,1,0:T(8,128)(2,1)}, u32[]{:S(2)}) %copy-start) | copy-done | bytes 3670040
  25.9 2.0 %copy-done.1 = bf16[2,3584,256]{2,1,0:T(8,128)(2,1)S(1)} copy-done((bf16[2,3584,256]{2,1,0:T(8,128)(2,1)S(1)}, bf16[2,3584,256]{2,1,0:T(8,128)(2,1)}, u32[]{:S(2)}) %copy-start.1) | copy-done | bytes 3670040
  28.0 2.0 %copy-done.2 = bf16[2,256,3584]{2,1,0:T(8,128)(2,1)S(1)} copy-done((bf16[2,256,3584]{2,1,0:T(8,128)(2,1)S(1)}, bf16[2,256,3584]{2,1,0:T(8,128)(2,1)}, u32[]{:S(2)}) %copy-start.2) | copy-done | bytes 3670040
  30.0 6.4 %shard_map.74 = (f32[192,256]{1,0:T(8,128)S(1)}, f32[192,256]{1,0:T(8,128)S(1)}, bf16[2,1792,256]{2,1,0:T(8,128)(2,1)S(1)}, bf16[2,1792,256]{2,1,0:T(8,128)(2,1)S(1)}, bf16[2,256,3584]{2,1,0:T(8,128)(2,1)S(1)}) custom-call(s32[8]{0:T(128)S(1)} %copy-done.6, bf16[2,3584,256]{2,1,0:T(8,128)(2,1)S(1)} %copy-done, bf16[2,3584,256]{2,1,0:T(8,128)(2,1)S(1)} %copy-done.1, ...), custom_call_target="tpu_custom_call" | custom-call | flops 352321536 | bytes 19431456 | tf_op jit(solution)/shard_map/pallas_call | solution.py:189
  36.4 0.2 collective-permute-start.2
  36.6 1.5 %collective-permute-done.2.refs_1_ = bf16[64,2688]{1,0:T(8,128)(2,1)S(1)} collective-permute-done((bf16[64,2688]{1,0:T(8,128)(2,1)S(1)}, bf16[64,2688]{1,0:T(8,128)(2,1)S(1)}, u32[]{:S(2)}, u32[]{:S(2)}) %collective-permute-start.2) | collective-permute-done | bytes 344096 | tf_op jit(solution)/shard_map/ppermute | solution.py:202
  38.1 1.0 %shard_map.75 = (bf16[192,256]{1,0:T(8,128)(2,1)S(1)}, bf16[64,2688]{1,0:T(8,128)(2,1)S(1)}, bf16[64,2688]{1,0:T(8,128)(2,1)S(1)}) custom-call(bf16[64,2688]{1,0:T(8,128)(2,1)S(1)} %collective-permute-done.refs_0_, bf16[64,2688]{1,0:T(8,128)(2,1)S(1)} %collective-permute-done.2.refs_1_, f32[192,256]{1,0:T(8,128)S(1)} %get-tuple-element.31.refs_2_, ...), custom_call_target="tpu_custom_call" | custom-call | flops 528482304 | bytes 9207808 | tf_op jit(solution)/shard_map/pallas_call | solution.py:189
  39.2 0.2 collective-permute-start.4
  39.4 0.4 shard_map.76
  39.8 0.4 collective-permute-start.3
  40.2 0.7 collective-permute-done.4
  41.0 1.6 %collective-permute-start.5 = (bf16[64,2688]{1,0:T(8,128)(2,1)S(1)}, bf16[64,2688]{1,0:T(8,128)(2,1)S(1)}, u32[]{:S(2)}, u32[]{:S(2)}) collective-permute-start(bf16[64,2688]{1,0:T(8,128)(2,1)S(1)} %add_convert_fusion.1), channel_id=1, source_target_pairs={{0,2},{1,3},{2,0},{3,1},{4,6},{5,7},{6,4},{7,5},{8,10},{9,11},{10,... | collective-permute-start | bytes 1032200 | tf_op jit(solution)/shard_map/ppermute | solution.py:202
  42.6 8.6 %collective-permute-done.5 = bf16[64,2688]{1,0:T(8,128)(2,1)S(1)} collective-permute-done((bf16[64,2688]{1,0:T(8,128)(2,1)S(1)}, bf16[64,2688]{1,0:T(8,128)(2,1)S(1)}, u32[]{:S(2)}, u32[]{:S(2)}) %collective-permute-start.5) | collective-permute-done | bytes 344096 | tf_op jit(solution)/shard_map/ppermute | solution.py:202
  51.2 0.1 fusion
  51.3 13.6 %all_to_all.11 = bf16[8,8,2688]{2,1,0:T(8,128)(2,1)S(1)} all-to-all(bf16[8,8,2688]{2,1,0:T(8,128)(2,1)S(1)} %fusion), channel_id=1, replica_groups=mesh['expert'=8,'dp'=4] {'expert'}, dimensions={0} | all-to-all | bytes 688128 | tf_op jit(solution)/shard_map/all_to_all | solution.py:237
  64.9 1.2 %shard_map.77 = bf16[128,896]{1,0:T(8,128)(2,1)} custom-call(bf16[64,2688]{1,0:T(8,128)(2,1)S(1)} %bitcast.10, bf16[3,64,128]{2,1,0:T(8,128)(2,1)S(1)} %get-tuple-element.41.mix_high, bf16[3,64,128]{2,1,0:T(8,128)(2,1)S(1)} %get-tuple-element.42.mix_low), custom_call_target="tpu_custom_call" | custom-call | bytes 671744 | tf_op jit(solution)/shard_map/pallas_call | solution.py:189
  (11 shorter events, 0.1 us)
Async XLA Ops:
  0.0 0.9 %copy-start.3 = (bf16[128,896]{1,0:T(8,128)(2,1)S(1)}, bf16[128,896]{1,0:T(8,128)(2,1)}, u32[]{:S(2)}) copy-start(bf16[128,896]{1,0:T(8,128)(2,1)} %tokens_hbm.1) | copy-start | bytes 688132
  0.9 0.7 %copy-start.4 = (s32[128,8]{0,1:T(8,128)S(1)}, s32[128,8]{0,1:T(8,128)}, u32[]{:S(2)}) copy-start(s32[128,8]{0,1:T(8,128)} %param.8) | copy-start | bytes 12292
  1.6 0.7 %copy-start.5 = (f32[128,8]{0,1:T(8,128)S(1)}, f32[128,8]{0,1:T(8,128)}, u32[]{:S(2)}) copy-start(f32[128,8]{0,1:T(8,128)} %param.9) | copy-start | bytes 12292
  2.3 0.7 copy-start.6
  22.3 1.7 %collective-permute-start.1 = (bf16[64,2688]{1,0:T(8,128)(2,1)S(1)}, bf16[64,2688]{1,0:T(8,128)(2,1)S(1)}, u32[]{:S(2)}, u32[]{:S(2)}) collective-permute-start(bf16[64,2688]{1,0:T(8,128)(2,1)S(1)} %bitcast.7), channel_id=1, source_target_pairs={{0,1},{1,0},{2,3},{3,2},{4,5},{5,4},{6,7},{7,6},{8,9},{9,8},{10,11... | collective-permute-start | bytes 1032200 | tf_op jit(solution)/shard_map/ppermute | solution.py:202
  22.3 14.2 %collective-permute-start = (bf16[64,2688]{1,0:T(8,128)(2,1)S(1)}, bf16[64,2688]{1,0:T(8,128)(2,1)S(1)}, u32[]{:S(2)}, u32[]{:S(2)}) collective-permute-start(bf16[64,2688]{1,0:T(8,128)(2,1)S(1)} %bitcast.8), channel_id=1, source_target_pairs={{0,2},{1,3},{2,0},{3,1},{4,6},{5,7},{6,4},{7,5},{8,10},{9,11},{10,... | collective-permute-start | bytes 1032200 | tf_op jit(solution)/shard_map/ppermute | solution.py:202
  23.9 2.0 %copy-start = (bf16[2,3584,256]{2,1,0:T(8,128)(2,1)S(1)}, bf16[2,3584,256]{2,1,0:T(8,128)(2,1)}, u32[]{:S(2)}) copy-start(bf16[2,3584,256]{2,1,0:T(8,128)(2,1)} %gate_hbm.1) | copy-start | bytes 11010052
  25.9 2.0 %copy-start.1 = (bf16[2,3584,256]{2,1,0:T(8,128)(2,1)S(1)}, bf16[2,3584,256]{2,1,0:T(8,128)(2,1)}, u32[]{:S(2)}) copy-start(bf16[2,3584,256]{2,1,0:T(8,128)(2,1)} %up_hbm.1) | copy-start | bytes 11010052
  28.0 2.0 %copy-start.2 = (bf16[2,256,3584]{2,1,0:T(8,128)(2,1)S(1)}, bf16[2,256,3584]{2,1,0:T(8,128)(2,1)}, u32[]{:S(2)}) copy-start(bf16[2,256,3584]{2,1,0:T(8,128)(2,1)} %down_hbm.1) | copy-start | bytes 11010052
  36.4 1.7 %collective-permute-start.2 = (bf16[64,2688]{1,0:T(8,128)(2,1)S(1)}, bf16[64,2688]{1,0:T(8,128)(2,1)S(1)}, u32[]{:S(2)}, u32[]{:S(2)}) collective-permute-start(bf16[64,2688]{1,0:T(8,128)(2,1)S(1)} %collective-permute-done.refs_0_), channel_id=1, source_target_pairs={{0,1},{1,0},{2,3},{3,2},{4,5},{5,4},{6,7},{7,6},{8,9},{9,8},{10,11... | collective-permute-start | bytes 1032200 | tf_op jit(solution)/shard_map/ppermute | solution.py:202
  39.2 1.7 %collective-permute-start.4 = (bf16[64,2688]{1,0:T(8,128)(2,1)S(1)}, bf16[64,2688]{1,0:T(8,128)(2,1)S(1)}, u32[]{:S(2)}, u32[]{:S(2)}) collective-permute-start(bf16[64,2688]{1,0:T(8,128)(2,1)S(1)} %get-tuple-element.40), channel_id=1, source_target_pairs={{0,1},{1,0},{2,3},{3,2},{4,5},{5,4},{6,7},{7,6},{8,9},{9,8},{10,11... | collective-permute-start | bytes 1032200 | tf_op jit(solution)/shard_map/ppermute | solution.py:202
  39.8 2.7 %collective-permute-start.3 = (bf16[64,2688]{1,0:T(8,128)(2,1)S(1)}, bf16[64,2688]{1,0:T(8,128)(2,1)S(1)}, u32[]{:S(2)}, u32[]{:S(2)}) collective-permute-start(bf16[64,2688]{1,0:T(8,128)(2,1)S(1)} %get-tuple-element.38), channel_id=1, source_target_pairs={{0,1},{1,0},{2,3},{3,2},{4,5},{5,4},{6,7},{7,6},{8,9},{9,8},{10,11... | collective-permute-start | bytes 1032200 | tf_op jit(solution)/shard_map/ppermute | solution.py:202
  41.0 10.2 %collective-permute-start.5 = (bf16[64,2688]{1,0:T(8,128)(2,1)S(1)}, bf16[64,2688]{1,0:T(8,128)(2,1)S(1)}, u32[]{:S(2)}, u32[]{:S(2)}) collective-permute-start(bf16[64,2688]{1,0:T(8,128)(2,1)S(1)} %add_convert_fusion.1), channel_id=1, source_target_pairs={{0,2},{1,3},{2,0},{3,1},{4,6},{5,7},{6,4},{7,5},{8,10},{9,11},{10,... | collective-permute-start | bytes 1032200 | tf_op jit(solution)/shard_map/ppermute | solution.py:202

commit v3 on v2

--- a/solution.py
+++ b/solution.py
@@ -194,7 +194,7 @@
         scratch_shapes=list(scratch),
         compiler_params=pltpu.CompilerParams(vmem_limit_bytes=LIMIT),
         cost_estimate=pl.CostEstimate(flops=flops, bytes_accessed=moved, transcendentals=0),
-    )(*args)
+    )(*[pltpu.with_memory_space_constraint(a, s.memory_space) for a, s in zip(args, specs)])
 
 
 def swapped(value, axis, mask):

time: 66.5 us -> 59.9 us (0.901)
  local copies, waits for them, and re-layouts: 9.08 us -> 0 us
  waiting for transfers between devices: 10.9 us -> 14.9 us
  Pallas kernels: 10.1 us -> 8.98 us
    unnamed x14 -> x0, local copies, waits for them, and re-layouts: 9.08 us -> none
    ppermute x6, waiting for transfers between devices: 10.9 us -> 14.9 us  [swapped(): lax.ppermute(value, axis, [(source, source ^ mask) for source in range(co...]
    pallas_call x5, Pallas kernels: 10.1 us -> 8.98 us  [call(): pl.pallas_call(kernel, out_shape=outs, in_specs=specs, out_specs=[VMEM] *...]
  transfers between devices with their start and end apart: 6 -> 6, of which waited for: 4 -> 5; matrix products, arithmetic and copies ran while one was open for 0% -> 0% of each run, Pallas kernels for 10% -> 9%
where the time goes in v3:
time: 59.9 us; the launch traced here: 59.7 us
  blocking collectives  31.9 us (53%)
  waiting for transfers between devices  14.9 us (25%)
  Pallas kernels  8.98 us (15%)
  starting transfers between devices  3.69 us (6%)
    all_to_all x2, blocking collectives, exchanged(): lax.all_to_all(value, 'expert', split_axis=0, concat_axis=0, tiled=True)  31.9 us
    ppermute x6, waiting for transfers between devices, swapped(): lax.ppermute(value, axis, [(source, source ^ mask) for source in range(co...  14.9 us
    pallas_call x5, Pallas kernels, call(): pl.pallas_call(kernel, out_shape=outs, in_specs=specs, out_specs=[VMEM] *...  8.98 us
    ppermute x6, starting transfers between devices, swapped(): lax.ppermute(value, axis, [(source, source ^ mask) for source in range(co...  3.69 us
  transfers between devices with their start and end apart: 6, of which 5 were waited for; matrix products, arithmetic and copies ran while one was open for 0% of the time, Pallas kernels for 9%

profile of v3, /device:TPU:0, one launch (start us, length us, event | category | flops | bytes accessed | tf_op | source)
XLA Modules:
  0.0 59.7 jit_solution(2249020791228907470)
XLA Ops:
  0.0 1.3 %shard_map.73 = (bf16[64,2688]{1,0:T(8,128)(2,1)S(1)}, bf16[3,64,128]{2,1,0:T(8,128)(2,1)S(1)}, bf16[3,64,128]{2,1,0:T(8,128)(2,1)S(1)}) custom-call(s32[8]{0:T(128)} %plan_hbm.3, s32[8,128]{1,0:T(8,128)} %bitcast.12, f32[8,128]{1,0:T(8,128)} %bitcast.13, bf16[128,896]{1,0:T(8,128)(2,1)} %tokens_hbm.1), custom_call_target="tpu_custom_call" | custom-call | bytes 679968 | tf_op jit(solution)/shard_map/pallas_call | solution.py:189
  1.3 18.3 %all_to_all.10 = bf16[8,8,2688]{2,1,0:T(8,128)(2,1)S(1)} all-to-all(bf16[8,8,2688]{2,1,0:T(8,128)(2,1)S(1)} %bitcast.11), channel_id=1, replica_groups=mesh['expert'=8,'dp'=4] {'expert'}, dimensions={0} | all-to-all | bytes 688128 | tf_op jit(solution)/shard_map/all_to_all | solution.py:237
  19.6 0.0 collective-permute-start.1
  19.6 1.5 %collective-permute-start = (bf16[64,2688]{1,0:T(8,128)(2,1)S(1)}, bf16[64,2688]{1,0:T(8,128)(2,1)S(1)}, u32[]{:S(2)}, u32[]{:S(2)}) collective-permute-start(bf16[64,2688]{1,0:T(8,128)(2,1)S(1)} %bitcast.8), channel_id=1, source_target_pairs={{0,2},{1,3},{2,0},{3,1},{4,6},{5,7},{6,4},{7,5},{8,10},{9,11},{10,... | collective-permute-start | bytes 1032200 | tf_op jit(solution)/shard_map/ppermute | solution.py:202
  21.1 0.2 collective-permute-done.1.refs_1_
  21.2 5.0 %shard_map.74 = (f32[192,256]{1,0:T(8,128)S(1)}, f32[192,256]{1,0:T(8,128)S(1)}, bf16[2,1792,256]{2,1,0:T(8,128)(2,1)S(1)}, bf16[2,1792,256]{2,1,0:T(8,128)(2,1)S(1)}, bf16[2,256,3584]{2,1,0:T(8,128)(2,1)S(1)}) custom-call(s32[8]{0:T(128)} %plan_hbm.3, bf16[2,3584,256]{2,1,0:T(8,128)(2,1)} %gate_hbm.1, bf16[2,3584,256]{2,1,0:T(8,128)(2,1)} %up_hbm.1, ...), custom_call_target="tpu_custom_call" | custom-call | flops 352321536 | bytes 19431456 | tf_op jit(solution)/shard_map/pallas_call | solution.py:189
  26.2 3.8 %collective-permute-done.refs_0_ = bf16[64,2688]{1,0:T(8,128)(2,1)S(1)} collective-permute-done((bf16[64,2688]{1,0:T(8,128)(2,1)S(1)}, bf16[64,2688]{1,0:T(8,128)(2,1)S(1)}, u32[]{:S(2)}, u32[]{:S(2)}) %collective-permute-start) | collective-permute-done | bytes 344096 | tf_op jit(solution)/shard_map/ppermute | solution.py:202
  30.0 0.0 collective-permute-start.2
  30.0 1.6 %collective-permute-done.2.refs_1_ = bf16[64,2688]{1,0:T(8,128)(2,1)S(1)} collective-permute-done((bf16[64,2688]{1,0:T(8,128)(2,1)S(1)}, bf16[64,2688]{1,0:T(8,128)(2,1)S(1)}, u32[]{:S(2)}, u32[]{:S(2)}) %collective-permute-start.2) | collective-permute-done | bytes 344096 | tf_op jit(solution)/shard_map/ppermute | solution.py:202
  31.7 1.0 %shard_map.75 = (bf16[192,256]{1,0:T(8,128)(2,1)S(1)}, bf16[64,2688]{1,0:T(8,128)(2,1)S(1)}, bf16[64,2688]{1,0:T(8,128)(2,1)S(1)}) custom-call(bf16[64,2688]{1,0:T(8,128)(2,1)S(1)} %collective-permute-done.refs_0_, bf16[64,2688]{1,0:T(8,128)(2,1)S(1)} %collective-permute-done.2.refs_1_, f32[192,256]{1,0:T(8,128)S(1)} %get-tuple-element.31.refs_2_, ...), custom_call_target="tpu_custom_call" | custom-call | flops 528482304 | bytes 9207808 | tf_op jit(solution)/shard_map/pallas_call | solution.py:189
  32.7 0.2 collective-permute-start.4
  32.9 0.4 shard_map.76
  33.4 0.4 collective-permute-start.3
  33.8 0.7 %collective-permute-done.4 = bf16[64,2688]{1,0:T(8,128)(2,1)S(1)} collective-permute-done((bf16[64,2688]{1,0:T(8,128)(2,1)S(1)}, bf16[64,2688]{1,0:T(8,128)(2,1)S(1)}, u32[]{:S(2)}, u32[]{:S(2)}) %collective-permute-start.4) | collective-permute-done | bytes 344096 | tf_op jit(solution)/shard_map/ppermute | solution.py:202
  34.5 0.1 add_convert_fusion.1
  34.5 1.6 %collective-permute-start.5 = (bf16[64,2688]{1,0:T(8,128)(2,1)S(1)}, bf16[64,2688]{1,0:T(8,128)(2,1)S(1)}, u32[]{:S(2)}, u32[]{:S(2)}) collective-permute-start(bf16[64,2688]{1,0:T(8,128)(2,1)S(1)} %add_convert_fusion.1), channel_id=1, source_target_pairs={{0,2},{1,3},{2,0},{3,1},{4,6},{5,7},{6,4},{7,5},{8,10},{9,11},{10,... | collective-permute-start | bytes 1032200 | tf_op jit(solution)/shard_map/ppermute | solution.py:202
  36.1 0.0 collective-permute-done.3
  36.1 8.6 %collective-permute-done.5 = bf16[64,2688]{1,0:T(8,128)(2,1)S(1)} collective-permute-done((bf16[64,2688]{1,0:T(8,128)(2,1)S(1)}, bf16[64,2688]{1,0:T(8,128)(2,1)S(1)}, u32[]{:S(2)}, u32[]{:S(2)}) %collective-permute-start.5) | collective-permute-done | bytes 344096 | tf_op jit(solution)/shard_map/ppermute | solution.py:202
  44.7 0.1 fusion
  44.8 13.6 %all_to_all.11 = bf16[8,8,2688]{2,1,0:T(8,128)(2,1)S(1)} all-to-all(bf16[8,8,2688]{2,1,0:T(8,128)(2,1)S(1)} %fusion), channel_id=1, replica_groups=mesh['expert'=8,'dp'=4] {'expert'}, dimensions={0} | all-to-all | bytes 688128 | tf_op jit(solution)/shard_map/all_to_all | solution.py:237
  58.4 1.2 %shard_map.77 = bf16[128,896]{1,0:T(8,128)(2,1)} custom-call(bf16[64,2688]{1,0:T(8,128)(2,1)S(1)} %bitcast.10, bf16[3,64,128]{2,1,0:T(8,128)(2,1)S(1)} %get-tuple-element.41.mix_high, bf16[3,64,128]{2,1,0:T(8,128)(2,1)S(1)} %get-tuple-element.42.mix_low), custom_call_target="tpu_custom_call" | custom-call | bytes 671744 | tf_op jit(solution)/shard_map/pallas_call | solution.py:189
Async XLA Ops:
  19.6 1.7 %collective-permute-start.1 = (bf16[64,2688]{1,0:T(8,128)(2,1)S(1)}, bf16[64,2688]{1,0:T(8,128)(2,1)S(1)}, u32[]{:S(2)}, u32[]{:S(2)}) collective-permute-start(bf16[64,2688]{1,0:T(8,128)(2,1)S(1)} %bitcast.7), channel_id=1, source_target_pairs={{0,1},{1,0},{2,3},{3,2},{4,5},{5,4},{6,7},{7,6},{8,9},{9,8},{10,11... | collective-permute-start | bytes 1032200 | tf_op jit(solution)/shard_map/ppermute | solution.py:202
  19.6 10.5 %collective-permute-start = (bf16[64,2688]{1,0:T(8,128)(2,1)S(1)}, bf16[64,2688]{1,0:T(8,128)(2,1)S(1)}, u32[]{:S(2)}, u32[]{:S(2)}) collective-permute-start(bf16[64,2688]{1,0:T(8,128)(2,1)S(1)} %bitcast.8), channel_id=1, source_target_pairs={{0,2},{1,3},{2,0},{3,1},{4,6},{5,7},{6,4},{7,5},{8,10},{9,11},{10,... | collective-permute-start | bytes 1032200 | tf_op jit(solution)/shard_map/ppermute | solution.py:202
  30.0 1.7 %collective-permute-start.2 = (bf16[64,2688]{1,0:T(8,128)(2,1)S(1)}, bf16[64,2688]{1,0:T(8,128)(2,1)S(1)}, u32[]{:S(2)}, u32[]{:S(2)}) collective-permute-start(bf16[64,2688]{1,0:T(8,128)(2,1)S(1)} %collective-permute-done.refs_0_), channel_id=1, source_target_pairs={{0,1},{1,0},{2,3},{3,2},{4,5},{5,4},{6,7},{7,6},{8,9},{9,8},{10,11... | collective-permute-start | bytes 1032200 | tf_op jit(solution)/shard_map/ppermute | solution.py:202
  32.7 1.7 %collective-permute-start.4 = (bf16[64,2688]{1,0:T(8,128)(2,1)S(1)}, bf16[64,2688]{1,0:T(8,128)(2,1)S(1)}, u32[]{:S(2)}, u32[]{:S(2)}) collective-permute-start(bf16[64,2688]{1,0:T(8,128)(2,1)S(1)} %get-tuple-element.40), channel_id=1, source_target_pairs={{0,1},{1,0},{2,3},{3,2},{4,5},{5,4},{6,7},{7,6},{8,9},{9,8},{10,11... | collective-permute-start | bytes 1032200 | tf_op jit(solution)/shard_map/ppermute | solution.py:202
  33.4 2.7 %collective-permute-start.3 = (bf16[64,2688]{1,0:T(8,128)(2,1)S(1)}, bf16[64,2688]{1,0:T(8,128)(2,1)S(1)}, u32[]{:S(2)}, u32[]{:S(2)}) collective-permute-start(bf16[64,2688]{1,0:T(8,128)(2,1)S(1)} %get-tuple-element.38), channel_id=1, source_target_pairs={{0,1},{1,0},{2,3},{3,2},{4,5},{5,4},{6,7},{7,6},{8,9},{9,8},{10,11... | collective-permute-start | bytes 1032200 | tf_op jit(solution)/shard_map/ppermute | solution.py:202
  34.5 10.2 %collective-permute-start.5 = (bf16[64,2688]{1,0:T(8,128)(2,1)S(1)}, bf16[64,2688]{1,0:T(8,128)(2,1)S(1)}, u32[]{:S(2)}, u32[]{:S(2)}) collective-permute-start(bf16[64,2688]{1,0:T(8,128)(2,1)S(1)} %add_convert_fusion.1), channel_id=1, source_target_pairs={{0,2},{1,3},{2,0},{3,1},{4,6},{5,7},{6,4},{7,5},{8,10},{9,11},{10,... | collective-permute-start | bytes 1032200 | tf_op jit(solution)/shard_map/ppermute | solution.py:202

commit v4 on v1

v4 whole, which is shorter than its diff:
```python
import functools

import jax
import jax.numpy as jnp
from jax import lax
from jax.experimental import pallas as pl
from jax.experimental.pallas import tpu as pltpu
from jax.sharding import PartitionSpec as P

CAP = 8
F32 = jnp.float32
BF16 = jnp.bfloat16
HBM = pl.BlockSpec(memory_space=pltpu.HBM)
VMEM = pl.BlockSpec(memory_space=pltpu.VMEM)
LIMIT = 20 * 2**20


def dot(left, right):
    return jnp.dot(left, right, preferred_element_type=F32)


def dot_rows(left, right):
    return lax.dot_general(left, right, (((0,), (0,)), ((), ())), preferred_element_type=F32)


def route_kernel(owned, low, plan_hbm, ids_hbm, gates_hbm, tokens_hbm, *refs):
    lots, (info, mix_high, mix_low) = refs[:low], refs[low : low + 3]
    plan, ids, gates, tokens, place, weight, sems = refs[low + 3 :]
    sources = (plan_hbm, ids_hbm, gates_hbm, tokens_hbm)
    copies = [
        pltpu.make_async_copy(source, target, sems.at[n])
        for n, (source, target) in enumerate(zip(sources, (plan, ids, gates, tokens)))
    ]
    for copy in copies:
        copy.start()
    choices, tok_rows = ids.shape
    share = tokens.shape[1]
    owners = plan.shape[0]
    high = owners // low
    experts = owners * owned
    own_index = lax.axis_index("expert")
    row = lax.broadcasted_iota(jnp.int32, (tok_rows, tok_rows), 0)
    col = lax.broadcasted_iota(jnp.int32, (tok_rows, tok_rows), 1)
    earlier = (row < col).astype(F32).astype(BF16)
    expert = lax.broadcasted_iota(jnp.int32, (experts, tok_rows), 0)
    owner = expert // owned
    within = expert - owner * owned
    named = jnp.zeros((experts, tok_rows), F32)
    weights = jnp.zeros((experts, tok_rows), F32)
    hot = jnp.zeros((experts, tok_rows), jnp.int32)
    copies[0].wait()
    for host in range(owners):
        source = (host + owners // 2) % owners
        hot = jnp.where(owner == source, plan[host] - source * owned, hot)
    own_hot = plan[lax.rem(own_index + owners // 2, owners)] - own_index * owned
    info[...] = jnp.full(info.shape, own_hot, jnp.int32)
    copies[1].wait()
    copies[2].wait()
    for choice in range(choices):
        hit = expert == ids[choice : choice + 1, :]
        named = named + hit.astype(F32)
        weights = weights + jnp.where(hit, gates[choice : choice + 1, :], 0.0)
    weight[...] = weights
    rank = dot(named.astype(BF16), earlier).astype(jnp.int32)
    limit = jnp.where(within == hot, 2 * CAP, CAP)
    start = jnp.where(within == hot, 0, CAP * (1 + within + (within < hot).astype(jnp.int32)))
    place[...] = jnp.where((named > 0.0) & (rank < limit), start + rank, -1)
    slot = lax.broadcasted_iota(jnp.int32, (CAP, tok_rows), 0)
    zero = jnp.zeros((CAP, tok_rows), F32)
    copies[3].wait()
    for chunk in range(owned + 1):
        picks, mixes = [], []
        for m in range(low):
            for k in range(high):
                index = own_index ^ (k * low + m)
                pick, mix = zero, zero
                for number in range(owned):
                    line = pl.ds(index * owned + number, 1)
                    match = place[line, :] == slot + chunk * CAP
                    pick = pick + match.astype(F32)
                    mix = mix + jnp.where(match, weight[line, :], 0.0)
                picks.append(pick)
                mixes.append(mix)
        pick = jnp.concatenate(picks, axis=0).astype(BF16)
        values = dot(pick, tokens[...]).astype(BF16)
        for m, lot in enumerate(lots):
            lines = slice(m * high * CAP, (m + 1) * high * CAP)
            lot[:, chunk * share : (chunk + 1) * share] = values[lines]
        straight = [mixes[k] if m == 0 else zero for k in range(high) for m in range(low)]
        mix = jnp.concatenate(straight + mixes[high:], axis=0)
        rounded = mix.astype(BF16)
        mix_high[chunk] = rounded
        mix_low[chunk] = (mix - rounded.astype(F32)).astype(BF16)


def join_kernel(low, *refs):
    lots, pieces = refs[:low], refs[low:]
    values = [lot[...].astype(F32) for lot in lots]
    for k, piece in enumerate(pieces):
        rows = [value[k * CAP : (k + 1) * CAP] for value in values]
        piece[...] = jnp.concatenate(rows, axis=0).astype(BF16)


def split_kernel(high, *refs):
    pieces, lots = refs[:high], refs[high:]
    values = [piece[...].astype(F32) for piece in pieces]
    for m, lot in enumerate(lots):
        rows = [value[(m + 1) * CAP : (m + 2) * CAP] for value in values]
        lot[...] = jnp.concatenate(rows, axis=0).astype(BF16)


def groups_of(owned):
    return [(0, 1)] + [(number + 1,) for number in range(1, owned)]


def order_of(info, owned):
    hot = jnp.max(info[...].astype(F32)).astype(jnp.int32)
    return [hot] + [n + (n >= hot).astype(jnp.int32) for n in range(owned - 1)]


def features_of(m, share):
    return pl.ds(pl.multiple_of((lax.axis_index("dp") ^ m) * share, share), share)


def projections(order, numbers, blocks, gate, up):
    owned = gate.shape[0]
    share = blocks[0][0].shape[1] // (owned + 1)
    for group, chunks in enumerate(groups_of(owned)):
        gate_value = up_value = None
        for m, pieces in zip(numbers, blocks):
            rows = jnp.concatenate(
                [p[:, c * share : (c + 1) * share] for c in chunks for p in pieces], axis=0
            )
            gate_part = dot(rows, gate[order[group], features_of(m, share), :])
            up_part = dot(rows, up[order[group], features_of(m, share), :])
            gate_value = gate_part if gate_value is None else gate_value + gate_part
            up_value = up_part if up_value is None else up_value + up_part
        yield chunks, gate_value, up_value


def listed(refs, count, size):
    return [refs[n * size : (n + 1) * size] for n in range(count)], refs[count * size :]


def near_kernel(near, high, info, gate, up, *refs):
    blocks, (gate_out, up_out) = listed(refs, len(near), high)
    lines = high * blocks[0][0].shape[0]
    order = order_of(info, gate.shape[0])
    for chunks, gate_value, up_value in projections(order, near, blocks, gate, up):
        place = slice(chunks[0] * lines, (chunks[-1] + 1) * lines)
        gate_out[place, :] = gate_value
        up_out[place, :] = up_value


def down_parts(order, numbers, hidden, down, outs):
    owned = down.shape[0]
    lines, wide = outs[0].shape
    share = wide // (owned + 1)
    for m, out in zip(numbers, outs):
        for group, chunks in enumerate(groups_of(owned)):
            rows = hidden[chunks[0] * lines : (chunks[-1] + 1) * lines, :]
            value = dot(rows, down[order[group], :, features_of(m, share)]).astype(out.dtype)
            for spot, chunk in enumerate(chunks):
                out[:, chunk * share : (chunk + 1) * share] = value[spot * lines : (spot + 1) * lines]


def far_kernel(far, high, info, gate, up, down, gate_in, up_in, *refs):
    blocks, (hidden, *outs) = listed(refs, len(far), high)
    lines = outs[0].shape[0]
    order = order_of(info, gate.shape[0])
    for chunks, gate_value, up_value in projections(order, far, blocks, gate, up):
        place = slice(chunks[0] * lines, (chunks[-1] + 1) * lines)
        gate_value = gate_value + gate_in[place, :]
        up_value = up_value + up_in[place, :]
        hidden[place, :] = (jax.nn.silu(gate_value) * up_value).astype(BF16)
    down_parts(order, far, hidden, down, outs)


def own_kernel(near, info, down, hidden, *outs):
    down_parts(order_of(info, down.shape[0]), near, hidden, down, outs)


def sum_kernel(count, *refs):
    terms, pieces = refs[:count], refs[count:]
    size = pieces[0].shape[0]
    for k, piece in enumerate(pieces):
        total = sum(term[k * size : (k + 1) * size, :].astype(F32) for term in terms)
        piece[...] = total.astype(piece.dtype)


def mix_kernel(count, mix_high, mix_low, *refs):
    arrays, out = refs[:count], refs[count]
    share = out.shape[1]
    total = jnp.zeros(out.shape, F32)
    for chunk in range(mix_high.shape[0]):
        rows = jnp.concatenate([a[:, chunk * share : (chunk + 1) * share] for a in arrays], axis=0)
        total = total + dot_rows(mix_high[chunk], rows) + dot_rows(mix_low[chunk], rows)
    out[...] = total.astype(out.dtype)


def call(kernel, outs, *args, specs=None, scratch=(), flops=0):
    moved = sum(a.size * a.dtype.itemsize for a in (*args, *outs))
    if specs:
        args = [
            pltpu.with_memory_space_constraint(a, s.memory_space) for a, s in zip(args, specs)
        ]
    return pl.pallas_call(
        kernel,
        out_shape=outs,
        in_specs=specs or [VMEM] * len(args),
        out_specs=[VMEM] * len(outs),
        scratch_shapes=list(scratch),
        compiler_params=pltpu.CompilerParams(vmem_limit_bytes=LIMIT),
        cost_estimate=pl.CostEstimate(flops=flops, bytes_accessed=moved, transcendentals=0),
    )(*args)


def swapped(value, axis, mask):
    count = lax.axis_size(axis)
    return lax.ppermute(value, axis, [(source, source ^ mask) for source in range(count)])


def per_device(tokens, expert_ids, gate_weights, replica_plan, w_gate, w_up, w_down):
    owners = lax.axis_size("expert")
    parts = lax.axis_size("dp")
    owned, model_width, hidden_share = w_gate.shape
    tok_rows, share = tokens.shape
    choices = expert_ids.shape[1]
    chunks = owned + 1
    lines = owners * CAP
    wide = chunks * share
    low = 1 << ((owners.bit_length() - 1) // 2)
    high = owners // low
    shape = jax.ShapeDtypeStruct
    lot = shape((high * CAP, wide), BF16)
    piece = shape((low * CAP, wide), BF16)
    whole = shape((lines, wide), BF16)
    mixes = shape((chunks, lines + (low - 1) * high * CAP, tok_rows), BF16)

    *lots, info, mix_high, mix_low = call(
        functools.partial(route_kernel, owned, low),
        [lot] * low + [shape((8, 128), jnp.int32), mixes, mixes],
        replica_plan, expert_ids.T, gate_weights.T, tokens,
        specs=[HBM] * 4,
        scratch=[
            pltpu.SMEM((owners,), jnp.int32),
            pltpu.VMEM((choices, tok_rows), jnp.int32),
            pltpu.VMEM((choices, tok_rows), F32),
            pltpu.VMEM((tok_rows, share), BF16),
            pltpu.VMEM((owners * owned, tok_rows), jnp.int32),
            pltpu.VMEM((owners * owned, tok_rows), F32),
            pltpu.SemaphoreType.DMA((4,)),
        ],
        flops=4 * 10**10,
    )
    lots = [lots[0]] + [swapped(lots[m], "expert", m) for m in range(1, low)]
    pieces = call(functools.partial(join_kernel, low), [piece] * high, *lots)
    arrived = {k: swapped(pieces[k], "expert", k * low) for k in range(high - 1, 0, -1)}
    arrived[0] = pieces[0]

    near = [m for m in range(parts) if m < parts // 2]
    far = [m for m in range(parts) if m >= parts // 2]
    top = parts // 2
    blocks = {m: {} for m in range(parts)}
    for k in range(high):
        blocks[0][k] = arrived[k]
        blocks[top][k] = swapped(arrived[k], "dp", top)
        mask = top // 2
        while mask:
            for m in range(0, parts, 2 * mask):
                blocks[m ^ mask][k] = swapped(blocks[m][k], "dp", mask)
            mask //= 2

    def flat(numbers):
        return [blocks[m][k] for m in numbers for k in range(high)]

    near_flops = 4 * len(near) * chunks * lines * share * hidden_share
    sums = [shape((chunks * lines, hidden_share), F32)] * 2
    gate_sum, up_sum = call(
        functools.partial(near_kernel, near, high),
        sums,
        info, w_gate, w_up, *flat(near),
        flops=near_flops,
    )
    hidden, *far_outs = call(
        functools.partial(far_kernel, far, high),
        [shape((chunks * lines, hidden_share), BF16)] + [whole] * len(far),
        info, w_gate, w_up, w_down, gate_sum, up_sum, *flat(far),
        flops=near_flops * 3 // 2,
    )

    def reduced(found):
        mask = 1
        while 2 * mask < top:
            for m in [m for m in found if m & mask]:
                there = swapped(found.pop(m), "dp", mask)
                (found[m ^ mask],) = call(
                    functools.partial(sum_kernel, 2), [whole], found[m ^ mask], there
                )
            mask *= 2
        terms = []
        for m, value in found.items():
            terms.append(swapped(value, "dp", mask) if m & mask else value)
        return call(functools.partial(sum_kernel, len(terms)), [piece] * high, *terms)

    far_pieces = reduced(dict(zip(far, far_outs)))
    crossed = {k: swapped(far_pieces[k], "dp", top) for k in range(high - 1, -1, -1)}
    near_outs = call(
        functools.partial(own_kernel, near),
        [whole] * len(near),
        info, w_down, hidden,
        flops=near_flops // 2,
    )
    near_pieces = reduced(dict(zip(near, near_outs)))
    back = {}
    for k in range(high - 1, -1, -1):
        (total,) = call(functools.partial(sum_kernel, 2), [piece], near_pieces[k], crossed[k])
        back[k] = swapped(total, "expert", k * low) if k else total
    back = [back[k] for k in range(high)]
    others = call(functools.partial(split_kernel, high), [lot] * (low - 1), *back)
    others = [swapped(others[m - 1], "expert", m) for m in range(1, low)]
    (mixed_out,) = call(
        functools.partial(mix_kernel, high + low - 1),
        [shape((tok_rows, share), BF16)],
        mix_high, mix_low, *back, *others,
    )
    return mixed_out


def solution(mesh):
    in_specs = (
        P("expert", "dp"),
        P("expert", None),
        P("expert", None),
        P(),
        P("expert", None, "dp"),
        P("expert", None, "dp"),
        P("expert", "dp", None),
    )
    out_specs = P("expert", "dp")
    return jax.shard_map(
        per_device, mesh=mesh, in_specs=in_specs, out_specs=out_specs, check_vma=False
    )
```

time: 73.1 us -> 54.5 us (0.75)
  blocking collectives: 34.2 us -> 0 us
  starting transfers between devices: 3.7 us -> 25.1 us
  local copies, waits for them, and re-layouts: 12.4 us -> 0.79 us
  waiting for transfers between devices: 15.1 us -> 22.8 us
    all_to_all x2 -> x0, blocking collectives: 34.2 us -> none  [exchanged(): lax.all_to_all(value, 'expert', split_axis=0, concat_axis=0, tiled=True)]
    ppermute x6 -> x26, starting transfers between devices: 3.7 us -> 25.1 us  [swapped(): lax.ppermute(value, axis, [(source, source ^ mask) for source in range(co...]
    unnamed x16 -> x6, local copies, waits for them, and re-layouts: 11.1 us -> 0.79 us
    ppermute x6 -> x26, waiting for transfers between devices: 15.1 us -> 22.8 us  [swapped(): lax.ppermute(value, axis, [(source, source ^ mask) for source in range(co...]
    dynamic_slice x1 -> x0, local copies, waits for them, and re-layouts: 1.24 us -> none  [per_device(): hot = replica_plan[(own_index + owners // 2) % owners] - own_index * owned]
    pallas_call x5 -> x13, Pallas kernels: 6.26 us -> 5.57 us  [call(): pl.pallas_call(kernel, out_shape=outs, in_specs=specs or [VMEM] * len(arg...]
  transfers between devices with their start and end apart: 6 -> 26, of which waited for: 3 -> 11; matrix products, arithmetic and copies ran while one was open for 2% -> 0% of each run, Pallas kernels for 3% -> 3%
where the time goes in v4:
time: 54.5 us; the launch traced here: 54.4 us
  starting transfers between devices  25.1 us (46%)
  waiting for transfers between devices  22.8 us (42%)
  Pallas kernels  5.57 us (10%)
  local copies, waits for them, and re-layouts  0.79 us (1%)
    ppermute x26, starting transfers between devices, swapped(): lax.ppermute(value, axis, [(source, source ^ mask) for source in range(co...  25.1 us
    ppermute x26, waiting for transfers between devices, swapped(): lax.ppermute(value, axis, [(source, source ^ mask) for source in range(co...  22.8 us
    pallas_call x13, Pallas kernels, call(): pl.pallas_call(kernel, out_shape=outs, in_specs=specs or [VMEM] * len(arg...  5.57 us
  transfers between devices with their start and end apart: 26, of which 11 were waited for; matrix products, arithmetic and copies ran while one was open for 0% of the time, Pallas kernels for 3%

profile of v4, /device:TPU:0, one launch (start us, length us, event | category | flops | bytes accessed | tf_op | source)
XLA Modules:
  0.0 54.4 jit_solution(14691742093563066694)
XLA Ops:
  0.0 1.4 %shard_map.73 = (bf16[32,2688]{1,0:T(8,128)(2,1)S(1)}, bf16[32,2688]{1,0:T(8,128)(2,1)S(1)}, s32[8,128]{1,0:T(8,128)S(1)}, bf16[3,96,128]{2,1,0:T(8,128)(2,1)S(1)}, bf16[3,96,128]{2,1,0:T(8,128)(2,1)S(1)}) custom-call(s32[8]{0:T(128)} %plan_hbm.1, s32[8,128]{1,0:T(8,128)} %bitcast.2, f32[8,128]{1,0:T(8,128)} %bitcast.3, bf16[128,896]{1,0:T(8,128)(2,1)} %tokens_hbm.1), custom_call_target="tpu_custom_call" | custom-call | flops 40000000000 | bytes 733216 | tf_op jit(solution)/shard_map/pallas_call | solution.py:207
  1.4 3.0 %collective-permute-start = (bf16[32,2688]{1,0:T(8,128)(2,1)S(1)}, bf16[32,2688]{1,0:T(8,128)(2,1)S(1)}, u32[]{:S(2)}, u32[]{:S(2)}) collective-permute-start(bf16[32,2688]{1,0:T(8,128)(2,1)S(1)} %get-tuple-element.33), channel_id=1, source_target_pairs={{0,4},{4,0},{8,12},{12,8},{16,20},{20,16},{24,28},{28,24},{1,5},{5... | collective-permute-start | bytes 516104 | tf_op jit(solution)/shard_map/ppermute | solution.py:220
  4.5 4.4 %collective-permute-done.refs_1_ = bf16[32,2688]{1,0:T(8,128)(2,1)S(1)} collective-permute-done((bf16[32,2688]{1,0:T(8,128)(2,1)S(1)}, bf16[32,2688]{1,0:T(8,128)(2,1)S(1)}, u32[]{:S(2)}, u32[]{:S(2)}) %collective-permute-start) | collective-permute-done | bytes 172064 | tf_op jit(solution)/shard_map/ppermute | solution.py:220
  8.9 1.9 %collective-permute-start.1 = (bf16[16,2688]{1,0:T(8,128)(2,1)S(1)}, bf16[16,2688]{1,0:T(8,128)(2,1)S(1)}, u32[]{:S(2)}, u32[]{:S(2)}) collective-permute-start(bf16[16,2688]{1,0:T(8,128)(2,1)S(1)} %get-tuple-element.35), channel_id=1, source_target_pairs={{0,8},{4,12},{8,0},{12,4},{16,24},{20,28},{24,16},{28,20},{1,9},{5... | collective-permute-start | bytes 258056 | tf_op jit(solution)/shard_map/ppermute | solution.py:220
  10.7 2.6 %collective-permute-start.2 = (bf16[16,2688]{1,0:T(8,128)(2,1)S(1)}, bf16[16,2688]{1,0:T(8,128)(2,1)S(1)}, u32[]{:S(2)}, u32[]{:S(2)}) collective-permute-start(bf16[16,2688]{1,0:T(8,128)(2,1)S(1)} %get-tuple-element.36), channel_id=1, source_target_pairs={{0,16},{4,20},{8,24},{12,28},{16,0},{20,4},{24,8},{28,12},{1,17},{... | collective-permute-start | bytes 258056 | tf_op jit(solution)/shard_map/ppermute | solution.py:220
  13.3 1.7 %collective-permute-start.8 = (bf16[16,2688]{1,0:T(8,128)(2,1)S(1)}, bf16[16,2688]{1,0:T(8,128)(2,1)S(1)}, u32[]{:S(2)}, u32[]{:S(2)}) collective-permute-start(bf16[16,2688]{1,0:T(8,128)(2,1)S(1)} %get-tuple-element.34.refs_0_), channel_id=1, source_target_pairs={{0,2},{1,3},{2,0},{3,1},{4,6},{5,7},{6,4},{7,5},{8,10},{9,11},{10,... | collective-permute-start | bytes 258056 | tf_op jit(solution)/shard_map/ppermute | solution.py:220
  15.0 0.9 %collective-permute-start.9 = (bf16[16,2688]{1,0:T(8,128)(2,1)S(1)}, bf16[16,2688]{1,0:T(8,128)(2,1)S(1)}, u32[]{:S(2)}, u32[]{:S(2)}) collective-permute-start(bf16[16,2688]{1,0:T(8,128)(2,1)S(1)} %collective-permute-done.1.refs_1_), channel_id=1, source_target_pairs={{0,2},{1,3},{2,0},{3,1},{4,6},{5,7},{6,4},{7,5},{8,10},{9,11},{10,... | collective-permute-start | bytes 258056 | tf_op jit(solution)/shard_map/ppermute | solution.py:220
  16.0 2.4 %collective-permute-done.2.refs_2_ = bf16[16,2688]{1,0:T(8,128)(2,1)S(1)} collective-permute-done((bf16[16,2688]{1,0:T(8,128)(2,1)S(1)}, bf16[16,2688]{1,0:T(8,128)(2,1)S(1)}, u32[]{:S(2)}, u32[]{:S(2)}) %collective-permute-start.2) | collective-permute-done | bytes 86048 | tf_op jit(solution)/shard_map/ppermute | solution.py:220
  18.4 1.3 %collective-permute-done.3.refs_3_ = bf16[16,2688]{1,0:T(8,128)(2,1)S(1)} collective-permute-done((bf16[16,2688]{1,0:T(8,128)(2,1)S(1)}, bf16[16,2688]{1,0:T(8,128)(2,1)S(1)}, u32[]{:S(2)}, u32[]{:S(2)}) %collective-permute-start.3) | collective-permute-done | bytes 86048 | tf_op jit(solution)/shard_map/ppermute | solution.py:220
  19.7 1.5 %collective-permute-start.10 = (bf16[16,2688]{1,0:T(8,128)(2,1)S(1)}, bf16[16,2688]{1,0:T(8,128)(2,1)S(1)}, u32[]{:S(2)}, u32[]{:S(2)}) collective-permute-start(bf16[16,2688]{1,0:T(8,128)(2,1)S(1)} %collective-permute-done.2.refs_2_), channel_id=1, source_target_pairs={{0,2},{1,3},{2,0},{3,1},{4,6},{5,7},{6,4},{7,5},{8,10},{9,11},{10,... | collective-permute-start | bytes 258056 | tf_op jit(solution)/shard_map/ppermute | solution.py:220
  22.3 1.9 %collective-permute-done.10.refs_2_ = bf16[16,2688]{1,0:T(8,128)(2,1)S(1)} collective-permute-done((bf16[16,2688]{1,0:T(8,128)(2,1)S(1)}, bf16[16,2688]{1,0:T(8,128)(2,1)S(1)}, u32[]{:S(2)}, u32[]{:S(2)}) %collective-permute-start.10) | collective-permute-done | bytes 86048 | tf_op jit(solution)/shard_map/ppermute | solution.py:220
  24.7 1.4 %collective-permute-done.11.refs_3_ = bf16[16,2688]{1,0:T(8,128)(2,1)S(1)} collective-permute-done((bf16[16,2688]{1,0:T(8,128)(2,1)S(1)}, bf16[16,2688]{1,0:T(8,128)(2,1)S(1)}, u32[]{:S(2)}, u32[]{:S(2)}) %collective-permute-start.11) | collective-permute-done | bytes 86048 | tf_op jit(solution)/shard_map/ppermute | solution.py:220
  26.2 0.9 %shard_map.75 = (f32[192,256]{1,0:T(8,128)S(1)}, f32[192,256]{1,0:T(8,128)S(1)}) custom-call(s32[8,128]{1,0:T(8,128)S(1)} %get-tuple-element.31.info, bf16[2,3584,256]{2,1,0:T(8,128)(2,1)S(1)} %copy-done, bf16[2,3584,256]{2,1,0:T(8,128)(2,1)S(1)} %copy-done.1, bf16[16,2688]{1,0:T(8,128)(2,1)S(1)} %get-tuple-element.34.refs_0_, ...), custom_call_target="tpu_custom_call" | custom-call | flops 352321536 | bytes 8425472 | tf_op jit(solution)/shard_map/pallas_call | solution.py:207
  28.2 1.2 %shard_map.76 = (bf16[192,256]{1,0:T(8,128)(2,1)S(1)}, bf16[64,2688]{1,0:T(8,128)(2,1)S(1)}, bf16[64,2688]{1,0:T(8,128)(2,1)S(1)}) custom-call(s32[8,128]{1,0:T(8,128)S(1)} %get-tuple-element.31.info, bf16[2,3584,256]{2,1,0:T(8,128)(2,1)S(1)} %copy-done, bf16[2,3584,256]{2,1,0:T(8,128)(2,1)S(1)} %copy-done.1, bf16[2,256,3584]{2,1,0:T(8,128)(2,1)S(1)} %copy-done.2, ...), custom_call_target="tpu_custom_call" | custom-call | flops 528482304 | bytes 12881920 | tf_op jit(solution)/shard_map/pallas_call | solution.py:207
  31.4 1.5 %collective-permute-start.19 = (bf16[16,2688]{1,0:T(8,128)(2,1)S(1)}, bf16[16,2688]{1,0:T(8,128)(2,1)S(1)}, u32[]{:S(2)}, u32[]{:S(2)}) collective-permute-start(bf16[16,2688]{1,0:T(8,128)(2,1)S(1)} %get-tuple-element.48), channel_id=1, source_target_pairs={{0,2},{1,3},{2,0},{3,1},{4,6},{5,7},{6,4},{7,5},{8,10},{9,11},{10,... | collective-permute-start | bytes 258056 | tf_op jit(solution)/shard_map/ppermute | solution.py:220
  33.5 1.4 %collective-permute-start.23 = (bf16[16,2688]{1,0:T(8,128)(2,1)S(1)}, bf16[16,2688]{1,0:T(8,128)(2,1)S(1)}, u32[]{:S(2)}, u32[]{:S(2)}) collective-permute-start(bf16[16,2688]{1,0:T(8,128)(2,1)S(1)} %get-tuple-element.52), channel_id=1, source_target_pairs={{0,2},{1,3},{2,0},{3,1},{4,6},{5,7},{6,4},{7,5},{8,10},{9,11},{10,... | collective-permute-start | bytes 258056 | tf_op jit(solution)/shard_map/ppermute | solution.py:220
  35.6 1.2 %collective-permute-done.19.refs_1_ = bf16[16,2688]{1,0:T(8,128)(2,1)S(1)} collective-permute-done((bf16[16,2688]{1,0:T(8,128)(2,1)S(1)}, bf16[16,2688]{1,0:T(8,128)(2,1)S(1)}, u32[]{:S(2)}, u32[]{:S(2)}) %collective-permute-start.19) | collective-permute-done | bytes 86048 | tf_op jit(solution)/shard_map/ppermute | solution.py:220
  36.8 1.2 %collective-permute-start.20 = (bf16[16,2688]{1,0:T(8,128)(2,1)S(1)}, bf16[16,2688]{1,0:T(8,128)(2,1)S(1)}, u32[]{:S(2)}, u32[]{:S(2)}) collective-permute-start(bf16[16,2688]{1,0:T(8,128)(2,1)S(1)} %shard_map.81), channel_id=1, source_target_pairs={{0,8},{4,12},{8,0},{12,4},{16,24},{20,28},{24,16},{28,20},{1,9},{5... | collective-permute-start | bytes 258056 | tf_op jit(solution)/shard_map/ppermute | solution.py:220
  38.7 2.2 %collective-permute-start.22 = (bf16[16,2688]{1,0:T(8,128)(2,1)S(1)}, bf16[16,2688]{1,0:T(8,128)(2,1)S(1)}, u32[]{:S(2)}, u32[]{:S(2)}) collective-permute-start(bf16[16,2688]{1,0:T(8,128)(2,1)S(1)} %shard_map.82), channel_id=1, source_target_pairs={{0,16},{4,20},{8,24},{12,28},{16,0},{20,4},{24,8},{28,12},{1,17},{... | collective-permute-start | bytes 258056 | tf_op jit(solution)/shard_map/ppermute | solution.py:220
  40.9 2.1 %collective-permute-start.24 = (bf16[16,2688]{1,0:T(8,128)(2,1)S(1)}, bf16[16,2688]{1,0:T(8,128)(2,1)S(1)}, u32[]{:S(2)}, u32[]{:S(2)}) collective-permute-start(bf16[16,2688]{1,0:T(8,128)(2,1)S(1)} %shard_map.83), channel_id=1, source_target_pairs={{0,24},{4,28},{8,16},{12,20},{16,8},{20,12},{24,0},{28,4},{1,25},{... | collective-permute-start | bytes 258056 | tf_op jit(solution)/shard_map/ppermute | solution.py:220
  43.1 4.6 %collective-permute-done.22.refs_2_ = bf16[16,2688]{1,0:T(8,128)(2,1)S(1)} collective-permute-done((bf16[16,2688]{1,0:T(8,128)(2,1)S(1)}, bf16[16,2688]{1,0:T(8,128)(2,1)S(1)}, u32[]{:S(2)}, u32[]{:S(2)}) %collective-permute-start.22) | collective-permute-done | bytes 86048 | tf_op jit(solution)/shard_map/ppermute | solution.py:220
  47.7 1.6 %collective-permute-start.25 = (bf16[32,2688]{1,0:T(8,128)(2,1)S(1)}, bf16[32,2688]{1,0:T(8,128)(2,1)S(1)}, u32[]{:S(2)}, u32[]{:S(2)}) collective-permute-start(bf16[32,2688]{1,0:T(8,128)(2,1)S(1)} %shard_map.84), channel_id=1, source_target_pairs={{0,4},{4,0},{8,12},{12,8},{16,20},{20,16},{24,28},{28,24},{1,5},{5... | collective-permute-start | bytes 516104 | tf_op jit(solution)/shard_map/ppermute | solution.py:220
  49.3 3.9 %collective-permute-done.25.refs_4_ = bf16[32,2688]{1,0:T(8,128)(2,1)S(1)} collective-permute-done((bf16[32,2688]{1,0:T(8,128)(2,1)S(1)}, bf16[32,2688]{1,0:T(8,128)(2,1)S(1)}, u32[]{:S(2)}, u32[]{:S(2)}) %collective-permute-start.25) | collective-permute-done | bytes 172064 | tf_op jit(solution)/shard_map/ppermute | solution.py:220
  53.2 1.2 %shard_map.85 = bf16[128,896]{1,0:T(8,128)(2,1)} custom-call(bf16[3,96,128]{2,1,0:T(8,128)(2,1)S(1)} %get-tuple-element.29.mix_high, bf16[3,96,128]{2,1,0:T(8,128)(2,1)S(1)} %get-tuple-element.30.mix_low, bf16[16,2688]{1,0:T(8,128)(2,1)S(1)} %shard_map.80.refs_0_, bf16[16,2688]{1,0:T(8,128)(2,1)S(1)} %collective-permute-done.20.refs_1_, ...), custom_call_target="tpu_custom_call" | custom-call | bytes 892928 | tf_op jit(solution)/shard_map/pallas_call | solution.py:207
  (47 shorter events, 6.9 us)
Async XLA Ops:
  1.4 7.4 %collective-permute-start = (bf16[32,2688]{1,0:T(8,128)(2,1)S(1)}, bf16[32,2688]{1,0:T(8,128)(2,1)S(1)}, u32[]{:S(2)}, u32[]{:S(2)}) collective-permute-start(bf16[32,2688]{1,0:T(8,128)(2,1)S(1)} %get-tuple-element.33), channel_id=1, source_target_pairs={{0,4},{4,0},{8,12},{12,8},{16,20},{20,16},{24,28},{28,24},{1,5},{5... | collective-permute-start | bytes 516104 | tf_op jit(solution)/shard_map/ppermute | solution.py:220
  8.9 6.2 %collective-permute-start.1 = (bf16[16,2688]{1,0:T(8,128)(2,1)S(1)}, bf16[16,2688]{1,0:T(8,128)(2,1)S(1)}, u32[]{:S(2)}, u32[]{:S(2)}) collective-permute-start(bf16[16,2688]{1,0:T(8,128)(2,1)S(1)} %get-tuple-element.35), channel_id=1, source_target_pairs={{0,8},{4,12},{8,0},{12,4},{16,24},{20,28},{24,16},{28,20},{1,9},{5... | collective-permute-start | bytes 258056 | tf_op jit(solution)/shard_map/ppermute | solution.py:220
  10.7 7.7 %collective-permute-start.2 = (bf16[16,2688]{1,0:T(8,128)(2,1)S(1)}, bf16[16,2688]{1,0:T(8,128)(2,1)S(1)}, u32[]{:S(2)}, u32[]{:S(2)}) collective-permute-start(bf16[16,2688]{1,0:T(8,128)(2,1)S(1)} %get-tuple-element.36), channel_id=1, source_target_pairs={{0,16},{4,20},{8,24},{12,28},{16,0},{20,4},{24,8},{28,12},{1,17},{... | collective-permute-start | bytes 258056 | tf_op jit(solution)/shard_map/ppermute | solution.py:220
  13.3 6.4 %collective-permute-start.3 = (bf16[16,2688]{1,0:T(8,128)(2,1)S(1)}, bf16[16,2688]{1,0:T(8,128)(2,1)S(1)}, u32[]{:S(2)}, u32[]{:S(2)}) collective-permute-start(bf16[16,2688]{1,0:T(8,128)(2,1)S(1)} %get-tuple-element.37), channel_id=1, source_target_pairs={{0,24},{4,28},{8,16},{12,20},{16,8},{20,12},{24,0},{28,4},{1,25},{... | collective-permute-start | bytes 258056 | tf_op jit(solution)/shard_map/ppermute | solution.py:220
  13.3 7.9 %collective-permute-start.8 = (bf16[16,2688]{1,0:T(8,128)(2,1)S(1)}, bf16[16,2688]{1,0:T(8,128)(2,1)S(1)}, u32[]{:S(2)}, u32[]{:S(2)}) collective-permute-start(bf16[16,2688]{1,0:T(8,128)(2,1)S(1)} %get-tuple-element.34.refs_0_), channel_id=1, source_target_pairs={{0,2},{1,3},{2,0},{3,1},{4,6},{5,7},{6,4},{7,5},{8,10},{9,11},{10,... | collective-permute-start | bytes 258056 | tf_op jit(solution)/shard_map/ppermute | solution.py:220
  15.0 6.2 %collective-permute-start.4 = (bf16[16,2688]{1,0:T(8,128)(2,1)S(1)}, bf16[16,2688]{1,0:T(8,128)(2,1)S(1)}, u32[]{:S(2)}, u32[]{:S(2)}) collective-permute-start(bf16[16,2688]{1,0:T(8,128)(2,1)S(1)} %get-tuple-element.34.refs_0_), channel_id=1, source_target_pairs={{0,1},{1,0},{2,3},{3,2},{4,5},{5,4},{6,7},{7,6},{8,9},{9,8},{10,11... | collective-permute-start | bytes 258056 | tf_op jit(solution)/shard_map/ppermute | solution.py:220
  15.0 6.8 %collective-permute-start.9 = (bf16[16,2688]{1,0:T(8,128)(2,1)S(1)}, bf16[16,2688]{1,0:T(8,128)(2,1)S(1)}, u32[]{:S(2)}, u32[]{:S(2)}) collective-permute-start(bf16[16,2688]{1,0:T(8,128)(2,1)S(1)} %collective-permute-done.1.refs_1_), channel_id=1, source_target_pairs={{0,2},{1,3},{2,0},{3,1},{4,6},{5,7},{6,4},{7,5},{8,10},{9,11},{10,... | collective-permute-start | bytes 258056 | tf_op jit(solution)/shard_map/ppermute | solution.py:220
  18.4 3.6 %collective-permute-start.5 = (bf16[16,2688]{1,0:T(8,128)(2,1)S(1)}, bf16[16,2688]{1,0:T(8,128)(2,1)S(1)}, u32[]{:S(2)}, u32[]{:S(2)}) collective-permute-start(bf16[16,2688]{1,0:T(8,128)(2,1)S(1)} %collective-permute-done.1.refs_1_), channel_id=1, source_target_pairs={{0,1},{1,0},{2,3},{3,2},{4,5},{5,4},{6,7},{7,6},{8,9},{9,8},{10,11... | collective-permute-start | bytes 258056 | tf_op jit(solution)/shard_map/ppermute | solution.py:220
  19.7 4.5 %collective-permute-start.10 = (bf16[16,2688]{1,0:T(8,128)(2,1)S(1)}, bf16[16,2688]{1,0:T(8,128)(2,1)S(1)}, u32[]{:S(2)}, u32[]{:S(2)}) collective-permute-start(bf16[16,2688]{1,0:T(8,128)(2,1)S(1)} %collective-permute-done.2.refs_2_), channel_id=1, source_target_pairs={{0,2},{1,3},{2,0},{3,1},{4,6},{5,7},{6,4},{7,5},{8,10},{9,11},{10,... | collective-permute-start | bytes 258056 | tf_op jit(solution)/shard_map/ppermute | solution.py:220
  21.2 3.0 %collective-permute-start.6 = (bf16[16,2688]{1,0:T(8,128)(2,1)S(1)}, bf16[16,2688]{1,0:T(8,128)(2,1)S(1)}, u32[]{:S(2)}, u32[]{:S(2)}) collective-permute-start(bf16[16,2688]{1,0:T(8,128)(2,1)S(1)} %collective-permute-done.2.refs_2_), channel_id=1, source_target_pairs={{0,1},{1,0},{2,3},{3,2},{4,5},{5,4},{6,7},{7,6},{8,9},{9,8},{10,11... | collective-permute-start | bytes 258056 | tf_op jit(solution)/shard_map/ppermute | solution.py:220
  21.2 4.9 %collective-permute-start.11 = (bf16[16,2688]{1,0:T(8,128)(2,1)S(1)}, bf16[16,2688]{1,0:T(8,128)(2,1)S(1)}, u32[]{:S(2)}, u32[]{:S(2)}) collective-permute-start(bf16[16,2688]{1,0:T(8,128)(2,1)S(1)} %collective-permute-done.3.refs_3_), channel_id=1, source_target_pairs={{0,2},{1,3},{2,0},{3,1},{4,6},{5,7},{6,4},{7,5},{8,10},{9,11},{10,... | collective-permute-start | bytes 258056 | tf_op jit(solution)/shard_map/ppermute | solution.py:220
  21.8 4.3 %collective-permute-start.7 = (bf16[16,2688]{1,0:T(8,128)(2,1)S(1)}, bf16[16,2688]{1,0:T(8,128)(2,1)S(1)}, u32[]{:S(2)}, u32[]{:S(2)}) collective-permute-start(bf16[16,2688]{1,0:T(8,128)(2,1)S(1)} %collective-permute-done.3.refs_3_), channel_id=1, source_target_pairs={{0,1},{1,0},{2,3},{3,2},{4,5},{5,4},{6,7},{7,6},{8,9},{9,8},{10,11... | collective-permute-start | bytes 258056 | tf_op jit(solution)/shard_map/ppermute | solution.py:220
  22.0 5.1 %collective-permute-start.12 = (bf16[16,2688]{1,0:T(8,128)(2,1)S(1)}, bf16[16,2688]{1,0:T(8,128)(2,1)S(1)}, u32[]{:S(2)}, u32[]{:S(2)}) collective-permute-start(bf16[16,2688]{1,0:T(8,128)(2,1)S(1)} %collective-permute-done.8.refs_0_), channel_id=1, source_target_pairs={{0,1},{1,0},{2,3},{3,2},{4,5},{5,4},{6,7},{7,6},{8,9},{9,8},{10,11... | collective-permute-start | bytes 258056 | tf_op jit(solution)/shard_map/ppermute | solution.py:220
  24.2 2.9 %collective-permute-start.13 = (bf16[16,2688]{1,0:T(8,128)(2,1)S(1)}, bf16[16,2688]{1,0:T(8,128)(2,1)S(1)}, u32[]{:S(2)}, u32[]{:S(2)}) collective-permute-start(bf16[16,2688]{1,0:T(8,128)(2,1)S(1)} %collective-permute-done.9.refs_1_), channel_id=1, source_target_pairs={{0,1},{1,0},{2,3},{3,2},{4,5},{5,4},{6,7},{7,6},{8,9},{9,8},{10,11... | collective-permute-start | bytes 258056 | tf_op jit(solution)/shard_map/ppermute | solution.py:220
  24.2 2.9 %collective-permute-start.14 = (bf16[16,2688]{1,0:T(8,128)(2,1)S(1)}, bf16[16,2688]{1,0:T(8,128)(2,1)S(1)}, u32[]{:S(2)}, u32[]{:S(2)}) collective-permute-start(bf16[16,2688]{1,0:T(8,128)(2,1)S(1)} %collective-permute-done.10.refs_2_), channel_id=1, source_target_pairs={{0,1},{1,0},{2,3},{3,2},{4,5},{5,4},{6,7},{7,6},{8,9},{9,8},{10,11... | collective-permute-start | bytes 258056 | tf_op jit(solution)/shard_map/ppermute | solution.py:220
  30.5 4.9 %collective-permute-start.16 = (bf16[64,2688]{1,0:T(8,128)(2,1)S(1)}, bf16[64,2688]{1,0:T(8,128)(2,1)S(1)}, u32[]{:S(2)}, u32[]{:S(2)}) collective-permute-start(bf16[64,2688]{1,0:T(8,128)(2,1)S(1)} %get-tuple-element.42), channel_id=1, source_target_pairs={{0,1},{1,0},{2,3},{3,2},{4,5},{5,4},{6,7},{7,6},{8,9},{9,8},{10,11... | collective-permute-start | bytes 1032200 | tf_op jit(solution)/shard_map/ppermute | solution.py:220
  31.4 5.4 %collective-permute-start.19 = (bf16[16,2688]{1,0:T(8,128)(2,1)S(1)}, bf16[16,2688]{1,0:T(8,128)(2,1)S(1)}, u32[]{:S(2)}, u32[]{:S(2)}) collective-permute-start(bf16[16,2688]{1,0:T(8,128)(2,1)S(1)} %get-tuple-element.48), channel_id=1, source_target_pairs={{0,2},{1,3},{2,0},{3,1},{4,6},{5,7},{6,4},{7,5},{8,10},{9,11},{10,... | collective-permute-start | bytes 258056 | tf_op jit(solution)/shard_map/ppermute | solution.py:220
  32.8 5.8 %collective-permute-start.21 = (bf16[16,2688]{1,0:T(8,128)(2,1)S(1)}, bf16[16,2688]{1,0:T(8,128)(2,1)S(1)}, u32[]{:S(2)}, u32[]{:S(2)}) collective-permute-start(bf16[16,2688]{1,0:T(8,128)(2,1)S(1)} %get-tuple-element.50), channel_id=1, source_target_pairs={{0,2},{1,3},{2,0},{3,1},{4,6},{5,7},{6,4},{7,5},{8,10},{9,11},{10,... | collective-permute-start | bytes 258056 | tf_op jit(solution)/shard_map/ppermute | solution.py:220
  33.5 7.4 %collective-permute-start.23 = (bf16[16,2688]{1,0:T(8,128)(2,1)S(1)}, bf16[16,2688]{1,0:T(8,128)(2,1)S(1)}, u32[]{:S(2)}, u32[]{:S(2)}) collective-permute-start(bf16[16,2688]{1,0:T(8,128)(2,1)S(1)} %get-tuple-element.52), channel_id=1, source_target_pairs={{0,2},{1,3},{2,0},{3,1},{4,6},{5,7},{6,4},{7,5},{8,10},{9,11},{10,... | collective-permute-start | bytes 258056 | tf_op jit(solution)/shard_map/ppermute | solution.py:220
  34.8 8.2 %collective-permute-start.18 = (bf16[16,2688]{1,0:T(8,128)(2,1)S(1)}, bf16[16,2688]{1,0:T(8,128)(2,1)S(1)}, u32[]{:S(2)}, u32[]{:S(2)}) collective-permute-start(bf16[16,2688]{1,0:T(8,128)(2,1)S(1)} %get-tuple-element.46), channel_id=1, source_target_pairs={{0,2},{1,3},{2,0},{3,1},{4,6},{5,7},{6,4},{7,5},{8,10},{9,11},{10,... | collective-permute-start | bytes 258056 | tf_op jit(solution)/shard_map/ppermute | solution.py:220
  36.8 6.3 %collective-permute-start.20 = (bf16[16,2688]{1,0:T(8,128)(2,1)S(1)}, bf16[16,2688]{1,0:T(8,128)(2,1)S(1)}, u32[]{:S(2)}, u32[]{:S(2)}) collective-permute-start(bf16[16,2688]{1,0:T(8,128)(2,1)S(1)} %shard_map.81), channel_id=1, source_target_pairs={{0,8},{4,12},{8,0},{12,4},{16,24},{20,28},{24,16},{28,20},{1,9},{5... | collective-permute-start | bytes 258056 | tf_op jit(solution)/shard_map/ppermute | solution.py:220
  38.7 9.0 %collective-permute-start.22 = (bf16[16,2688]{1,0:T(8,128)(2,1)S(1)}, bf16[16,2688]{1,0:T(8,128)(2,1)S(1)}, u32[]{:S(2)}, u32[]{:S(2)}) collective-permute-start(bf16[16,2688]{1,0:T(8,128)(2,1)S(1)} %shard_map.82), channel_id=1, source_target_pairs={{0,16},{4,20},{8,24},{12,28},{16,0},{20,4},{24,8},{28,12},{1,17},{... | collective-permute-start | bytes 258056 | tf_op jit(solution)/shard_map/ppermute | solution.py:220
  40.9 6.8 %collective-permute-start.24 = (bf16[16,2688]{1,0:T(8,128)(2,1)S(1)}, bf16[16,2688]{1,0:T(8,128)(2,1)S(1)}, u32[]{:S(2)}, u32[]{:S(2)}) collective-permute-start(bf16[16,2688]{1,0:T(8,128)(2,1)S(1)} %shard_map.83), channel_id=1, source_target_pairs={{0,24},{4,28},{8,16},{12,20},{16,8},{20,12},{24,0},{28,4},{1,25},{... | collective-permute-start | bytes 258056 | tf_op jit(solution)/shard_map/ppermute | solution.py:220
  47.7 5.5 %collective-permute-start.25 = (bf16[32,2688]{1,0:T(8,128)(2,1)S(1)}, bf16[32,2688]{1,0:T(8,128)(2,1)S(1)}, u32[]{:S(2)}, u32[]{:S(2)}) collective-permute-start(bf16[32,2688]{1,0:T(8,128)(2,1)S(1)} %shard_map.84), channel_id=1, source_target_pairs={{0,4},{4,0},{8,12},{12,8},{16,20},{20,16},{24,28},{28,24},{1,5},{5... | collective-permute-start | bytes 516104 | tf_op jit(solution)/shard_map/ppermute | solution.py:220
  (5 other events, 57.5 us)

commit v5 on v4

v5 whole, which is shorter than its diff:
```python
import functools

import jax
import jax.numpy as jnp
from jax import lax
from jax.experimental import pallas as pl
from jax.experimental.pallas import tpu as pltpu
from jax.sharding import PartitionSpec as P

CAP = 8
F32 = jnp.float32
BF16 = jnp.bfloat16
HBM = pl.BlockSpec(memory_space=pltpu.HBM)
VMEM = pl.BlockSpec(memory_space=pltpu.VMEM)
LIMIT = 20 * 2**20


def dot(left, right):
    return jnp.dot(left, right, preferred_element_type=F32)


def dot_rows(left, right):
    return lax.dot_general(left, right, (((0,), (0,)), ((), ())), preferred_element_type=F32)


def route_kernel(owned, low, high_steps, plan_hbm, ids_hbm, gates_hbm, tokens_hbm, *refs):
    high = len(high_steps)
    pieces, (info, mixtures, plan, ids, gates, tokens, place, weight, sems) = refs[:high], refs[high:]
    sources = (plan_hbm, ids_hbm, gates_hbm, tokens_hbm)
    copies = [
        pltpu.make_async_copy(source, target, sems.at[n])
        for n, (source, target) in enumerate(zip(sources, (plan, ids, gates, tokens)))
    ]
    for copy in copies:
        copy.start()
    choices, tok_rows = ids.shape
    share = tokens.shape[1]
    owners = plan.shape[0]
    experts = owners * owned
    steps = [(k, m) for k in high_steps for m in range(low)]
    own_index = lax.axis_index("expert")
    row = lax.broadcasted_iota(jnp.int32, (tok_rows, tok_rows), 0)
    col = lax.broadcasted_iota(jnp.int32, (tok_rows, tok_rows), 1)
    earlier = (row < col).astype(F32).astype(BF16)
    expert = lax.broadcasted_iota(jnp.int32, (experts, tok_rows), 0)
    owner = expert // owned
    within = expert - owner * owned
    named = jnp.zeros((experts, tok_rows), F32)
    weights = jnp.zeros((experts, tok_rows), F32)
    hot = jnp.zeros((experts, tok_rows), jnp.int32)
    copies[0].wait()
    for host in range(owners):
        source = (host + owners // 2) % owners
        hot = jnp.where(owner == source, plan[host] - source * owned, hot)
    own_hot = plan[lax.rem(own_index + owners // 2, owners)] - own_index * owned
    info[...] = jnp.full(info.shape, own_hot, jnp.int32)
    copies[1].wait()
    copies[2].wait()
    for choice in range(choices):
        hit = expert == ids[choice : choice + 1, :]
        named = named + hit.astype(F32)
        weights = weights + jnp.where(hit, gates[choice : choice + 1, :], 0.0)
    weight[...] = weights
    rank = dot(named.astype(BF16), earlier).astype(jnp.int32)
    limit = jnp.where(within == hot, 2 * CAP, CAP)
    start = jnp.where(within == hot, 0, CAP * (1 + within + (within < hot).astype(jnp.int32)))
    place[...] = jnp.where((named > 0.0) & (rank < limit), start + rank, -1)
    slot = lax.broadcasted_iota(jnp.int32, (CAP, tok_rows), 0)
    zero = jnp.zeros((CAP, tok_rows), F32)
    copies[3].wait()
    for chunk in range(owned + 1):
        picks, mixes = [], []
        for k, m in steps:
            index = own_index ^ (k * low + m)
            pick, mix = zero, zero
            for number in range(owned):
                line = pl.ds(index * owned + number, 1)
                match = place[line, :] == slot + chunk * CAP
                pick = pick + match.astype(F32)
                mix = mix + jnp.where(match, weight[line, :], 0.0)
            picks.append(pick)
            mixes.append(mix)
        pick = jnp.concatenate(picks, axis=0).astype(BF16)
        values = dot(pick, tokens[...]).astype(BF16)
        size = low * CAP
        for n, piece in enumerate(pieces):
            piece[:, chunk * share : (chunk + 1) * share] = values[n * size : (n + 1) * size]
        mix = jnp.concatenate(mixes, axis=0)
        rounded = mix.astype(BF16)
        mixtures[chunk, 0] = rounded
        mixtures[chunk, 1] = (mix - rounded.astype(F32)).astype(BF16)


def blocks_of(value):
    return [value[begin : begin + CAP] for begin in range(0, value.shape[0], CAP)]


def regroup_kernel(count, moves, *refs):
    values = [blocks_of(ref[...].astype(F32)) for ref in refs[:count]]
    for out, blocks in zip(refs[count:], moves):
        out[...] = jnp.concatenate([values[n][b] for n, b in blocks], axis=0).astype(out.dtype)


def sum_kernel(count, moves, *refs):
    values = [blocks_of(ref[...].astype(F32)) for ref in refs[:count]]
    for out, blocks in zip(refs[count:], moves):
        rows = [sum(values[n][b] for n, b in terms) for terms in blocks]
        out[...] = jnp.concatenate(rows, axis=0).astype(out.dtype)


def groups_of(owned):
    return [(0, 1)] + [(number + 1,) for number in range(1, owned)]


def order_of(info, owned):
    hot = jnp.max(info[...].astype(F32)).astype(jnp.int32)
    return [hot] + [n + (n >= hot).astype(jnp.int32) for n in range(owned - 1)]


def features_of(m, share):
    return pl.ds(pl.multiple_of((lax.axis_index("dp") ^ m) * share, share), share)


def projections(order, numbers, blocks, gate, up):
    owned = gate.shape[0]
    share = blocks[0].shape[1] // (owned + 1)
    for group, chunks in enumerate(groups_of(owned)):
        gate_value = up_value = None
        for m, block in zip(numbers, blocks):
            rows = jnp.concatenate([block[:, c * share : (c + 1) * share] for c in chunks], axis=0)
            gate_part = dot(rows, gate[order[group], features_of(m, share), :])
            up_part = dot(rows, up[order[group], features_of(m, share), :])
            gate_value = gate_part if gate_value is None else gate_value + gate_part
            up_value = up_part if up_value is None else up_value + up_part
        lines = block.shape[0]
        yield slice(chunks[0] * lines, (chunks[-1] + 1) * lines), gate_value, up_value


def first_kernel(numbers, info, gate, up, down, *refs):
    *blocks, gate_out, up_out = refs
    order = order_of(info, gate.shape[0])
    for place, gate_value, up_value in projections(order, numbers, blocks, gate, up):
        gate_out[place, :] = gate_value
        up_out[place, :] = up_value


def down_parts(order, numbers, hidden, down, outs):
    owned = down.shape[0]
    lines, wide = outs[0].shape
    share = wide // (owned + 1)
    for m, out in zip(numbers, outs):
        for group, chunks in enumerate(groups_of(owned)):
            rows = hidden[chunks[0] * lines : (chunks[-1] + 1) * lines, :]
            value = dot(rows, down[order[group], :, features_of(m, share)]).astype(out.dtype)
            for spot, chunk in enumerate(chunks):
                out[:, chunk * share : (chunk + 1) * share] = value[spot * lines : (spot + 1) * lines]


def second_kernel(numbers, out_number, info, gate, up, down, gate_in, up_in, *refs):
    *blocks, hidden, out = refs
    order = order_of(info, gate.shape[0])
    for place, gate_value, up_value in projections(order, numbers, blocks, gate, up):
        gate_value = gate_value + gate_in[place, :]
        up_value = up_value + up_in[place, :]
        hidden[place, :] = (jax.nn.silu(gate_value) * up_value).astype(BF16)
    down_parts(order, [out_number], hidden, down, [out])


def down_kernel(numbers, info, down, hidden, *outs):
    down_parts(order_of(info, down.shape[0]), numbers, hidden, down, outs)


def mix_kernel(mixtures, *refs):
    *pieces, out = refs
    share = out.shape[1]
    total = jnp.zeros(out.shape, F32)
    for chunk in range(mixtures.shape[0]):
        rows = jnp.concatenate([p[:, chunk * share : (chunk + 1) * share] for p in pieces], axis=0)
        total = total + dot_rows(mixtures[chunk, 0], rows) + dot_rows(mixtures[chunk, 1], rows)
    out[...] = total.astype(out.dtype)


def call(kernel, outs, *args, specs=None, scratch=(), flops=0):
    if specs:
        args = [
            pltpu.with_memory_space_constraint(a, s.memory_space) for a, s in zip(args, specs)
        ]
    return pl.pallas_call(
        kernel,
        out_shape=outs,
        in_specs=specs or [VMEM] * len(args),
        out_specs=[VMEM] * len(outs),
        scratch_shapes=list(scratch),
        compiler_params=pltpu.CompilerParams(vmem_limit_bytes=LIMIT),
        cost_estimate=pl.CostEstimate(flops=flops + 1000, bytes_accessed=1000, transcendentals=0),
    )(*args)


def swapped(value, axis, mask):
    count = lax.axis_size(axis)
    return lax.ppermute(value, axis, [(source, source ^ mask) for source in range(count)])


def turned(value, low_step, across):
    parts = lax.axis_size("dp")
    if not across:
        return swapped(value, "expert", low_step)
    return swapped(value, ("expert", "dp"), low_step * parts + across)


def per_device(tokens, expert_ids, gate_weights, replica_plan, w_gate, w_up, w_down):
    owners = lax.axis_size("expert")
    parts = lax.axis_size("dp")
    owned, model_width, hidden_share = w_gate.shape
    tok_rows, share = tokens.shape
    choices = expert_ids.shape[1]
    chunks = owned + 1
    lines = owners * CAP
    wide = chunks * share
    low = 1 << ((owners.bit_length() - 1) // 2)
    high = owners // low
    high_steps = list(range(high - 1, -1, -1))
    ways_in = [high_steps]
    ways_out = [high_steps[: high // 2], high_steps[high // 2 :]]
    shape = jax.ShapeDtypeStruct
    piece = shape((low * CAP, wide), BF16)
    whole = shape((lines, wide), BF16)

    def lot(group):
        return shape((len(group) * CAP, wide), BF16)

    *pieces, info, mixtures = call(
        functools.partial(route_kernel, owned, low, high_steps),
        [piece] * high
        + [shape((8, 128), jnp.int32), shape((chunks, 2, lines, tok_rows), BF16)],
        replica_plan, expert_ids.T, gate_weights.T, tokens,
        specs=[HBM] * 4,
        scratch=[
            pltpu.SMEM((owners,), jnp.int32),
            pltpu.VMEM((choices, tok_rows), jnp.int32),
            pltpu.VMEM((choices, tok_rows), F32),
            pltpu.VMEM((tok_rows, share), BF16),
            pltpu.VMEM((owners * owned, tok_rows), jnp.int32),
            pltpu.VMEM((owners * owned, tok_rows), F32),
            pltpu.SemaphoreType.DMA((4,)),
        ],
        flops=16 * 10**10,
    )
    arrived = {k: swapped(p, "expert", k * low) if k else p for k, p in zip(high_steps, pieces)}

    top = parts // 2
    rows, here, there = [], [], []
    for group in ways_in:
        lots = call(
            functools.partial(regroup_kernel, len(group), [
                [(n, m) for n in range(len(group))] for m in range(low)
            ]),
            [lot(group)] * low,
            *[arrived[k] for k in group],
        )
        there += [turned(value, m, top) for m, value in enumerate(lots)]
        here += [turned(value, m, 0) if m else value for m, value in enumerate(lots)]
        rows += [(k, m) for m in range(low) for k in group]
    moves = [(n, b) for n, value in enumerate(here) for b in range(value.shape[0] // CAP)]
    moves = [moves, [(n + len(here), b) for n, b in moves]]
    here, there = call(
        functools.partial(regroup_kernel, 2 * len(here), moves), [whole] * 2, *here, *there
    )
    blocks = {0: here, top: there}
    mask = top // 2
    while mask:
        for n in list(blocks):
            blocks[n ^ mask] = swapped(blocks[n], "dp", mask)
        mask //= 2
    first = [0, top]
    second = [n for n in range(parts) if n not in first]
    sums = [shape((chunks * lines, hidden_share), F32)] * 2
    gate_sum, up_sum = call(
        functools.partial(first_kernel, first),
        sums,
        info, w_gate, w_up, w_down, *[blocks[n] for n in first],
    )
    outs = {}
    hidden, outs[parts - 1] = call(
        functools.partial(second_kernel, second, parts - 1),
        [shape((chunks * lines, hidden_share), BF16), whole],
        info, w_gate, w_up, w_down, gate_sum, up_sum, *[blocks[n] for n in second],
    )
    far, near = list(range(top, parts - 1)), list(range(top))
    for numbers in (far, near):
        found = call(
            functools.partial(down_kernel, numbers), [whole] * len(numbers), info, w_down, hidden
        )
        outs |= dict(zip(numbers, found))

    def reduced(begin):
        found = {n: outs[n] for n in range(begin, begin + top)}
        mask = 1
        while 2 * mask < top:
            for n in [n for n in found if n & mask]:
                value = swapped(found.pop(n), "dp", mask)
                (found[n ^ mask],) = call(
                    functools.partial(sum_kernel, 2, [
                        [[(0, b), (1, b)] for b in range(len(rows))]
                    ]),
                    [whole], found[n ^ mask], value,
                )
            mask *= 2
        terms = [swapped(value, "dp", mask) if n & mask else value for n, value in found.items()]
        moves = [
            [[(t, rows.index((k, m))) for t in range(len(terms))] for k in group]
            for group in ways_out for m in range(low)
        ]
        sums = call(
            functools.partial(sum_kernel, len(terms), moves),
            [lot(group) for group in ways_out for m in range(low)],
            *terms,
        )
        return [sums[n : n + low] for n in range(0, len(sums), low)]

    back = {}
    for group, far_lots, near_lots in zip(ways_out, reduced(top), reduced(0)):
        terms = []
        for m in range(low):
            terms.append(turned(far_lots[m], m, top))
            terms.append(turned(near_lots[m], m, 0) if m else near_lots[m])
        moves = [[[(2 * m, n), (2 * m + 1, n)] for m in range(low)] for n in range(len(group))]
        totals = call(
            functools.partial(sum_kernel, 2 * low, moves), [piece] * len(group), *terms
        )
        for k, value in zip(group, totals):
            back[k] = swapped(value, "expert", k * low) if k else value
    (mixed_out,) = call(
        mix_kernel,
        [shape((tok_rows, share), BF16)],
        mixtures, *[back[k] for k in high_steps],
    )
    return mixed_out


def solution(mesh):
    in_specs = (
        P("expert", "dp"),
        P("expert", None),
        P("expert", None),
        P(),
        P("expert", None, "dp"),
        P("expert", None, "dp"),
        P("expert", "dp", None),
    )
    out_specs = P("expert", "dp")
    return jax.shard_map(
        per_device, mesh=mesh, in_specs=in_specs, out_specs=out_specs, check_vma=False
    )
```

time: 54.5 us -> 50.3 us (0.923)
  starting transfers between devices: 25.1 us -> 22.1 us
  local copies, waits for them, and re-layouts: 0.79 us -> 0.01 us
  waiting for transfers between devices: 22.8 us -> 22.1 us
    ppermute x26 -> x19, starting transfers between devices: 25.1 us -> 22.1 us  [swapped(): lax.ppermute(value, axis, [(source, source ^ mask) for source in range(co...]
    unnamed x6, local copies, waits for them, and re-layouts: 0.79 us -> 0.01 us
    ppermute x26 -> x19, waiting for transfers between devices: 22.8 us -> 22.1 us  [swapped(): lax.ppermute(value, axis, [(source, source ^ mask) for source in range(co...]
    pallas_call x13 -> x12, Pallas kernels: 5.57 us -> 5.81 us  [call(): pl.pallas_call(kernel, out_shape=outs, in_specs=specs or [VMEM] * len(arg...]
  transfers between devices with their start and end apart: 26 -> 19, of which waited for: 11 -> 12; matrix products, arithmetic and copies ran while one was open for 0% -> 0% of each run, Pallas kernels for 3% -> 4%
where the time goes in v5:
time: 50.3 us; the launch traced here: 50.2 us
  starting transfers between devices  22.1 us (44%)
  waiting for transfers between devices  22.1 us (44%)
  Pallas kernels  5.81 us (12%)
    ppermute x19, waiting for transfers between devices, swapped(): lax.ppermute(value, axis, [(source, source ^ mask) for source in range(co...  22.1 us
    ppermute x19, starting transfers between devices, swapped(): lax.ppermute(value, axis, [(source, source ^ mask) for source in range(co...  22.1 us
    pallas_call x12, Pallas kernels, call(): pl.pallas_call(kernel, out_shape=outs, in_specs=specs or [VMEM] * len(arg...  5.81 us
  transfers between devices with their start and end apart: 19, of which 12 were waited for; matrix products, arithmetic and copies ran while one was open for 0% of the time, Pallas kernels for 4%

profile of v5, /device:TPU:0, one launch (start us, length us, event | category | flops | bytes accessed | tf_op | source)
XLA Modules:
  0.0 50.2 jit_solution(12181300507737978974)
XLA Ops:
  0.0 1.4 %shard_map.73 = (bf16[16,2688]{1,0:T(8,128)(2,1)S(1)}, bf16[16,2688]{1,0:T(8,128)(2,1)S(1)}, bf16[16,2688]{1,0:T(8,128)(2,1)S(1)}, bf16[16,2688]{1,0:T(8,128)(2,...) custom-call(s32[8]{0:T(128)} %plan_hbm.1, s32[8,128]{1,0:T(8,128)} %bitcast.2, f32[8,128]{1,0:T(8,128)} %bitcast.3, ...), custom_call_target="tpu_custom_call" | custom-call | flops 160000000000 | bytes 1000 | tf_op jit(solution)/shard_map/pallas_call | solution.py:188
  1.4 5.1 %collective-permute-start = (bf16[16,2688]{1,0:T(8,128)(2,1)S(1)}, bf16[16,2688]{1,0:T(8,128)(2,1)S(1)}, u32[]{:S(2)}, u32[]{:S(2)}) collective-permute-start(bf16[16,2688]{1,0:T(8,128)(2,1)S(1)} %get-tuple-element.35), channel_id=1, source_target_pairs={{0,24},{4,28},{8,16},{12,20},{16,8},{20,12},{24,0},{28,4},{1,25},{... | collective-permute-start | bytes 258056 | tf_op jit(solution)/shard_map/ppermute | solution.py:201
  6.5 0.6 %collective-permute-start.2 = (bf16[16,2688]{1,0:T(8,128)(2,1)S(1)}, bf16[16,2688]{1,0:T(8,128)(2,1)S(1)}, u32[]{:S(2)}, u32[]{:S(2)}) collective-permute-start(bf16[16,2688]{1,0:T(8,128)(2,1)S(1)} %get-tuple-element.37), channel_id=1, source_target_pairs={{0,8},{4,12},{8,0},{12,4},{16,24},{20,28},{24,16},{28,20},{1,9},{5... | collective-permute-start | bytes 258056 | tf_op jit(solution)/shard_map/ppermute | solution.py:201
  7.2 2.6 %collective-permute-done.refs_0_ = bf16[16,2688]{1,0:T(8,128)(2,1)S(1)} collective-permute-done((bf16[16,2688]{1,0:T(8,128)(2,1)S(1)}, bf16[16,2688]{1,0:T(8,128)(2,1)S(1)}, u32[]{:S(2)}, u32[]{:S(2)}) %collective-permute-start) | collective-permute-done | bytes 86048 | tf_op jit(solution)/shard_map/ppermute | solution.py:201
  9.8 4.0 %collective-permute-done.1.refs_1_ = bf16[16,2688]{1,0:T(8,128)(2,1)S(1)} collective-permute-done((bf16[16,2688]{1,0:T(8,128)(2,1)S(1)}, bf16[16,2688]{1,0:T(8,128)(2,1)S(1)}, u32[]{:S(2)}, u32[]{:S(2)}) %collective-permute-start.1) | collective-permute-done | bytes 86048 | tf_op jit(solution)/shard_map/ppermute | solution.py:201
  13.8 1.6 %collective-permute-start.3 = (bf16[32,2688]{1,0:T(8,128)(2,1)S(1)}, bf16[32,2688]{1,0:T(8,128)(2,1)S(1)}, u32[]{:S(2)}, u32[]{:S(2)}) collective-permute-start(bf16[32,2688]{1,0:T(8,128)(2,1)S(1)} %get-tuple-element.40), channel_id=1, source_target_pairs={{0,4},{4,0},{8,12},{12,8},{16,20},{20,16},{24,28},{28,24},{1,5},{5... | collective-permute-start | bytes 516104 | tf_op jit(solution)/shard_map/ppermute | solution.py:201
  15.4 1.5 %collective-permute-start.4 = (bf16[32,2688]{1,0:T(8,128)(2,1)S(1)}, bf16[32,2688]{1,0:T(8,128)(2,1)S(1)}, u32[]{:S(2)}, u32[]{:S(2)}) collective-permute-start(bf16[32,2688]{1,0:T(8,128)(2,1)S(1)} %get-tuple-element.39.refs_0_), channel_id=1, source_target_pairs={{0,2},{1,3},{2,0},{3,1},{4,6},{5,7},{6,4},{7,5},{8,10},{9,11},{10,... | collective-permute-start | bytes 516104 | tf_op jit(solution)/shard_map/ppermute | solution.py:201
  17.3 2.2 %collective-permute-done.3.refs_1_ = bf16[32,2688]{1,0:T(8,128)(2,1)S(1)} collective-permute-done((bf16[32,2688]{1,0:T(8,128)(2,1)S(1)}, bf16[32,2688]{1,0:T(8,128)(2,1)S(1)}, u32[]{:S(2)}, u32[]{:S(2)}) %collective-permute-start.3) | collective-permute-done | bytes 172064 | tf_op jit(solution)/shard_map/ppermute | solution.py:201
  19.6 2.9 %collective-permute-done.4.refs_2_ = bf16[32,2688]{1,0:T(8,128)(2,1)S(1)} collective-permute-done((bf16[32,2688]{1,0:T(8,128)(2,1)S(1)}, bf16[32,2688]{1,0:T(8,128)(2,1)S(1)}, u32[]{:S(2)}, u32[]{:S(2)}) %collective-permute-start.4) | collective-permute-done | bytes 172064 | tf_op jit(solution)/shard_map/ppermute | solution.py:201
  22.5 1.9 %collective-permute-done.5.refs_3_ = bf16[32,2688]{1,0:T(8,128)(2,1)S(1)} collective-permute-done((bf16[32,2688]{1,0:T(8,128)(2,1)S(1)}, bf16[32,2688]{1,0:T(8,128)(2,1)S(1)}, u32[]{:S(2)}, u32[]{:S(2)}) %collective-permute-start.5) | collective-permute-done | bytes 172064 | tf_op jit(solution)/shard_map/ppermute | solution.py:201
  25.0 0.8 %shard_map.76 = (f32[192,256]{1,0:T(8,128)S(1)}, f32[192,256]{1,0:T(8,128)S(1)}) custom-call(s32[8,128]{1,0:T(8,128)S(1)} %get-tuple-element.34.info, bf16[2,3584,256]{2,1,0:T(8,128)(2,1)S(1)} %copy-done.1, bf16[2,3584,256]{2,1,0:T(8,128)(2,1)S(1)} %copy-done.2, bf16[2,256,3584]{2,1,0:T(8,128)(2,1)S(1)} %copy-done, ...), custom_call_target="tpu_custom_call" | custom-call | flops 1000 | bytes 1000 | tf_op jit(solution)/shard_map/pallas_call | solution.py:188
  26.7 1.0 %shard_map.77 = (bf16[192,256]{1,0:T(8,128)(2,1)S(1)}, bf16[64,2688]{1,0:T(8,128)(2,1)S(1)}) custom-call(s32[8,128]{1,0:T(8,128)S(1)} %get-tuple-element.34.info, bf16[2,3584,256]{2,1,0:T(8,128)(2,1)S(1)} %copy-done.1, bf16[2,3584,256]{2,1,0:T(8,128)(2,1)S(1)} %copy-done.2, bf16[2,256,3584]{2,1,0:T(8,128)(2,1)S(1)} %copy-done, ...), custom_call_target="tpu_custom_call" | custom-call | flops 1000 | bytes 1000 | tf_op jit(solution)/shard_map/pallas_call | solution.py:188
  29.5 1.5 %collective-permute-start.9 = (bf16[16,2688]{1,0:T(8,128)(2,1)S(1)}, bf16[16,2688]{1,0:T(8,128)(2,1)S(1)}, u32[]{:S(2)}, u32[]{:S(2)}) collective-permute-start(bf16[16,2688]{1,0:T(8,128)(2,1)S(1)} %get-tuple-element.47), channel_id=1, source_target_pairs={{0,2},{1,3},{2,0},{3,1},{4,6},{5,7},{6,4},{7,5},{8,10},{9,11},{10,... | collective-permute-start | bytes 258056 | tf_op jit(solution)/shard_map/ppermute | solution.py:201
  31.0 1.5 %collective-permute-start.11 = (bf16[16,2688]{1,0:T(8,128)(2,1)S(1)}, bf16[16,2688]{1,0:T(8,128)(2,1)S(1)}, u32[]{:S(2)}, u32[]{:S(2)}) collective-permute-start(bf16[16,2688]{1,0:T(8,128)(2,1)S(1)} %get-tuple-element.51), channel_id=1, source_target_pairs={{0,6},{1,7},{2,4},{3,5},{4,2},{5,3},{6,0},{7,1},{8,14},{9,15},{10,... | collective-permute-start | bytes 258056 | tf_op jit(solution)/shard_map/ppermute | solution.py:201
  32.6 0.7 %collective-permute-start.12 = (bf16[16,2688]{1,0:T(8,128)(2,1)S(1)}, bf16[16,2688]{1,0:T(8,128)(2,1)S(1)}, u32[]{:S(2)}, u32[]{:S(2)}) collective-permute-start(bf16[16,2688]{1,0:T(8,128)(2,1)S(1)} %get-tuple-element.52), channel_id=1, source_target_pairs={{0,4},{4,0},{8,12},{12,8},{16,20},{20,16},{24,28},{28,24},{1,5},{5... | collective-permute-start | bytes 258056 | tf_op jit(solution)/shard_map/ppermute | solution.py:201
  33.2 1.4 %collective-permute-start.15 = (bf16[16,2688]{1,0:T(8,128)(2,1)S(1)}, bf16[16,2688]{1,0:T(8,128)(2,1)S(1)}, u32[]{:S(2)}, u32[]{:S(2)}) collective-permute-start(bf16[16,2688]{1,0:T(8,128)(2,1)S(1)} %get-tuple-element.55), channel_id=1, source_target_pairs={{0,2},{1,3},{2,0},{3,1},{4,6},{5,7},{6,4},{7,5},{8,10},{9,11},{10,... | collective-permute-start | bytes 258056 | tf_op jit(solution)/shard_map/ppermute | solution.py:201
  34.6 1.5 %collective-permute-start.16 = (bf16[16,2688]{1,0:T(8,128)(2,1)S(1)}, bf16[16,2688]{1,0:T(8,128)(2,1)S(1)}, u32[]{:S(2)}, u32[]{:S(2)}) collective-permute-start(bf16[16,2688]{1,0:T(8,128)(2,1)S(1)} %get-tuple-element.57), channel_id=1, source_target_pairs={{0,6},{1,7},{2,4},{3,5},{4,2},{5,3},{6,0},{7,1},{8,14},{9,15},{10,... | collective-permute-start | bytes 258056 | tf_op jit(solution)/shard_map/ppermute | solution.py:201
  36.7 0.8 %collective-permute-done.11.refs_2_ = bf16[16,2688]{1,0:T(8,128)(2,1)S(1)} collective-permute-done((bf16[16,2688]{1,0:T(8,128)(2,1)S(1)}, bf16[16,2688]{1,0:T(8,128)(2,1)S(1)}, u32[]{:S(2)}, u32[]{:S(2)}) %collective-permute-start.11) | collective-permute-done | bytes 86048 | tf_op jit(solution)/shard_map/ppermute | solution.py:201
  37.6 3.1 %collective-permute-done.12.refs_3_ = bf16[16,2688]{1,0:T(8,128)(2,1)S(1)} collective-permute-done((bf16[16,2688]{1,0:T(8,128)(2,1)S(1)}, bf16[16,2688]{1,0:T(8,128)(2,1)S(1)}, u32[]{:S(2)}, u32[]{:S(2)}) %collective-permute-start.12) | collective-permute-done | bytes 86048 | tf_op jit(solution)/shard_map/ppermute | solution.py:201
  40.8 2.3 %collective-permute-start.13 = (bf16[16,2688]{1,0:T(8,128)(2,1)S(1)}, bf16[16,2688]{1,0:T(8,128)(2,1)S(1)}, u32[]{:S(2)}, u32[]{:S(2)}) collective-permute-start(bf16[16,2688]{1,0:T(8,128)(2,1)S(1)} %get-tuple-element.53), channel_id=1, source_target_pairs={{0,24},{4,28},{8,16},{12,20},{16,8},{20,12},{24,0},{28,4},{1,25},{... | collective-permute-start | bytes 258056 | tf_op jit(solution)/shard_map/ppermute | solution.py:201
  43.1 2.3 %collective-permute-start.18 = (bf16[16,2688]{1,0:T(8,128)(2,1)S(1)}, bf16[16,2688]{1,0:T(8,128)(2,1)S(1)}, u32[]{:S(2)}, u32[]{:S(2)}) collective-permute-start(bf16[16,2688]{1,0:T(8,128)(2,1)S(1)} %get-tuple-element.59), channel_id=1, source_target_pairs={{0,8},{4,12},{8,0},{12,4},{16,24},{20,28},{24,16},{28,20},{1,9},{5... | collective-permute-start | bytes 258056 | tf_op jit(solution)/shard_map/ppermute | solution.py:201
  45.3 1.8 %collective-permute-done.13.refs_0_ = bf16[16,2688]{1,0:T(8,128)(2,1)S(1)} collective-permute-done((bf16[16,2688]{1,0:T(8,128)(2,1)S(1)}, bf16[16,2688]{1,0:T(8,128)(2,1)S(1)}, u32[]{:S(2)}, u32[]{:S(2)}) %collective-permute-start.13) | collective-permute-done | bytes 86048 | tf_op jit(solution)/shard_map/ppermute | solution.py:201
  47.1 1.8 %collective-permute-done.14.refs_1_ = bf16[16,2688]{1,0:T(8,128)(2,1)S(1)} collective-permute-done((bf16[16,2688]{1,0:T(8,128)(2,1)S(1)}, bf16[16,2688]{1,0:T(8,128)(2,1)S(1)}, u32[]{:S(2)}, u32[]{:S(2)}) %collective-permute-start.14) | collective-permute-done | bytes 86048 | tf_op jit(solution)/shard_map/ppermute | solution.py:201
  49.0 1.2 %shard_map.84 = bf16[128,896]{1,0:T(8,128)(2,1)} custom-call(bf16[3,2,64,128]{3,2,1,0:T(8,128)(2,1)S(1)} %get-tuple-element.33.mixtures, bf16[16,2688]{1,0:T(8,128)(2,1)S(1)} %collective-permute-done.13.refs_0_, bf16[16,2688]{1,0:T(8,128)(2,1)S(1)} %collective-permute-done.14.refs_1_, bf16[16,2688]{1,0:T(8,128)(2,1)S(1)} %collective-permute-done.18.refs_2_, ...), custom_call_target="tpu_custom_call" | custom-call | flops 1000 | bytes 1000 | tf_op jit(solution)/shard_map/pallas_call | solution.py:188
  (32 shorter events, 4.5 us)
Async XLA Ops:
  0.0 25.0 %copy-start = (bf16[2,256,3584]{2,1,0:T(8,128)(2,1)S(1)}, bf16[2,256,3584]{2,1,0:T(8,128)(2,1)}, u32[]{:S(2)}) copy-start(bf16[2,256,3584]{2,1,0:T(8,128)(2,1)} %down.7) | copy-start | bytes 11010052
  0.0 25.0 %copy-start.1 = (bf16[2,3584,256]{2,1,0:T(8,128)(2,1)S(1)}, bf16[2,3584,256]{2,1,0:T(8,128)(2,1)}, u32[]{:S(2)}) copy-start(bf16[2,3584,256]{2,1,0:T(8,128)(2,1)} %gate.3) | copy-start | bytes 11010052
  0.0 25.0 %copy-start.2 = (bf16[2,3584,256]{2,1,0:T(8,128)(2,1)S(1)}, bf16[2,3584,256]{2,1,0:T(8,128)(2,1)}, u32[]{:S(2)}) copy-start(bf16[2,3584,256]{2,1,0:T(8,128)(2,1)} %up.3) | copy-start | bytes 11010052
  1.4 8.4 %collective-permute-start = (bf16[16,2688]{1,0:T(8,128)(2,1)S(1)}, bf16[16,2688]{1,0:T(8,128)(2,1)S(1)}, u32[]{:S(2)}, u32[]{:S(2)}) collective-permute-start(bf16[16,2688]{1,0:T(8,128)(2,1)S(1)} %get-tuple-element.35), channel_id=1, source_target_pairs={{0,24},{4,28},{8,16},{12,20},{16,8},{20,12},{24,0},{28,4},{1,25},{... | collective-permute-start | bytes 258056 | tf_op jit(solution)/shard_map/ppermute | solution.py:201
  6.5 7.2 %collective-permute-start.1 = (bf16[16,2688]{1,0:T(8,128)(2,1)S(1)}, bf16[16,2688]{1,0:T(8,128)(2,1)S(1)}, u32[]{:S(2)}, u32[]{:S(2)}) collective-permute-start(bf16[16,2688]{1,0:T(8,128)(2,1)S(1)} %get-tuple-element.36), channel_id=1, source_target_pairs={{0,16},{4,20},{8,24},{12,28},{16,0},{20,4},{24,8},{28,12},{1,17},{... | collective-permute-start | bytes 258056 | tf_op jit(solution)/shard_map/ppermute | solution.py:201
  6.5 7.2 %collective-permute-start.2 = (bf16[16,2688]{1,0:T(8,128)(2,1)S(1)}, bf16[16,2688]{1,0:T(8,128)(2,1)S(1)}, u32[]{:S(2)}, u32[]{:S(2)}) collective-permute-start(bf16[16,2688]{1,0:T(8,128)(2,1)S(1)} %get-tuple-element.37), channel_id=1, source_target_pairs={{0,8},{4,12},{8,0},{12,4},{16,24},{20,28},{24,16},{28,20},{1,9},{5... | collective-permute-start | bytes 258056 | tf_op jit(solution)/shard_map/ppermute | solution.py:201
  13.8 5.8 %collective-permute-start.3 = (bf16[32,2688]{1,0:T(8,128)(2,1)S(1)}, bf16[32,2688]{1,0:T(8,128)(2,1)S(1)}, u32[]{:S(2)}, u32[]{:S(2)}) collective-permute-start(bf16[32,2688]{1,0:T(8,128)(2,1)S(1)} %get-tuple-element.40), channel_id=1, source_target_pairs={{0,4},{4,0},{8,12},{12,8},{16,20},{20,16},{24,28},{28,24},{1,5},{5... | collective-permute-start | bytes 516104 | tf_op jit(solution)/shard_map/ppermute | solution.py:201
  15.4 7.2 %collective-permute-start.4 = (bf16[32,2688]{1,0:T(8,128)(2,1)S(1)}, bf16[32,2688]{1,0:T(8,128)(2,1)S(1)}, u32[]{:S(2)}, u32[]{:S(2)}) collective-permute-start(bf16[32,2688]{1,0:T(8,128)(2,1)S(1)} %get-tuple-element.39.refs_0_), channel_id=1, source_target_pairs={{0,2},{1,3},{2,0},{3,1},{4,6},{5,7},{6,4},{7,5},{8,10},{9,11},{10,... | collective-permute-start | bytes 516104 | tf_op jit(solution)/shard_map/ppermute | solution.py:201
  16.9 7.5 %collective-permute-start.5 = (bf16[32,2688]{1,0:T(8,128)(2,1)S(1)}, bf16[32,2688]{1,0:T(8,128)(2,1)S(1)}, u32[]{:S(2)}, u32[]{:S(2)}) collective-permute-start(bf16[32,2688]{1,0:T(8,128)(2,1)S(1)} %get-tuple-element.40), channel_id=1, source_target_pairs={{0,6},{1,7},{2,4},{3,5},{4,2},{5,3},{6,0},{7,1},{8,14},{9,15},{10,... | collective-permute-start | bytes 516104 | tf_op jit(solution)/shard_map/ppermute | solution.py:201
  24.5 1.7 %collective-permute-start.6 = (bf16[64,2688]{1,0:T(8,128)(2,1)S(1)}, bf16[64,2688]{1,0:T(8,128)(2,1)S(1)}, u32[]{:S(2)}, u32[]{:S(2)}) collective-permute-start(bf16[64,2688]{1,0:T(8,128)(2,1)S(1)} %get-tuple-element.41.refs_0_), channel_id=1, source_target_pairs={{0,1},{1,0},{2,3},{3,2},{4,5},{5,4},{6,7},{7,6},{8,9},{9,8},{10,11... | collective-permute-start | bytes 1032200 | tf_op jit(solution)/shard_map/ppermute | solution.py:201
  24.5 2.1 %collective-permute-start.7 = (bf16[64,2688]{1,0:T(8,128)(2,1)S(1)}, bf16[64,2688]{1,0:T(8,128)(2,1)S(1)}, u32[]{:S(2)}, u32[]{:S(2)}) collective-permute-start(bf16[64,2688]{1,0:T(8,128)(2,1)S(1)} %get-tuple-element.42.refs_1_), channel_id=1, source_target_pairs={{0,1},{1,0},{2,3},{3,2},{4,5},{5,4},{6,7},{7,6},{8,9},{9,8},{10,11... | collective-permute-start | bytes 1032200 | tf_op jit(solution)/shard_map/ppermute | solution.py:201
  27.7 1.7 %collective-permute-start.8 = (bf16[64,2688]{1,0:T(8,128)(2,1)S(1)}, bf16[64,2688]{1,0:T(8,128)(2,1)S(1)}, u32[]{:S(2)}, u32[]{:S(2)}) collective-permute-start(bf16[64,2688]{1,0:T(8,128)(2,1)S(1)} %get-tuple-element.46), channel_id=1, source_target_pairs={{0,1},{1,0},{2,3},{3,2},{4,5},{5,4},{6,7},{7,6},{8,9},{9,8},{10,11... | collective-permute-start | bytes 1032200 | tf_op jit(solution)/shard_map/ppermute | solution.py:201
  28.5 4.0 %collective-permute-start.10 = (bf16[64,2688]{1,0:T(8,128)(2,1)S(1)}, bf16[64,2688]{1,0:T(8,128)(2,1)S(1)}, u32[]{:S(2)}, u32[]{:S(2)}) collective-permute-start(bf16[64,2688]{1,0:T(8,128)(2,1)S(1)} %get-tuple-element.49), channel_id=1, source_target_pairs={{0,1},{1,0},{2,3},{3,2},{4,5},{5,4},{6,7},{7,6},{8,9},{9,8},{10,11... | collective-permute-start | bytes 1032200 | tf_op jit(solution)/shard_map/ppermute | solution.py:201
  29.5 6.6 %collective-permute-start.9 = (bf16[16,2688]{1,0:T(8,128)(2,1)S(1)}, bf16[16,2688]{1,0:T(8,128)(2,1)S(1)}, u32[]{:S(2)}, u32[]{:S(2)}) collective-permute-start(bf16[16,2688]{1,0:T(8,128)(2,1)S(1)} %get-tuple-element.47), channel_id=1, source_target_pairs={{0,2},{1,3},{2,0},{3,1},{4,6},{5,7},{6,4},{7,5},{8,10},{9,11},{10,... | collective-permute-start | bytes 258056 | tf_op jit(solution)/shard_map/ppermute | solution.py:201
  31.0 6.6 %collective-permute-start.11 = (bf16[16,2688]{1,0:T(8,128)(2,1)S(1)}, bf16[16,2688]{1,0:T(8,128)(2,1)S(1)}, u32[]{:S(2)}, u32[]{:S(2)}) collective-permute-start(bf16[16,2688]{1,0:T(8,128)(2,1)S(1)} %get-tuple-element.51), channel_id=1, source_target_pairs={{0,6},{1,7},{2,4},{3,5},{4,2},{5,3},{6,0},{7,1},{8,14},{9,15},{10,... | collective-permute-start | bytes 258056 | tf_op jit(solution)/shard_map/ppermute | solution.py:201
  32.6 8.1 %collective-permute-start.12 = (bf16[16,2688]{1,0:T(8,128)(2,1)S(1)}, bf16[16,2688]{1,0:T(8,128)(2,1)S(1)}, u32[]{:S(2)}, u32[]{:S(2)}) collective-permute-start(bf16[16,2688]{1,0:T(8,128)(2,1)S(1)} %get-tuple-element.52), channel_id=1, source_target_pairs={{0,4},{4,0},{8,12},{12,8},{16,20},{20,16},{24,28},{28,24},{1,5},{5... | collective-permute-start | bytes 258056 | tf_op jit(solution)/shard_map/ppermute | solution.py:201
  33.2 9.8 %collective-permute-start.15 = (bf16[16,2688]{1,0:T(8,128)(2,1)S(1)}, bf16[16,2688]{1,0:T(8,128)(2,1)S(1)}, u32[]{:S(2)}, u32[]{:S(2)}) collective-permute-start(bf16[16,2688]{1,0:T(8,128)(2,1)S(1)} %get-tuple-element.55), channel_id=1, source_target_pairs={{0,2},{1,3},{2,0},{3,1},{4,6},{5,7},{6,4},{7,5},{8,10},{9,11},{10,... | collective-permute-start | bytes 258056 | tf_op jit(solution)/shard_map/ppermute | solution.py:201
  34.6 8.4 %collective-permute-start.16 = (bf16[16,2688]{1,0:T(8,128)(2,1)S(1)}, bf16[16,2688]{1,0:T(8,128)(2,1)S(1)}, u32[]{:S(2)}, u32[]{:S(2)}) collective-permute-start(bf16[16,2688]{1,0:T(8,128)(2,1)S(1)} %get-tuple-element.57), channel_id=1, source_target_pairs={{0,6},{1,7},{2,4},{3,5},{4,2},{5,3},{6,0},{7,1},{8,14},{9,15},{10,... | collective-permute-start | bytes 258056 | tf_op jit(solution)/shard_map/ppermute | solution.py:201
  36.1 6.9 %collective-permute-start.17 = (bf16[16,2688]{1,0:T(8,128)(2,1)S(1)}, bf16[16,2688]{1,0:T(8,128)(2,1)S(1)}, u32[]{:S(2)}, u32[]{:S(2)}) collective-permute-start(bf16[16,2688]{1,0:T(8,128)(2,1)S(1)} %get-tuple-element.58), channel_id=1, source_target_pairs={{0,4},{4,0},{8,12},{12,8},{16,20},{20,16},{24,28},{28,24},{1,5},{5... | collective-permute-start | bytes 258056 | tf_op jit(solution)/shard_map/ppermute | solution.py:201
  40.8 6.4 %collective-permute-start.13 = (bf16[16,2688]{1,0:T(8,128)(2,1)S(1)}, bf16[16,2688]{1,0:T(8,128)(2,1)S(1)}, u32[]{:S(2)}, u32[]{:S(2)}) collective-permute-start(bf16[16,2688]{1,0:T(8,128)(2,1)S(1)} %get-tuple-element.53), channel_id=1, source_target_pairs={{0,24},{4,28},{8,16},{12,20},{16,8},{20,12},{24,0},{28,4},{1,25},{... | collective-permute-start | bytes 258056 | tf_op jit(solution)/shard_map/ppermute | solution.py:201
  43.0 5.9 %collective-permute-start.14 = (bf16[16,2688]{1,0:T(8,128)(2,1)S(1)}, bf16[16,2688]{1,0:T(8,128)(2,1)S(1)}, u32[]{:S(2)}, u32[]{:S(2)}) collective-permute-start(bf16[16,2688]{1,0:T(8,128)(2,1)S(1)} %get-tuple-element.54), channel_id=1, source_target_pairs={{0,16},{4,20},{8,24},{12,28},{16,0},{20,4},{24,8},{28,12},{1,17},{... | collective-permute-start | bytes 258056 | tf_op jit(solution)/shard_map/ppermute | solution.py:201
  43.1 5.9 %collective-permute-start.18 = (bf16[16,2688]{1,0:T(8,128)(2,1)S(1)}, bf16[16,2688]{1,0:T(8,128)(2,1)S(1)}, u32[]{:S(2)}, u32[]{:S(2)}) collective-permute-start(bf16[16,2688]{1,0:T(8,128)(2,1)S(1)} %get-tuple-element.59), channel_id=1, source_target_pairs={{0,8},{4,12},{8,0},{12,4},{16,24},{20,28},{24,16},{28,20},{1,9},{5... | collective-permute-start | bytes 258056 | tf_op jit(solution)/shard_map/ppermute | solution.py:201

commit v6 on v5

--- a/solution.py
+++ b/solution.py
@@ -170,17 +170,34 @@
     down_parts(order_of(info, down.shape[0]), numbers, hidden, down, outs)
 
 
-def mix_kernel(mixtures, *refs):
-    *pieces, out = refs
+def mixed_part(mixtures, pieces, columns):
+    share = next(iter(pieces.values())).shape[1] // mixtures.shape[0]
+    weights, rows = [], []
+    for chunk in range(mixtures.shape[0]):
+        for n, piece in pieces.items():
+            size = piece.shape[0]
+            values = piece[:, chunk * share + columns.start : chunk * share + columns.stop]
+            for half in range(2):
+                weights.append(mixtures[chunk, half, n * size : (n + 1) * size, :])
+                rows.append(values)
+    return dot_rows(jnp.concatenate(weights, axis=0), jnp.concatenate(rows, axis=0))
+
+
+def mix_kernel(places, mixtures, *refs):
+    *pieces, out, result, sems = refs
     share = out.shape[1]
-    total = jnp.zeros(out.shape, F32)
-    for chunk in range(mixtures.shape[0]):
-        rows = jnp.concatenate([p[:, chunk * share : (chunk + 1) * share] for p in pieces], axis=0)
-        total = total + dot_rows(mixtures[chunk, 0], rows) + dot_rows(mixtures[chunk, 1], rows)
-    out[...] = total.astype(out.dtype)
-
-
-def call(kernel, outs, *args, specs=None, scratch=(), flops=0):
+    middle = share // 256 * 128
+    copies = []
+    for n, columns in enumerate((slice(0, middle), slice(middle, share))):
+        value = mixed_part(mixtures, dict(zip(places, pieces)), columns)
+        result[:, columns] = value.astype(result.dtype)
+        copies.append(pltpu.make_async_copy(result.at[:, columns], out.at[:, columns], sems.at[n]))
+        copies[-1].start()
+    for copy in copies:
+        copy.wait()
+
+
+def call(kernel, outs, *args, specs=None, out_specs=None, scratch=(), flops=0):
     if specs:
         args = [
             pltpu.with_memory_space_constraint(a, s.memory_space) for a, s in zip(args, specs)
@@ -189,7 +206,7 @@
         kernel,
         out_shape=outs,
         in_specs=specs or [VMEM] * len(args),
-        out_specs=[VMEM] * len(outs),
+        out_specs=out_specs or [VMEM] * len(outs),
         scratch_shapes=list(scratch),
         compiler_params=pltpu.CompilerParams(vmem_limit_bytes=LIMIT),
         cost_estimate=pl.CostEstimate(flops=flops + 1000, bytes_accessed=1000, transcendentals=0),
@@ -220,7 +237,8 @@
     low = 1 << ((owners.bit_length() - 1) // 2)
     high = owners // low
     high_steps = list(range(high - 1, -1, -1))
-    ways_in = [high_steps]
+    ways_in = [high_steps[:1] + high_steps[-1:], high_steps[1:-1]]
+    ways_in = [group for group in ways_in if group]
     ways_out = [high_steps[: high // 2], high_steps[high // 2 :]]
     shape = jax.ShapeDtypeStruct
     piece = shape((low * CAP, wide), BF16)
@@ -244,7 +262,7 @@
             pltpu.VMEM((owners * owned, tok_rows), F32),
             pltpu.SemaphoreType.DMA((4,)),
         ],
-        flops=16 * 10**10,
+        flops=10**10,
     )
     arrived = {k: swapped(p, "expert", k * low) if k else p for k, p in zip(high_steps, pieces)}
 
@@ -322,8 +340,8 @@
     for group, far_lots, near_lots in zip(ways_out, reduced(top), reduced(0)):
         terms = []
         for m in range(low):
+            terms.append(turned(near_lots[m], m, 0) if m else near_lots[m])
             terms.append(turned(far_lots[m], m, top))
-            terms.append(turned(near_lots[m], m, 0) if m else near_lots[m])
         moves = [[[(2 * m, n), (2 * m + 1, n)] for m in range(low)] for n in range(len(group))]
         totals = call(
             functools.partial(sum_kernel, 2 * low, moves), [piece] * len(group), *terms
@@ -331,9 +349,11 @@
         for k, value in zip(group, totals):
             back[k] = swapped(value, "expert", k * low) if k else value
     (mixed_out,) = call(
-        mix_kernel,
+        functools.partial(mix_kernel, range(high)),
         [shape((tok_rows, share), BF16)],
         mixtures, *[back[k] for k in high_steps],
+        out_specs=[HBM],
+        scratch=[pltpu.VMEM((tok_rows, share), BF16), pltpu.SemaphoreType.DMA((2,))],
     )
     return mixed_out
 

time: 50.3 us -> 47.8 us (0.950)
  waiting for transfers between devices: 22.1 us -> 14.8 us
  starting transfers between devices: 22.1 us -> 27.2 us
    ppermute x19 -> x22, waiting for transfers between devices: 22.1 us -> 14.8 us  [swapped(): lax.ppermute(value, axis, [(source, source ^ mask) for source in range(co...]
    ppermute x19 -> x22, starting transfers between devices: 22.1 us -> 27.2 us  [swapped(): lax.ppermute(value, axis, [(source, source ^ mask) for source in range(co...]
    pallas_call x12 -> x13, Pallas kernels: 5.81 us -> 5.59 us  [call(): pl.pallas_call(kernel, out_shape=outs, in_specs=specs or [VMEM] * len(arg...]
  transfers between devices with their start and end apart: 19 -> 22, of which waited for: 12 -> 11; matrix products, arithmetic and copies ran while one was open for 0% -> 0% of each run, Pallas kernels for 4% -> 4%
where the time goes in v6:
time: 47.8 us; the launch traced here: 47.6 us
  starting transfers between devices  27.2 us (57%)
  waiting for transfers between devices  14.8 us (31%)
  Pallas kernels  5.59 us (12%)
    ppermute x22, starting transfers between devices, swapped(): lax.ppermute(value, axis, [(source, source ^ mask) for source in range(co...  27.2 us
    ppermute x22, waiting for transfers between devices, swapped(): lax.ppermute(value, axis, [(source, source ^ mask) for source in range(co...  14.8 us
    pallas_call x13, Pallas kernels, call(): pl.pallas_call(kernel, out_shape=outs, in_specs=specs or [VMEM] * len(arg...  5.59 us
  transfers between devices with their start and end apart: 22, of which 11 were waited for; matrix products, arithmetic and copies ran while one was open for 0% of the time, Pallas kernels for 4%

profile of v6, /device:TPU:0, one launch (start us, length us, event | category | flops | bytes accessed | tf_op | source)
XLA Modules:
  0.0 47.6 jit_solution(4992351529221659011)
XLA Ops:
  0.0 1.4 %shard_map.73 = (bf16[16,2688]{1,0:T(8,128)(2,1)S(1)}, bf16[16,2688]{1,0:T(8,128)(2,1)S(1)}, bf16[16,2688]{1,0:T(8,128)(2,1)S(1)}, bf16[16,2688]{1,0:T(8,128)(2,...) custom-call(s32[8]{0:T(128)} %plan_hbm.1, s32[8,128]{1,0:T(8,128)} %bitcast.2, f32[8,128]{1,0:T(8,128)} %bitcast.3, ...), custom_call_target="tpu_custom_call" | custom-call | flops 10000001024 | bytes 1000 | tf_op jit(solution)/shard_map/pallas_call | solution.py:205
  1.4 5.1 %collective-permute-start = (bf16[16,2688]{1,0:T(8,128)(2,1)S(1)}, bf16[16,2688]{1,0:T(8,128)(2,1)S(1)}, u32[]{:S(2)}, u32[]{:S(2)}) collective-permute-start(bf16[16,2688]{1,0:T(8,128)(2,1)S(1)} %get-tuple-element.37), channel_id=1, source_target_pairs={{0,24},{4,28},{8,16},{12,20},{16,8},{20,12},{24,0},{28,4},{1,25},{... | collective-permute-start | bytes 258056 | tf_op jit(solution)/shard_map/ppermute | solution.py:218
  7.2 2.6 %collective-permute-done.refs_0_ = bf16[16,2688]{1,0:T(8,128)(2,1)S(1)} collective-permute-done((bf16[16,2688]{1,0:T(8,128)(2,1)S(1)}, bf16[16,2688]{1,0:T(8,128)(2,1)S(1)}, u32[]{:S(2)}, u32[]{:S(2)}) %collective-permute-start) | collective-permute-done | bytes 86048 | tf_op jit(solution)/shard_map/ppermute | solution.py:218
  9.8 1.7 %collective-permute-start.1 = (bf16[16,2688]{1,0:T(8,128)(2,1)S(1)}, bf16[16,2688]{1,0:T(8,128)(2,1)S(1)}, u32[]{:S(2)}, u32[]{:S(2)}) collective-permute-start(bf16[16,2688]{1,0:T(8,128)(2,1)S(1)} %get-tuple-element.40), channel_id=1, source_target_pairs={{0,4},{4,0},{8,12},{12,8},{16,20},{20,16},{24,28},{28,24},{1,5},{5... | collective-permute-start | bytes 258056 | tf_op jit(solution)/shard_map/ppermute | solution.py:218
  11.5 1.4 %collective-permute-start.6 = (bf16[16,2688]{1,0:T(8,128)(2,1)S(1)}, bf16[16,2688]{1,0:T(8,128)(2,1)S(1)}, u32[]{:S(2)}, u32[]{:S(2)}) collective-permute-start(bf16[16,2688]{1,0:T(8,128)(2,1)S(1)} %get-tuple-element.40), channel_id=1, source_target_pairs={{0,6},{1,7},{2,4},{3,5},{4,2},{5,3},{6,0},{7,1},{8,14},{9,15},{10,... | collective-permute-start | bytes 258056 | tf_op jit(solution)/shard_map/ppermute | solution.py:218
  13.8 1.6 %collective-permute-start.4 = (bf16[16,2688]{1,0:T(8,128)(2,1)S(1)}, bf16[16,2688]{1,0:T(8,128)(2,1)S(1)}, u32[]{:S(2)}, u32[]{:S(2)}) collective-permute-start(bf16[16,2688]{1,0:T(8,128)(2,1)S(1)} %get-tuple-element.44), channel_id=1, source_target_pairs={{0,4},{4,0},{8,12},{12,8},{16,20},{20,16},{24,28},{28,24},{1,5},{5... | collective-permute-start | bytes 258056 | tf_op jit(solution)/shard_map/ppermute | solution.py:218
  15.4 1.5 %collective-permute-start.5 = (bf16[16,2688]{1,0:T(8,128)(2,1)S(1)}, bf16[16,2688]{1,0:T(8,128)(2,1)S(1)}, u32[]{:S(2)}, u32[]{:S(2)}) collective-permute-start(bf16[16,2688]{1,0:T(8,128)(2,1)S(1)} %get-tuple-element.39.refs_0_), channel_id=1, source_target_pairs={{0,2},{1,3},{2,0},{3,1},{4,6},{5,7},{6,4},{7,5},{8,10},{9,11},{10,... | collective-permute-start | bytes 258056 | tf_op jit(solution)/shard_map/ppermute | solution.py:218
  17.4 1.4 %collective-permute-start.8 = (bf16[16,2688]{1,0:T(8,128)(2,1)S(1)}, bf16[16,2688]{1,0:T(8,128)(2,1)S(1)}, u32[]{:S(2)}, u32[]{:S(2)}) collective-permute-start(bf16[16,2688]{1,0:T(8,128)(2,1)S(1)} %get-tuple-element.44), channel_id=1, source_target_pairs={{0,6},{1,7},{2,4},{3,5},{4,2},{5,3},{6,0},{7,1},{8,14},{9,15},{10,... | collective-permute-start | bytes 258056 | tf_op jit(solution)/shard_map/ppermute | solution.py:218
  18.8 1.9 %collective-permute-done.5.refs_4_ = bf16[16,2688]{1,0:T(8,128)(2,1)S(1)} collective-permute-done((bf16[16,2688]{1,0:T(8,128)(2,1)S(1)}, bf16[16,2688]{1,0:T(8,128)(2,1)S(1)}, u32[]{:S(2)}, u32[]{:S(2)}) %collective-permute-start.5) | collective-permute-done | bytes 86048 | tf_op jit(solution)/shard_map/ppermute | solution.py:218
  20.7 1.2 %collective-permute-done.7.refs_6_ = bf16[16,2688]{1,0:T(8,128)(2,1)S(1)} collective-permute-done((bf16[16,2688]{1,0:T(8,128)(2,1)S(1)}, bf16[16,2688]{1,0:T(8,128)(2,1)S(1)}, u32[]{:S(2)}, u32[]{:S(2)}) %collective-permute-start.7) | collective-permute-done | bytes 86048 | tf_op jit(solution)/shard_map/ppermute | solution.py:218
  21.9 0.9 %collective-permute-done.8.refs_7_ = bf16[16,2688]{1,0:T(8,128)(2,1)S(1)} collective-permute-done((bf16[16,2688]{1,0:T(8,128)(2,1)S(1)}, bf16[16,2688]{1,0:T(8,128)(2,1)S(1)}, u32[]{:S(2)}, u32[]{:S(2)}) %collective-permute-start.8) | collective-permute-done | bytes 86048 | tf_op jit(solution)/shard_map/ppermute | solution.py:218
  25.0 1.0 %shard_map.78 = (bf16[192,256]{1,0:T(8,128)(2,1)S(1)}, bf16[64,2688]{1,0:T(8,128)(2,1)S(1)}) custom-call(s32[8,128]{1,0:T(8,128)S(1)} %get-tuple-element.36.info, bf16[2,3584,256]{2,1,0:T(8,128)(2,1)S(1)} %copy-done.1, bf16[2,3584,256]{2,1,0:T(8,128)(2,1)S(1)} %copy-done.2, bf16[2,256,3584]{2,1,0:T(8,128)(2,1)S(1)} %copy-done, ...), custom_call_target="tpu_custom_call" | custom-call | flops 1000 | bytes 1000 | tf_op jit(solution)/shard_map/pallas_call | solution.py:205
  27.9 1.6 %collective-permute-start.13 = (bf16[16,2688]{1,0:T(8,128)(2,1)S(1)}, bf16[16,2688]{1,0:T(8,128)(2,1)S(1)}, u32[]{:S(2)}, u32[]{:S(2)}) collective-permute-start(bf16[16,2688]{1,0:T(8,128)(2,1)S(1)} %get-tuple-element.54), channel_id=1, source_target_pairs={{0,2},{1,3},{2,0},{3,1},{4,6},{5,7},{6,4},{7,5},{8,10},{9,11},{10,... | collective-permute-start | bytes 258056 | tf_op jit(solution)/shard_map/ppermute | solution.py:218
  29.5 1.3 %collective-permute-start.14 = (bf16[16,2688]{1,0:T(8,128)(2,1)S(1)}, bf16[16,2688]{1,0:T(8,128)(2,1)S(1)}, u32[]{:S(2)}, u32[]{:S(2)}) collective-permute-start(bf16[16,2688]{1,0:T(8,128)(2,1)S(1)} %get-tuple-element.55), channel_id=1, source_target_pairs={{0,4},{4,0},{8,12},{12,8},{16,20},{20,16},{24,28},{28,24},{1,5},{5... | collective-permute-start | bytes 258056 | tf_op jit(solution)/shard_map/ppermute | solution.py:218
  30.8 0.9 %collective-permute-start.15 = (bf16[16,2688]{1,0:T(8,128)(2,1)S(1)}, bf16[16,2688]{1,0:T(8,128)(2,1)S(1)}, u32[]{:S(2)}, u32[]{:S(2)}) collective-permute-start(bf16[16,2688]{1,0:T(8,128)(2,1)S(1)} %get-tuple-element.56), channel_id=1, source_target_pairs={{0,6},{1,7},{2,4},{3,5},{4,2},{5,3},{6,0},{7,1},{8,14},{9,15},{10,... | collective-permute-start | bytes 258056 | tf_op jit(solution)/shard_map/ppermute | solution.py:218
  31.7 1.4 %collective-permute-start.18 = (bf16[16,2688]{1,0:T(8,128)(2,1)S(1)}, bf16[16,2688]{1,0:T(8,128)(2,1)S(1)}, u32[]{:S(2)}, u32[]{:S(2)}) collective-permute-start(bf16[16,2688]{1,0:T(8,128)(2,1)S(1)} %get-tuple-element.60), channel_id=1, source_target_pairs={{0,2},{1,3},{2,0},{3,1},{4,6},{5,7},{6,4},{7,5},{8,10},{9,11},{10,... | collective-permute-start | bytes 258056 | tf_op jit(solution)/shard_map/ppermute | solution.py:218
  33.1 1.2 %collective-permute-start.19 = (bf16[16,2688]{1,0:T(8,128)(2,1)S(1)}, bf16[16,2688]{1,0:T(8,128)(2,1)S(1)}, u32[]{:S(2)}, u32[]{:S(2)}) collective-permute-start(bf16[16,2688]{1,0:T(8,128)(2,1)S(1)} %get-tuple-element.61), channel_id=1, source_target_pairs={{0,4},{4,0},{8,12},{12,8},{16,20},{20,16},{24,28},{28,24},{1,5},{5... | collective-permute-start | bytes 258056 | tf_op jit(solution)/shard_map/ppermute | solution.py:218
  34.3 0.9 %collective-permute-start.20 = (bf16[16,2688]{1,0:T(8,128)(2,1)S(1)}, bf16[16,2688]{1,0:T(8,128)(2,1)S(1)}, u32[]{:S(2)}, u32[]{:S(2)}) collective-permute-start(bf16[16,2688]{1,0:T(8,128)(2,1)S(1)} %get-tuple-element.62), channel_id=1, source_target_pairs={{0,6},{1,7},{2,4},{3,5},{4,2},{5,3},{6,0},{7,1},{8,14},{9,15},{10,... | collective-permute-start | bytes 258056 | tf_op jit(solution)/shard_map/ppermute | solution.py:218
  35.2 1.6 %collective-permute-done.15.refs_3_ = bf16[16,2688]{1,0:T(8,128)(2,1)S(1)} collective-permute-done((bf16[16,2688]{1,0:T(8,128)(2,1)S(1)}, bf16[16,2688]{1,0:T(8,128)(2,1)S(1)}, u32[]{:S(2)}, u32[]{:S(2)}) %collective-permute-start.15) | collective-permute-done | bytes 86048 | tf_op jit(solution)/shard_map/ppermute | solution.py:218
  36.8 2.9 %collective-permute-start.16 = (bf16[16,2688]{1,0:T(8,128)(2,1)S(1)}, bf16[16,2688]{1,0:T(8,128)(2,1)S(1)}, u32[]{:S(2)}, u32[]{:S(2)}) collective-permute-start(bf16[16,2688]{1,0:T(8,128)(2,1)S(1)} %get-tuple-element.57), channel_id=1, source_target_pairs={{0,24},{4,28},{8,16},{12,20},{16,8},{20,12},{24,0},{28,4},{1,25},{... | collective-permute-start | bytes 258056 | tf_op jit(solution)/shard_map/ppermute | solution.py:218
  39.7 1.2 %collective-permute-start.17 = (bf16[16,2688]{1,0:T(8,128)(2,1)S(1)}, bf16[16,2688]{1,0:T(8,128)(2,1)S(1)}, u32[]{:S(2)}, u32[]{:S(2)}) collective-permute-start(bf16[16,2688]{1,0:T(8,128)(2,1)S(1)} %get-tuple-element.58), channel_id=1, source_target_pairs={{0,16},{4,20},{8,24},{12,28},{16,0},{20,4},{24,8},{28,12},{1,17},{... | collective-permute-start | bytes 258056 | tf_op jit(solution)/shard_map/ppermute | solution.py:218
  41.7 2.2 %collective-permute-done.16.refs_0_ = bf16[16,2688]{1,0:T(8,128)(2,1)S(1)} collective-permute-done((bf16[16,2688]{1,0:T(8,128)(2,1)S(1)}, bf16[16,2688]{1,0:T(8,128)(2,1)S(1)}, u32[]{:S(2)}, u32[]{:S(2)}) %collective-permute-start.16) | collective-permute-done | bytes 86048 | tf_op jit(solution)/shard_map/ppermute | solution.py:218
  43.9 2.7 %collective-permute-done.17.refs_1_ = bf16[16,2688]{1,0:T(8,128)(2,1)S(1)} collective-permute-done((bf16[16,2688]{1,0:T(8,128)(2,1)S(1)}, bf16[16,2688]{1,0:T(8,128)(2,1)S(1)}, u32[]{:S(2)}, u32[]{:S(2)}) %collective-permute-start.17) | collective-permute-done | bytes 86048 | tf_op jit(solution)/shard_map/ppermute | solution.py:218
  46.6 1.0 %shard_map.85 = bf16[128,896]{1,0:T(8,128)(2,1)} custom-call(bf16[3,2,64,128]{3,2,1,0:T(8,128)(2,1)S(1)} %get-tuple-element.35.mixtures, bf16[16,2688]{1,0:T(8,128)(2,1)S(1)} %collective-permute-done.16.refs_0_, bf16[16,2688]{1,0:T(8,128)(2,1)S(1)} %collective-permute-done.17.refs_1_, bf16[16,2688]{1,0:T(8,128)(2,1)S(1)} %collective-permute-done.21.refs_2_, ...), custom_call_target="tpu_custom_call" | custom-call | flops 1000 | bytes 1000 | tf_op jit(solution)/shard_map/pallas_call | solution.py:205
  (39 shorter events, 6.9 us)
Async XLA Ops:
  0.0 23.4 %copy-start.1 = (bf16[2,3584,256]{2,1,0:T(8,128)(2,1)S(1)}, bf16[2,3584,256]{2,1,0:T(8,128)(2,1)}, u32[]{:S(2)}) copy-start(bf16[2,3584,256]{2,1,0:T(8,128)(2,1)} %gate.3) | copy-start | bytes 11010052
  0.0 23.4 %copy-start.2 = (bf16[2,3584,256]{2,1,0:T(8,128)(2,1)S(1)}, bf16[2,3584,256]{2,1,0:T(8,128)(2,1)}, u32[]{:S(2)}) copy-start(bf16[2,3584,256]{2,1,0:T(8,128)(2,1)} %up.3) | copy-start | bytes 11010052
  1.4 8.4 %collective-permute-start = (bf16[16,2688]{1,0:T(8,128)(2,1)S(1)}, bf16[16,2688]{1,0:T(8,128)(2,1)S(1)}, u32[]{:S(2)}, u32[]{:S(2)}) collective-permute-start(bf16[16,2688]{1,0:T(8,128)(2,1)S(1)} %get-tuple-element.37), channel_id=1, source_target_pairs={{0,24},{4,28},{8,16},{12,20},{16,8},{20,12},{24,0},{28,4},{1,25},{... | collective-permute-start | bytes 258056 | tf_op jit(solution)/shard_map/ppermute | solution.py:218
  6.5 7.2 %collective-permute-start.2 = (bf16[16,2688]{1,0:T(8,128)(2,1)S(1)}, bf16[16,2688]{1,0:T(8,128)(2,1)S(1)}, u32[]{:S(2)}, u32[]{:S(2)}) collective-permute-start(bf16[16,2688]{1,0:T(8,128)(2,1)S(1)} %get-tuple-element.41), channel_id=1, source_target_pairs={{0,16},{4,20},{8,24},{12,28},{16,0},{20,4},{24,8},{28,12},{1,17},{... | collective-permute-start | bytes 258056 | tf_op jit(solution)/shard_map/ppermute | solution.py:218
  6.5 7.2 %collective-permute-start.3 = (bf16[16,2688]{1,0:T(8,128)(2,1)S(1)}, bf16[16,2688]{1,0:T(8,128)(2,1)S(1)}, u32[]{:S(2)}, u32[]{:S(2)}) collective-permute-start(bf16[16,2688]{1,0:T(8,128)(2,1)S(1)} %get-tuple-element.42), channel_id=1, source_target_pairs={{0,8},{4,12},{8,0},{12,4},{16,24},{20,28},{24,16},{28,20},{1,9},{5... | collective-permute-start | bytes 258056 | tf_op jit(solution)/shard_map/ppermute | solution.py:218
  9.8 7.6 %collective-permute-start.1 = (bf16[16,2688]{1,0:T(8,128)(2,1)S(1)}, bf16[16,2688]{1,0:T(8,128)(2,1)S(1)}, u32[]{:S(2)}, u32[]{:S(2)}) collective-permute-start(bf16[16,2688]{1,0:T(8,128)(2,1)S(1)} %get-tuple-element.40), channel_id=1, source_target_pairs={{0,4},{4,0},{8,12},{12,8},{16,20},{20,16},{24,28},{28,24},{1,5},{5... | collective-permute-start | bytes 258056 | tf_op jit(solution)/shard_map/ppermute | solution.py:218
  11.5 9.2 %collective-permute-start.6 = (bf16[16,2688]{1,0:T(8,128)(2,1)S(1)}, bf16[16,2688]{1,0:T(8,128)(2,1)S(1)}, u32[]{:S(2)}, u32[]{:S(2)}) collective-permute-start(bf16[16,2688]{1,0:T(8,128)(2,1)S(1)} %get-tuple-element.40), channel_id=1, source_target_pairs={{0,6},{1,7},{2,4},{3,5},{4,2},{5,3},{6,0},{7,1},{8,14},{9,15},{10,... | collective-permute-start | bytes 258056 | tf_op jit(solution)/shard_map/ppermute | solution.py:218
  13.8 5.1 %collective-permute-start.4 = (bf16[16,2688]{1,0:T(8,128)(2,1)S(1)}, bf16[16,2688]{1,0:T(8,128)(2,1)S(1)}, u32[]{:S(2)}, u32[]{:S(2)}) collective-permute-start(bf16[16,2688]{1,0:T(8,128)(2,1)S(1)} %get-tuple-element.44), channel_id=1, source_target_pairs={{0,4},{4,0},{8,12},{12,8},{16,20},{20,16},{24,28},{28,24},{1,5},{5... | collective-permute-start | bytes 258056 | tf_op jit(solution)/shard_map/ppermute | solution.py:218
  15.4 5.4 %collective-permute-start.5 = (bf16[16,2688]{1,0:T(8,128)(2,1)S(1)}, bf16[16,2688]{1,0:T(8,128)(2,1)S(1)}, u32[]{:S(2)}, u32[]{:S(2)}) collective-permute-start(bf16[16,2688]{1,0:T(8,128)(2,1)S(1)} %get-tuple-element.39.refs_0_), channel_id=1, source_target_pairs={{0,2},{1,3},{2,0},{3,1},{4,6},{5,7},{6,4},{7,5},{8,10},{9,11},{10,... | collective-permute-start | bytes 258056 | tf_op jit(solution)/shard_map/ppermute | solution.py:218
  16.9 5.0 %collective-permute-start.7 = (bf16[16,2688]{1,0:T(8,128)(2,1)S(1)}, bf16[16,2688]{1,0:T(8,128)(2,1)S(1)}, u32[]{:S(2)}, u32[]{:S(2)}) collective-permute-start(bf16[16,2688]{1,0:T(8,128)(2,1)S(1)} %get-tuple-element.43.refs_2_), channel_id=1, source_target_pairs={{0,2},{1,3},{2,0},{3,1},{4,6},{5,7},{6,4},{7,5},{8,10},{9,11},{10,... | collective-permute-start | bytes 258056 | tf_op jit(solution)/shard_map/ppermute | solution.py:218
  17.4 5.4 %collective-permute-start.8 = (bf16[16,2688]{1,0:T(8,128)(2,1)S(1)}, bf16[16,2688]{1,0:T(8,128)(2,1)S(1)}, u32[]{:S(2)}, u32[]{:S(2)}) collective-permute-start(bf16[16,2688]{1,0:T(8,128)(2,1)S(1)} %get-tuple-element.44), channel_id=1, source_target_pairs={{0,6},{1,7},{2,4},{3,5},{4,2},{5,3},{6,0},{7,1},{8,14},{9,15},{10,... | collective-permute-start | bytes 258056 | tf_op jit(solution)/shard_map/ppermute | solution.py:218
  22.8 1.7 %collective-permute-start.9 = (bf16[64,2688]{1,0:T(8,128)(2,1)S(1)}, bf16[64,2688]{1,0:T(8,128)(2,1)S(1)}, u32[]{:S(2)}, u32[]{:S(2)}) collective-permute-start(bf16[64,2688]{1,0:T(8,128)(2,1)S(1)} %get-tuple-element.45.refs_0_), channel_id=1, source_target_pairs={{0,1},{1,0},{2,3},{3,2},{4,5},{5,4},{6,7},{7,6},{8,9},{9,8},{10,11... | collective-permute-start | bytes 1032200 | tf_op jit(solution)/shard_map/ppermute | solution.py:218
  22.9 2.1 %collective-permute-start.10 = (bf16[64,2688]{1,0:T(8,128)(2,1)S(1)}, bf16[64,2688]{1,0:T(8,128)(2,1)S(1)}, u32[]{:S(2)}, u32[]{:S(2)}) collective-permute-start(bf16[64,2688]{1,0:T(8,128)(2,1)S(1)} %get-tuple-element.46.refs_1_), channel_id=1, source_target_pairs={{0,1},{1,0},{2,3},{3,2},{4,5},{5,4},{6,7},{7,6},{8,9},{9,8},{10,11... | collective-permute-start | bytes 1032200 | tf_op jit(solution)/shard_map/ppermute | solution.py:218
  26.1 1.7 %collective-permute-start.12 = (bf16[64,2688]{1,0:T(8,128)(2,1)S(1)}, bf16[64,2688]{1,0:T(8,128)(2,1)S(1)}, u32[]{:S(2)}, u32[]{:S(2)}) collective-permute-start(bf16[64,2688]{1,0:T(8,128)(2,1)S(1)} %get-tuple-element.53), channel_id=1, source_target_pairs={{0,1},{1,0},{2,3},{3,2},{4,5},{5,4},{6,7},{7,6},{8,9},{9,8},{10,11... | collective-permute-start | bytes 1032200 | tf_op jit(solution)/shard_map/ppermute | solution.py:218
  26.8 2.6 %collective-permute-start.11 = (bf16[64,2688]{1,0:T(8,128)(2,1)S(1)}, bf16[64,2688]{1,0:T(8,128)(2,1)S(1)}, u32[]{:S(2)}, u32[]{:S(2)}) collective-permute-start(bf16[64,2688]{1,0:T(8,128)(2,1)S(1)} %get-tuple-element.51), channel_id=1, source_target_pairs={{0,1},{1,0},{2,3},{3,2},{4,5},{5,4},{6,7},{7,6},{8,9},{9,8},{10,11... | collective-permute-start | bytes 1032200 | tf_op jit(solution)/shard_map/ppermute | solution.py:218
  27.9 6.4 %collective-permute-start.13 = (bf16[16,2688]{1,0:T(8,128)(2,1)S(1)}, bf16[16,2688]{1,0:T(8,128)(2,1)S(1)}, u32[]{:S(2)}, u32[]{:S(2)}) collective-permute-start(bf16[16,2688]{1,0:T(8,128)(2,1)S(1)} %get-tuple-element.54), channel_id=1, source_target_pairs={{0,2},{1,3},{2,0},{3,1},{4,6},{5,7},{6,4},{7,5},{8,10},{9,11},{10,... | collective-permute-start | bytes 258056 | tf_op jit(solution)/shard_map/ppermute | solution.py:218
  29.5 5.6 %collective-permute-start.14 = (bf16[16,2688]{1,0:T(8,128)(2,1)S(1)}, bf16[16,2688]{1,0:T(8,128)(2,1)S(1)}, u32[]{:S(2)}, u32[]{:S(2)}) collective-permute-start(bf16[16,2688]{1,0:T(8,128)(2,1)S(1)} %get-tuple-element.55), channel_id=1, source_target_pairs={{0,4},{4,0},{8,12},{12,8},{16,20},{20,16},{24,28},{28,24},{1,5},{5... | collective-permute-start | bytes 258056 | tf_op jit(solution)/shard_map/ppermute | solution.py:218
  30.8 6.0 %collective-permute-start.15 = (bf16[16,2688]{1,0:T(8,128)(2,1)S(1)}, bf16[16,2688]{1,0:T(8,128)(2,1)S(1)}, u32[]{:S(2)}, u32[]{:S(2)}) collective-permute-start(bf16[16,2688]{1,0:T(8,128)(2,1)S(1)} %get-tuple-element.56), channel_id=1, source_target_pairs={{0,6},{1,7},{2,4},{3,5},{4,2},{5,3},{6,0},{7,1},{8,14},{9,15},{10,... | collective-permute-start | bytes 258056 | tf_op jit(solution)/shard_map/ppermute | solution.py:218
  31.7 9.2 %collective-permute-start.18 = (bf16[16,2688]{1,0:T(8,128)(2,1)S(1)}, bf16[16,2688]{1,0:T(8,128)(2,1)S(1)}, u32[]{:S(2)}, u32[]{:S(2)}) collective-permute-start(bf16[16,2688]{1,0:T(8,128)(2,1)S(1)} %get-tuple-element.60), channel_id=1, source_target_pairs={{0,2},{1,3},{2,0},{3,1},{4,6},{5,7},{6,4},{7,5},{8,10},{9,11},{10,... | collective-permute-start | bytes 258056 | tf_op jit(solution)/shard_map/ppermute | solution.py:218
  33.1 7.8 %collective-permute-start.19 = (bf16[16,2688]{1,0:T(8,128)(2,1)S(1)}, bf16[16,2688]{1,0:T(8,128)(2,1)S(1)}, u32[]{:S(2)}, u32[]{:S(2)}) collective-permute-start(bf16[16,2688]{1,0:T(8,128)(2,1)S(1)} %get-tuple-element.61), channel_id=1, source_target_pairs={{0,4},{4,0},{8,12},{12,8},{16,20},{20,16},{24,28},{28,24},{1,5},{5... | collective-permute-start | bytes 258056 | tf_op jit(solution)/shard_map/ppermute | solution.py:218
  34.3 6.6 %collective-permute-start.20 = (bf16[16,2688]{1,0:T(8,128)(2,1)S(1)}, bf16[16,2688]{1,0:T(8,128)(2,1)S(1)}, u32[]{:S(2)}, u32[]{:S(2)}) collective-permute-start(bf16[16,2688]{1,0:T(8,128)(2,1)S(1)} %get-tuple-element.62), channel_id=1, source_target_pairs={{0,6},{1,7},{2,4},{3,5},{4,2},{5,3},{6,0},{7,1},{8,14},{9,15},{10,... | collective-permute-start | bytes 258056 | tf_op jit(solution)/shard_map/ppermute | solution.py:218
  36.8 7.0 %collective-permute-start.16 = (bf16[16,2688]{1,0:T(8,128)(2,1)S(1)}, bf16[16,2688]{1,0:T(8,128)(2,1)S(1)}, u32[]{:S(2)}, u32[]{:S(2)}) collective-permute-start(bf16[16,2688]{1,0:T(8,128)(2,1)S(1)} %get-tuple-element.57), channel_id=1, source_target_pairs={{0,24},{4,28},{8,16},{12,20},{16,8},{20,12},{24,0},{28,4},{1,25},{... | collective-permute-start | bytes 258056 | tf_op jit(solution)/shard_map/ppermute | solution.py:218
  39.7 6.9 %collective-permute-start.17 = (bf16[16,2688]{1,0:T(8,128)(2,1)S(1)}, bf16[16,2688]{1,0:T(8,128)(2,1)S(1)}, u32[]{:S(2)}, u32[]{:S(2)}) collective-permute-start(bf16[16,2688]{1,0:T(8,128)(2,1)S(1)} %get-tuple-element.58), channel_id=1, source_target_pairs={{0,16},{4,20},{8,24},{12,28},{16,0},{20,4},{24,8},{28,12},{1,17},{... | collective-permute-start | bytes 258056 | tf_op jit(solution)/shard_map/ppermute | solution.py:218
  41.0 5.6 %collective-permute-start.21 = (bf16[16,2688]{1,0:T(8,128)(2,1)S(1)}, bf16[16,2688]{1,0:T(8,128)(2,1)S(1)}, u32[]{:S(2)}, u32[]{:S(2)}) collective-permute-start(bf16[16,2688]{1,0:T(8,128)(2,1)S(1)} %get-tuple-element.63), channel_id=1, source_target_pairs={{0,8},{4,12},{8,0},{12,4},{16,24},{20,28},{24,16},{28,20},{1,9},{5... | collective-permute-start | bytes 258056 | tf_op jit(solution)/shard_map/ppermute | solution.py:218
  (1 other events, 23.4 us)

commit v7 on v6

--- a/solution.py
+++ b/solution.py
@@ -280,9 +280,9 @@
         here += [turned(value, m, 0) if m else value for m, value in enumerate(lots)]
         rows += [(k, m) for m in range(low) for k in group]
     moves = [(n, b) for n, value in enumerate(here) for b in range(value.shape[0] // CAP)]
-    moves = [moves, [(n + len(here), b) for n, b in moves]]
-    here, there = call(
-        functools.partial(regroup_kernel, 2 * len(here), moves), [whole] * 2, *here, *there
+    here, there = (
+        call(functools.partial(regroup_kernel, len(lots), [moves]), [whole], *lots)[0]
+        for lots in (here, there)
     )
     blocks = {0: here, top: there}
     mask = top // 2
@@ -290,7 +290,7 @@
         for n in list(blocks):
             blocks[n ^ mask] = swapped(blocks[n], "dp", mask)
         mask //= 2
-    first = [0, top]
+    first = list(range(top + 1))
     second = [n for n in range(parts) if n not in first]
     sums = [shape((chunks * lines, hidden_share), F32)] * 2
     gate_sum, up_sum = call(
@@ -324,21 +324,28 @@
                     [whole], found[n ^ mask], value,
                 )
             mask *= 2
-        terms = [swapped(value, "dp", mask) if n & mask else value for n, value in found.items()]
-        moves = [
-            [[(t, rows.index((k, m))) for t in range(len(terms))] for k in group]
-            for group in ways_out for m in range(low)
-        ]
-        sums = call(
-            functools.partial(sum_kernel, len(terms), moves),
-            [lot(group) for group in ways_out for m in range(low)],
-            *terms,
-        )
-        return [sums[n : n + low] for n in range(0, len(sums), low)]
-
+        return [swapped(value, "dp", mask) if n & mask else value for n, value in found.items()]
+
+    def summed(wanted, *terms):
+        values, moves, kinds = [value for both in terms for value in both], [], []
+        for group in ways_out:
+            for t, steps in wanted:
+                places = [t * len(terms[t]) + n for n in range(len(terms[t]))]
+                for m in steps:
+                    moves.append([[(n, rows.index((k, m))) for n in places] for k in group])
+                    kinds.append(lot(group))
+        return call(functools.partial(sum_kernel, len(values), moves), kinds, *values)
+
+    far_terms, near_terms = reduced(top), reduced(0)
+    across = summed([(0, [0])], far_terms)
+    others = summed([(0, range(low)), (1, range(1, low))], near_terms, far_terms)
+    lots_out = [
+        [across[g], *others[g * (2 * low - 1) : (g + 1) * (2 * low - 1)]]
+        for g in range(len(ways_out))
+    ]
     back = {}
-    for group, far_lots, near_lots in zip(ways_out, reduced(top), reduced(0)):
-        terms = []
+    for group, lots in zip(ways_out, lots_out):
+        terms, near_lots, far_lots = [], lots[1 : 1 + low], [lots[0], *lots[1 + low :]]
         for m in range(low):
             terms.append(turned(near_lots[m], m, 0) if m else near_lots[m])
             terms.append(turned(far_lots[m], m, top))

time: 47.8 us -> 47 us (0.983)
  waiting for transfers between devices: 14.8 us -> 14.2 us
    ppermute x22, waiting for transfers between devices: 14.8 us -> 14.2 us  [swapped(): lax.ppermute(value, axis, [(source, source ^ mask) for source in range(co...]
    pallas_call x13 -> x14, Pallas kernels: 5.59 us -> 5.6 us  [call(): pl.pallas_call(kernel, out_shape=outs, in_specs=specs or [VMEM] * len(arg...]
  transfers between devices with their start and end apart: 22 -> 22, of which waited for: 11 -> 10; matrix products, arithmetic and copies ran while one was open for 0% -> 0% of each run, Pallas kernels for 4% -> 5%
where the time goes in v7:
time: 47 us; the launch traced here: 46.8 us
  starting transfers between devices  26.8 us (57%)
  waiting for transfers between devices  14.2 us (30%)
  Pallas kernels  5.6 us (12%)
    ppermute x22, starting transfers between devices, swapped(): lax.ppermute(value, axis, [(source, source ^ mask) for source in range(co...  26.8 us
    ppermute x22, waiting for transfers between devices, swapped(): lax.ppermute(value, axis, [(source, source ^ mask) for source in range(co...  14.2 us
    pallas_call x14, Pallas kernels, call(): pl.pallas_call(kernel, out_shape=outs, in_specs=specs or [VMEM] * len(arg...  5.6 us
  transfers between devices with their start and end apart: 22, of which 10 were waited for; matrix products, arithmetic and copies ran while one was open for 0% of the time, Pallas kernels for 5%

profile of v7, /device:TPU:0, one launch (start us, length us, event | category | flops | bytes accessed | tf_op | source)
XLA Modules:
  0.0 46.8 jit_solution(3778922553848013517)
XLA Ops:
  0.0 1.4 %shard_map.73 = (bf16[16,2688]{1,0:T(8,128)(2,1)S(1)}, bf16[16,2688]{1,0:T(8,128)(2,1)S(1)}, bf16[16,2688]{1,0:T(8,128)(2,1)S(1)}, bf16[16,2688]{1,0:T(8,128)(2,...) custom-call(s32[8]{0:T(128)} %plan_hbm.1, s32[8,128]{1,0:T(8,128)} %bitcast.2, f32[8,128]{1,0:T(8,128)} %bitcast.3, ...), custom_call_target="tpu_custom_call" | custom-call | flops 10000001024 | bytes 1000 | tf_op jit(solution)/shard_map/pallas_call | solution.py:205
  1.4 5.1 %collective-permute-start = (bf16[16,2688]{1,0:T(8,128)(2,1)S(1)}, bf16[16,2688]{1,0:T(8,128)(2,1)S(1)}, u32[]{:S(2)}, u32[]{:S(2)}) collective-permute-start(bf16[16,2688]{1,0:T(8,128)(2,1)S(1)} %get-tuple-element.35), channel_id=1, source_target_pairs={{0,24},{4,28},{8,16},{12,20},{16,8},{20,12},{24,0},{28,4},{1,25},{... | collective-permute-start | bytes 258056 | tf_op jit(solution)/shard_map/ppermute | solution.py:218
  7.2 2.6 %collective-permute-done.refs_0_ = bf16[16,2688]{1,0:T(8,128)(2,1)S(1)} collective-permute-done((bf16[16,2688]{1,0:T(8,128)(2,1)S(1)}, bf16[16,2688]{1,0:T(8,128)(2,1)S(1)}, u32[]{:S(2)}, u32[]{:S(2)}) %collective-permute-start) | collective-permute-done | bytes 86048 | tf_op jit(solution)/shard_map/ppermute | solution.py:218
  9.8 1.7 %collective-permute-start.1 = (bf16[16,2688]{1,0:T(8,128)(2,1)S(1)}, bf16[16,2688]{1,0:T(8,128)(2,1)S(1)}, u32[]{:S(2)}, u32[]{:S(2)}) collective-permute-start(bf16[16,2688]{1,0:T(8,128)(2,1)S(1)} %get-tuple-element.38), channel_id=1, source_target_pairs={{0,4},{4,0},{8,12},{12,8},{16,20},{20,16},{24,28},{28,24},{1,5},{5... | collective-permute-start | bytes 258056 | tf_op jit(solution)/shard_map/ppermute | solution.py:218
  11.5 1.4 %collective-permute-start.7 = (bf16[16,2688]{1,0:T(8,128)(2,1)S(1)}, bf16[16,2688]{1,0:T(8,128)(2,1)S(1)}, u32[]{:S(2)}, u32[]{:S(2)}) collective-permute-start(bf16[16,2688]{1,0:T(8,128)(2,1)S(1)} %get-tuple-element.38), channel_id=1, source_target_pairs={{0,6},{1,7},{2,4},{3,5},{4,2},{5,3},{6,0},{7,1},{8,14},{9,15},{10,... | collective-permute-start | bytes 258056 | tf_op jit(solution)/shard_map/ppermute | solution.py:218
  13.8 1.6 %collective-permute-start.4 = (bf16[16,2688]{1,0:T(8,128)(2,1)S(1)}, bf16[16,2688]{1,0:T(8,128)(2,1)S(1)}, u32[]{:S(2)}, u32[]{:S(2)}) collective-permute-start(bf16[16,2688]{1,0:T(8,128)(2,1)S(1)} %get-tuple-element.42), channel_id=1, source_target_pairs={{0,4},{4,0},{8,12},{12,8},{16,20},{20,16},{24,28},{28,24},{1,5},{5... | collective-permute-start | bytes 258056 | tf_op jit(solution)/shard_map/ppermute | solution.py:218
  15.4 1.5 %collective-permute-start.6 = (bf16[16,2688]{1,0:T(8,128)(2,1)S(1)}, bf16[16,2688]{1,0:T(8,128)(2,1)S(1)}, u32[]{:S(2)}, u32[]{:S(2)}) collective-permute-start(bf16[16,2688]{1,0:T(8,128)(2,1)S(1)} %get-tuple-element.37.refs_0_), channel_id=1, source_target_pairs={{0,2},{1,3},{2,0},{3,1},{4,6},{5,7},{6,4},{7,5},{8,10},{9,11},{10,... | collective-permute-start | bytes 258056 | tf_op jit(solution)/shard_map/ppermute | solution.py:218
  17.4 1.4 %collective-permute-start.9 = (bf16[16,2688]{1,0:T(8,128)(2,1)S(1)}, bf16[16,2688]{1,0:T(8,128)(2,1)S(1)}, u32[]{:S(2)}, u32[]{:S(2)}) collective-permute-start(bf16[16,2688]{1,0:T(8,128)(2,1)S(1)} %get-tuple-element.42), channel_id=1, source_target_pairs={{0,6},{1,7},{2,4},{3,5},{4,2},{5,3},{6,0},{7,1},{8,14},{9,15},{10,... | collective-permute-start | bytes 258056 | tf_op jit(solution)/shard_map/ppermute | solution.py:218
  18.9 1.8 %collective-permute-done.6.refs_0_ = bf16[16,2688]{1,0:T(8,128)(2,1)S(1)} collective-permute-done((bf16[16,2688]{1,0:T(8,128)(2,1)S(1)}, bf16[16,2688]{1,0:T(8,128)(2,1)S(1)}, u32[]{:S(2)}, u32[]{:S(2)}) %collective-permute-start.6) | collective-permute-done | bytes 86048 | tf_op jit(solution)/shard_map/ppermute | solution.py:218
  20.7 1.2 %collective-permute-done.8.refs_2_ = bf16[16,2688]{1,0:T(8,128)(2,1)S(1)} collective-permute-done((bf16[16,2688]{1,0:T(8,128)(2,1)S(1)}, bf16[16,2688]{1,0:T(8,128)(2,1)S(1)}, u32[]{:S(2)}, u32[]{:S(2)}) %collective-permute-start.8) | collective-permute-done | bytes 86048 | tf_op jit(solution)/shard_map/ppermute | solution.py:218
  21.9 0.9 %collective-permute-done.9.refs_3_ = bf16[16,2688]{1,0:T(8,128)(2,1)S(1)} collective-permute-done((bf16[16,2688]{1,0:T(8,128)(2,1)S(1)}, bf16[16,2688]{1,0:T(8,128)(2,1)S(1)}, u32[]{:S(2)}, u32[]{:S(2)}) %collective-permute-start.9) | collective-permute-done | bytes 86048 | tf_op jit(solution)/shard_map/ppermute | solution.py:218
  22.9 1.1 %shard_map.78 = (f32[192,256]{1,0:T(8,128)S(1)}, f32[192,256]{1,0:T(8,128)S(1)}) custom-call(s32[8,128]{1,0:T(8,128)S(1)} %get-tuple-element.34.info, bf16[2,3584,256]{2,1,0:T(8,128)(2,1)S(1)} %copy-done.1, bf16[2,3584,256]{2,1,0:T(8,128)(2,1)S(1)} %copy-done.2, bf16[2,256,3584]{2,1,0:T(8,128)(2,1)S(1)} %copy-done, bf16[64,2688]{1,0:T(8,128)(2,1)S(1)} %shard_map.76.refs_0_, ...), custom_call_target="tpu_custom_call" | custom-call | flops 1000 | bytes 1000 | tf_op jit(solution)/shard_map/pallas_call | solution.py:205
  27.0 1.6 %collective-permute-start.13 = (bf16[16,2688]{1,0:T(8,128)(2,1)S(1)}, bf16[16,2688]{1,0:T(8,128)(2,1)S(1)}, u32[]{:S(2)}, u32[]{:S(2)}) collective-permute-start(bf16[16,2688]{1,0:T(8,128)(2,1)S(1)} %get-tuple-element.50), channel_id=1, source_target_pairs={{0,2},{1,3},{2,0},{3,1},{4,6},{5,7},{6,4},{7,5},{8,10},{9,11},{10,... | collective-permute-start | bytes 258056 | tf_op jit(solution)/shard_map/ppermute | solution.py:218
  28.7 1.3 %collective-permute-start.14 = (bf16[16,2688]{1,0:T(8,128)(2,1)S(1)}, bf16[16,2688]{1,0:T(8,128)(2,1)S(1)}, u32[]{:S(2)}, u32[]{:S(2)}) collective-permute-start(bf16[16,2688]{1,0:T(8,128)(2,1)S(1)} %get-tuple-element.51), channel_id=1, source_target_pairs={{0,4},{4,0},{8,12},{12,8},{16,20},{20,16},{24,28},{28,24},{1,5},{5... | collective-permute-start | bytes 258056 | tf_op jit(solution)/shard_map/ppermute | solution.py:218
  30.0 0.9 %collective-permute-start.15 = (bf16[16,2688]{1,0:T(8,128)(2,1)S(1)}, bf16[16,2688]{1,0:T(8,128)(2,1)S(1)}, u32[]{:S(2)}, u32[]{:S(2)}) collective-permute-start(bf16[16,2688]{1,0:T(8,128)(2,1)S(1)} %get-tuple-element.52), channel_id=1, source_target_pairs={{0,6},{1,7},{2,4},{3,5},{4,2},{5,3},{6,0},{7,1},{8,14},{9,15},{10,... | collective-permute-start | bytes 258056 | tf_op jit(solution)/shard_map/ppermute | solution.py:218
  30.9 1.4 %collective-permute-start.18 = (bf16[16,2688]{1,0:T(8,128)(2,1)S(1)}, bf16[16,2688]{1,0:T(8,128)(2,1)S(1)}, u32[]{:S(2)}, u32[]{:S(2)}) collective-permute-start(bf16[16,2688]{1,0:T(8,128)(2,1)S(1)} %get-tuple-element.56), channel_id=1, source_target_pairs={{0,2},{1,3},{2,0},{3,1},{4,6},{5,7},{6,4},{7,5},{8,10},{9,11},{10,... | collective-permute-start | bytes 258056 | tf_op jit(solution)/shard_map/ppermute | solution.py:218
  32.3 1.2 %collective-permute-start.19 = (bf16[16,2688]{1,0:T(8,128)(2,1)S(1)}, bf16[16,2688]{1,0:T(8,128)(2,1)S(1)}, u32[]{:S(2)}, u32[]{:S(2)}) collective-permute-start(bf16[16,2688]{1,0:T(8,128)(2,1)S(1)} %get-tuple-element.57), channel_id=1, source_target_pairs={{0,4},{4,0},{8,12},{12,8},{16,20},{20,16},{24,28},{28,24},{1,5},{5... | collective-permute-start | bytes 258056 | tf_op jit(solution)/shard_map/ppermute | solution.py:218
  33.5 0.9 %collective-permute-start.20 = (bf16[16,2688]{1,0:T(8,128)(2,1)S(1)}, bf16[16,2688]{1,0:T(8,128)(2,1)S(1)}, u32[]{:S(2)}, u32[]{:S(2)}) collective-permute-start(bf16[16,2688]{1,0:T(8,128)(2,1)S(1)} %get-tuple-element.58), channel_id=1, source_target_pairs={{0,6},{1,7},{2,4},{3,5},{4,2},{5,3},{6,0},{7,1},{8,14},{9,15},{10,... | collective-permute-start | bytes 258056 | tf_op jit(solution)/shard_map/ppermute | solution.py:218
  34.4 1.6 %collective-permute-done.15.refs_3_ = bf16[16,2688]{1,0:T(8,128)(2,1)S(1)} collective-permute-done((bf16[16,2688]{1,0:T(8,128)(2,1)S(1)}, bf16[16,2688]{1,0:T(8,128)(2,1)S(1)}, u32[]{:S(2)}, u32[]{:S(2)}) %collective-permute-start.15) | collective-permute-done | bytes 86048 | tf_op jit(solution)/shard_map/ppermute | solution.py:218
  36.0 2.9 %collective-permute-start.16 = (bf16[16,2688]{1,0:T(8,128)(2,1)S(1)}, bf16[16,2688]{1,0:T(8,128)(2,1)S(1)}, u32[]{:S(2)}, u32[]{:S(2)}) collective-permute-start(bf16[16,2688]{1,0:T(8,128)(2,1)S(1)} %get-tuple-element.53), channel_id=1, source_target_pairs={{0,24},{4,28},{8,16},{12,20},{16,8},{20,12},{24,0},{28,4},{1,25},{... | collective-permute-start | bytes 258056 | tf_op jit(solution)/shard_map/ppermute | solution.py:218
  38.9 1.2 %collective-permute-start.17 = (bf16[16,2688]{1,0:T(8,128)(2,1)S(1)}, bf16[16,2688]{1,0:T(8,128)(2,1)S(1)}, u32[]{:S(2)}, u32[]{:S(2)}) collective-permute-start(bf16[16,2688]{1,0:T(8,128)(2,1)S(1)} %get-tuple-element.54), channel_id=1, source_target_pairs={{0,16},{4,20},{8,24},{12,28},{16,0},{20,4},{24,8},{28,12},{1,17},{... | collective-permute-start | bytes 258056 | tf_op jit(solution)/shard_map/ppermute | solution.py:218
  41.0 2.1 %collective-permute-done.16.refs_0_ = bf16[16,2688]{1,0:T(8,128)(2,1)S(1)} collective-permute-done((bf16[16,2688]{1,0:T(8,128)(2,1)S(1)}, bf16[16,2688]{1,0:T(8,128)(2,1)S(1)}, u32[]{:S(2)}, u32[]{:S(2)}) %collective-permute-start.16) | collective-permute-done | bytes 86048 | tf_op jit(solution)/shard_map/ppermute | solution.py:218
  43.1 2.7 %collective-permute-done.17.refs_1_ = bf16[16,2688]{1,0:T(8,128)(2,1)S(1)} collective-permute-done((bf16[16,2688]{1,0:T(8,128)(2,1)S(1)}, bf16[16,2688]{1,0:T(8,128)(2,1)S(1)}, u32[]{:S(2)}, u32[]{:S(2)}) %collective-permute-start.17) | collective-permute-done | bytes 86048 | tf_op jit(solution)/shard_map/ppermute | solution.py:218
  45.8 1.0 %shard_map.86 = bf16[128,896]{1,0:T(8,128)(2,1)} custom-call(bf16[3,2,64,128]{3,2,1,0:T(8,128)(2,1)S(1)} %get-tuple-element.33.mixtures, bf16[16,2688]{1,0:T(8,128)(2,1)S(1)} %collective-permute-done.16.refs_0_, bf16[16,2688]{1,0:T(8,128)(2,1)S(1)} %collective-permute-done.17.refs_1_, bf16[16,2688]{1,0:T(8,128)(2,1)S(1)} %collective-permute-done.21.refs_2_, ...), custom_call_target="tpu_custom_call" | custom-call | flops 1000 | bytes 1000 | tf_op jit(solution)/shard_map/pallas_call | solution.py:205
  (40 shorter events, 6.2 us)
Async XLA Ops:
  0.0 22.9 %copy-start.1 = (bf16[2,3584,256]{2,1,0:T(8,128)(2,1)S(1)}, bf16[2,3584,256]{2,1,0:T(8,128)(2,1)}, u32[]{:S(2)}) copy-start(bf16[2,3584,256]{2,1,0:T(8,128)(2,1)} %gate.3) | copy-start | bytes 11010052
  0.0 22.9 %copy-start.2 = (bf16[2,3584,256]{2,1,0:T(8,128)(2,1)S(1)}, bf16[2,3584,256]{2,1,0:T(8,128)(2,1)}, u32[]{:S(2)}) copy-start(bf16[2,3584,256]{2,1,0:T(8,128)(2,1)} %up.3) | copy-start | bytes 11010052
  1.4 8.4 %collective-permute-start = (bf16[16,2688]{1,0:T(8,128)(2,1)S(1)}, bf16[16,2688]{1,0:T(8,128)(2,1)S(1)}, u32[]{:S(2)}, u32[]{:S(2)}) collective-permute-start(bf16[16,2688]{1,0:T(8,128)(2,1)S(1)} %get-tuple-element.35), channel_id=1, source_target_pairs={{0,24},{4,28},{8,16},{12,20},{16,8},{20,12},{24,0},{28,4},{1,25},{... | collective-permute-start | bytes 258056 | tf_op jit(solution)/shard_map/ppermute | solution.py:218
  6.5 7.2 %collective-permute-start.2 = (bf16[16,2688]{1,0:T(8,128)(2,1)S(1)}, bf16[16,2688]{1,0:T(8,128)(2,1)S(1)}, u32[]{:S(2)}, u32[]{:S(2)}) collective-permute-start(bf16[16,2688]{1,0:T(8,128)(2,1)S(1)} %get-tuple-element.39), channel_id=1, source_target_pairs={{0,16},{4,20},{8,24},{12,28},{16,0},{20,4},{24,8},{28,12},{1,17},{... | collective-permute-start | bytes 258056 | tf_op jit(solution)/shard_map/ppermute | solution.py:218
  6.5 7.2 %collective-permute-start.3 = (bf16[16,2688]{1,0:T(8,128)(2,1)S(1)}, bf16[16,2688]{1,0:T(8,128)(2,1)S(1)}, u32[]{:S(2)}, u32[]{:S(2)}) collective-permute-start(bf16[16,2688]{1,0:T(8,128)(2,1)S(1)} %get-tuple-element.40), channel_id=1, source_target_pairs={{0,8},{4,12},{8,0},{12,4},{16,24},{20,28},{24,16},{28,20},{1,9},{5... | collective-permute-start | bytes 258056 | tf_op jit(solution)/shard_map/ppermute | solution.py:218
  9.8 7.6 %collective-permute-start.1 = (bf16[16,2688]{1,0:T(8,128)(2,1)S(1)}, bf16[16,2688]{1,0:T(8,128)(2,1)S(1)}, u32[]{:S(2)}, u32[]{:S(2)}) collective-permute-start(bf16[16,2688]{1,0:T(8,128)(2,1)S(1)} %get-tuple-element.38), channel_id=1, source_target_pairs={{0,4},{4,0},{8,12},{12,8},{16,20},{20,16},{24,28},{28,24},{1,5},{5... | collective-permute-start | bytes 258056 | tf_op jit(solution)/shard_map/ppermute | solution.py:218
  11.5 9.2 %collective-permute-start.7 = (bf16[16,2688]{1,0:T(8,128)(2,1)S(1)}, bf16[16,2688]{1,0:T(8,128)(2,1)S(1)}, u32[]{:S(2)}, u32[]{:S(2)}) collective-permute-start(bf16[16,2688]{1,0:T(8,128)(2,1)S(1)} %get-tuple-element.38), channel_id=1, source_target_pairs={{0,6},{1,7},{2,4},{3,5},{4,2},{5,3},{6,0},{7,1},{8,14},{9,15},{10,... | collective-permute-start | bytes 258056 | tf_op jit(solution)/shard_map/ppermute | solution.py:218
  13.8 5.1 %collective-permute-start.4 = (bf16[16,2688]{1,0:T(8,128)(2,1)S(1)}, bf16[16,2688]{1,0:T(8,128)(2,1)S(1)}, u32[]{:S(2)}, u32[]{:S(2)}) collective-permute-start(bf16[16,2688]{1,0:T(8,128)(2,1)S(1)} %get-tuple-element.42), channel_id=1, source_target_pairs={{0,4},{4,0},{8,12},{12,8},{16,20},{20,16},{24,28},{28,24},{1,5},{5... | collective-permute-start | bytes 258056 | tf_op jit(solution)/shard_map/ppermute | solution.py:218
  15.4 5.4 %collective-permute-start.6 = (bf16[16,2688]{1,0:T(8,128)(2,1)S(1)}, bf16[16,2688]{1,0:T(8,128)(2,1)S(1)}, u32[]{:S(2)}, u32[]{:S(2)}) collective-permute-start(bf16[16,2688]{1,0:T(8,128)(2,1)S(1)} %get-tuple-element.37.refs_0_), channel_id=1, source_target_pairs={{0,2},{1,3},{2,0},{3,1},{4,6},{5,7},{6,4},{7,5},{8,10},{9,11},{10,... | collective-permute-start | bytes 258056 | tf_op jit(solution)/shard_map/ppermute | solution.py:218
  16.9 5.0 %collective-permute-start.8 = (bf16[16,2688]{1,0:T(8,128)(2,1)S(1)}, bf16[16,2688]{1,0:T(8,128)(2,1)S(1)}, u32[]{:S(2)}, u32[]{:S(2)}) collective-permute-start(bf16[16,2688]{1,0:T(8,128)(2,1)S(1)} %get-tuple-element.41.refs_2_), channel_id=1, source_target_pairs={{0,2},{1,3},{2,0},{3,1},{4,6},{5,7},{6,4},{7,5},{8,10},{9,11},{10,... | collective-permute-start | bytes 258056 | tf_op jit(solution)/shard_map/ppermute | solution.py:218
  17.4 5.4 %collective-permute-start.9 = (bf16[16,2688]{1,0:T(8,128)(2,1)S(1)}, bf16[16,2688]{1,0:T(8,128)(2,1)S(1)}, u32[]{:S(2)}, u32[]{:S(2)}) collective-permute-start(bf16[16,2688]{1,0:T(8,128)(2,1)S(1)} %get-tuple-element.42), channel_id=1, source_target_pairs={{0,6},{1,7},{2,4},{3,5},{4,2},{5,3},{6,0},{7,1},{8,14},{9,15},{10,... | collective-permute-start | bytes 258056 | tf_op jit(solution)/shard_map/ppermute | solution.py:218
  18.9 4.0 %collective-permute-start.5 = (bf16[64,2688]{1,0:T(8,128)(2,1)S(1)}, bf16[64,2688]{1,0:T(8,128)(2,1)S(1)}, u32[]{:S(2)}, u32[]{:S(2)}) collective-permute-start(bf16[64,2688]{1,0:T(8,128)(2,1)S(1)} %shard_map.76.refs_0_), channel_id=1, source_target_pairs={{0,1},{1,0},{2,3},{3,2},{4,5},{5,4},{6,7},{7,6},{8,9},{9,8},{10,11... | collective-permute-start | bytes 1032200 | tf_op jit(solution)/shard_map/ppermute | solution.py:218
  22.8 1.7 %collective-permute-start.10 = (bf16[64,2688]{1,0:T(8,128)(2,1)S(1)}, bf16[64,2688]{1,0:T(8,128)(2,1)S(1)}, u32[]{:S(2)}, u32[]{:S(2)}) collective-permute-start(bf16[64,2688]{1,0:T(8,128)(2,1)S(1)} %shard_map.77.refs_2_), channel_id=1, source_target_pairs={{0,1},{1,0},{2,3},{3,2},{4,5},{5,4},{6,7},{7,6},{8,9},{9,8},{10,11... | collective-permute-start | bytes 1032200 | tf_op jit(solution)/shard_map/ppermute | solution.py:218
  25.3 1.7 %collective-permute-start.12 = (bf16[64,2688]{1,0:T(8,128)(2,1)S(1)}, bf16[64,2688]{1,0:T(8,128)(2,1)S(1)}, u32[]{:S(2)}, u32[]{:S(2)}) collective-permute-start(bf16[64,2688]{1,0:T(8,128)(2,1)S(1)} %get-tuple-element.48), channel_id=1, source_target_pairs={{0,1},{1,0},{2,3},{3,2},{4,5},{5,4},{6,7},{7,6},{8,9},{9,8},{10,11... | collective-permute-start | bytes 1032200 | tf_op jit(solution)/shard_map/ppermute | solution.py:218
  26.0 2.6 %collective-permute-start.11 = (bf16[64,2688]{1,0:T(8,128)(2,1)S(1)}, bf16[64,2688]{1,0:T(8,128)(2,1)S(1)}, u32[]{:S(2)}, u32[]{:S(2)}) collective-permute-start(bf16[64,2688]{1,0:T(8,128)(2,1)S(1)} %get-tuple-element.47), channel_id=1, source_target_pairs={{0,1},{1,0},{2,3},{3,2},{4,5},{5,4},{6,7},{7,6},{8,9},{9,8},{10,11... | collective-permute-start | bytes 1032200 | tf_op jit(solution)/shard_map/ppermute | solution.py:218
  27.0 6.5 %collective-permute-start.13 = (bf16[16,2688]{1,0:T(8,128)(2,1)S(1)}, bf16[16,2688]{1,0:T(8,128)(2,1)S(1)}, u32[]{:S(2)}, u32[]{:S(2)}) collective-permute-start(bf16[16,2688]{1,0:T(8,128)(2,1)S(1)} %get-tuple-element.50), channel_id=1, source_target_pairs={{0,2},{1,3},{2,0},{3,1},{4,6},{5,7},{6,4},{7,5},{8,10},{9,11},{10,... | collective-permute-start | bytes 258056 | tf_op jit(solution)/shard_map/ppermute | solution.py:218
  28.7 5.7 %collective-permute-start.14 = (bf16[16,2688]{1,0:T(8,128)(2,1)S(1)}, bf16[16,2688]{1,0:T(8,128)(2,1)S(1)}, u32[]{:S(2)}, u32[]{:S(2)}) collective-permute-start(bf16[16,2688]{1,0:T(8,128)(2,1)S(1)} %get-tuple-element.51), channel_id=1, source_target_pairs={{0,4},{4,0},{8,12},{12,8},{16,20},{20,16},{24,28},{28,24},{1,5},{5... | collective-permute-start | bytes 258056 | tf_op jit(solution)/shard_map/ppermute | solution.py:218
  30.0 6.0 %collective-permute-start.15 = (bf16[16,2688]{1,0:T(8,128)(2,1)S(1)}, bf16[16,2688]{1,0:T(8,128)(2,1)S(1)}, u32[]{:S(2)}, u32[]{:S(2)}) collective-permute-start(bf16[16,2688]{1,0:T(8,128)(2,1)S(1)} %get-tuple-element.52), channel_id=1, source_target_pairs={{0,6},{1,7},{2,4},{3,5},{4,2},{5,3},{6,0},{7,1},{8,14},{9,15},{10,... | collective-permute-start | bytes 258056 | tf_op jit(solution)/shard_map/ppermute | solution.py:218
  30.9 9.2 %collective-permute-start.18 = (bf16[16,2688]{1,0:T(8,128)(2,1)S(1)}, bf16[16,2688]{1,0:T(8,128)(2,1)S(1)}, u32[]{:S(2)}, u32[]{:S(2)}) collective-permute-start(bf16[16,2688]{1,0:T(8,128)(2,1)S(1)} %get-tuple-element.56), channel_id=1, source_target_pairs={{0,2},{1,3},{2,0},{3,1},{4,6},{5,7},{6,4},{7,5},{8,10},{9,11},{10,... | collective-permute-start | bytes 258056 | tf_op jit(solution)/shard_map/ppermute | solution.py:218
  32.3 7.8 %collective-permute-start.19 = (bf16[16,2688]{1,0:T(8,128)(2,1)S(1)}, bf16[16,2688]{1,0:T(8,128)(2,1)S(1)}, u32[]{:S(2)}, u32[]{:S(2)}) collective-permute-start(bf16[16,2688]{1,0:T(8,128)(2,1)S(1)} %get-tuple-element.57), channel_id=1, source_target_pairs={{0,4},{4,0},{8,12},{12,8},{16,20},{20,16},{24,28},{28,24},{1,5},{5... | collective-permute-start | bytes 258056 | tf_op jit(solution)/shard_map/ppermute | solution.py:218
  33.5 6.6 %collective-permute-start.20 = (bf16[16,2688]{1,0:T(8,128)(2,1)S(1)}, bf16[16,2688]{1,0:T(8,128)(2,1)S(1)}, u32[]{:S(2)}, u32[]{:S(2)}) collective-permute-start(bf16[16,2688]{1,0:T(8,128)(2,1)S(1)} %get-tuple-element.58), channel_id=1, source_target_pairs={{0,6},{1,7},{2,4},{3,5},{4,2},{5,3},{6,0},{7,1},{8,14},{9,15},{10,... | collective-permute-start | bytes 258056 | tf_op jit(solution)/shard_map/ppermute | solution.py:218
  36.0 7.0 %collective-permute-start.16 = (bf16[16,2688]{1,0:T(8,128)(2,1)S(1)}, bf16[16,2688]{1,0:T(8,128)(2,1)S(1)}, u32[]{:S(2)}, u32[]{:S(2)}) collective-permute-start(bf16[16,2688]{1,0:T(8,128)(2,1)S(1)} %get-tuple-element.53), channel_id=1, source_target_pairs={{0,24},{4,28},{8,16},{12,20},{16,8},{20,12},{24,0},{28,4},{1,25},{... | collective-permute-start | bytes 258056 | tf_op jit(solution)/shard_map/ppermute | solution.py:218
  38.9 6.9 %collective-permute-start.17 = (bf16[16,2688]{1,0:T(8,128)(2,1)S(1)}, bf16[16,2688]{1,0:T(8,128)(2,1)S(1)}, u32[]{:S(2)}, u32[]{:S(2)}) collective-permute-start(bf16[16,2688]{1,0:T(8,128)(2,1)S(1)} %get-tuple-element.54), channel_id=1, source_target_pairs={{0,16},{4,20},{8,24},{12,28},{16,0},{20,4},{24,8},{28,12},{1,17},{... | collective-permute-start | bytes 258056 | tf_op jit(solution)/shard_map/ppermute | solution.py:218
  40.2 5.6 %collective-permute-start.21 = (bf16[16,2688]{1,0:T(8,128)(2,1)S(1)}, bf16[16,2688]{1,0:T(8,128)(2,1)S(1)}, u32[]{:S(2)}, u32[]{:S(2)}) collective-permute-start(bf16[16,2688]{1,0:T(8,128)(2,1)S(1)} %get-tuple-element.59), channel_id=1, source_target_pairs={{0,8},{4,12},{8,0},{12,4},{16,24},{20,28},{24,16},{28,20},{1,9},{5... | collective-permute-start | bytes 258056 | tf_op jit(solution)/shard_map/ppermute | solution.py:218
  (1 other events, 22.9 us)

commit v8 on v7

--- a/solution.py
+++ b/solution.py
@@ -23,9 +23,27 @@
     return lax.dot_general(left, right, (((0,), (0,)), ((), ())), preferred_element_type=F32)
 
 
+def dispatch(owned, low, high_steps, place, tokens, pieces):
+    tok_rows, share = tokens.shape
+    own_index = lax.axis_index("expert")
+    slot = lax.broadcasted_iota(jnp.int32, (CAP, tok_rows), 0)
+    size = low * CAP
+    for chunk in range(owned + 1):
+        picks = []
+        for k, m in [(k, m) for k in high_steps for m in range(low)]:
+            pick = jnp.zeros((CAP, tok_rows), F32)
+            for number in range(owned):
+                line = pl.ds((own_index ^ (k * low + m)) * owned + number, 1)
+                pick = pick + (place[line, :] == slot + chunk * CAP).astype(F32)
+            picks.append(pick)
+        values = dot(jnp.concatenate(picks, axis=0).astype(BF16), tokens[...]).astype(BF16)
+        for n, piece in enumerate(pieces):
+            piece[:, chunk * share : (chunk + 1) * share] = values[n * size : (n + 1) * size]
+
+
 def route_kernel(owned, low, high_steps, plan_hbm, ids_hbm, gates_hbm, tokens_hbm, *refs):
-    high = len(high_steps)
-    pieces, (info, mixtures, plan, ids, gates, tokens, place, weight, sems) = refs[:high], refs[high:]
+    pieces = refs[: len(high_steps)]
+    info, place, weight, tokens, plan, ids, gates, sems = refs[len(high_steps) :]
     sources = (plan_hbm, ids_hbm, gates_hbm, tokens_hbm)
     copies = [
         pltpu.make_async_copy(source, target, sems.at[n])
@@ -34,10 +52,8 @@
     for copy in copies:
         copy.start()
     choices, tok_rows = ids.shape
-    share = tokens.shape[1]
     owners = plan.shape[0]
     experts = owners * owned
-    steps = [(k, m) for k in high_steps for m in range(low)]
     own_index = lax.axis_index("expert")
     row = lax.broadcasted_iota(jnp.int32, (tok_rows, tok_rows), 0)
     col = lax.broadcasted_iota(jnp.int32, (tok_rows, tok_rows), 1)
@@ -65,26 +81,23 @@
     limit = jnp.where(within == hot, 2 * CAP, CAP)
     start = jnp.where(within == hot, 0, CAP * (1 + within + (within < hot).astype(jnp.int32)))
     place[...] = jnp.where((named > 0.0) & (rank < limit), start + rank, -1)
-    slot = lax.broadcasted_iota(jnp.int32, (CAP, tok_rows), 0)
-    zero = jnp.zeros((CAP, tok_rows), F32)
     copies[3].wait()
+    dispatch(owned, low, high_steps, place, tokens, pieces)
+
+
+def rest_kernel(owned, low, rest_steps, high_steps, place, weight, tokens, *refs):
+    *pieces, mixtures = refs
+    dispatch(owned, low, rest_steps, place, tokens, pieces)
+    own_index = lax.axis_index("expert")
+    slot = lax.broadcasted_iota(jnp.int32, (CAP, place.shape[1]), 0)
     for chunk in range(owned + 1):
-        picks, mixes = [], []
-        for k, m in steps:
-            index = own_index ^ (k * low + m)
-            pick, mix = zero, zero
+        mixes = []
+        for k, m in [(k, m) for k in high_steps for m in range(low)]:
+            mix = jnp.zeros(slot.shape, F32)
             for number in range(owned):
-                line = pl.ds(index * owned + number, 1)
-                match = place[line, :] == slot + chunk * CAP
-                pick = pick + match.astype(F32)
-                mix = mix + jnp.where(match, weight[line, :], 0.0)
-            picks.append(pick)
+                line = pl.ds((own_index ^ (k * low + m)) * owned + number, 1)
+                mix = mix + jnp.where(place[line, :] == slot + chunk * CAP, weight[line, :], 0.0)
             mixes.append(mix)
-        pick = jnp.concatenate(picks, axis=0).astype(BF16)
-        values = dot(pick, tokens[...]).astype(BF16)
-        size = low * CAP
-        for n, piece in enumerate(pieces):
-            piece[:, chunk * share : (chunk + 1) * share] = values[n * size : (n + 1) * size]
         mix = jnp.concatenate(mixes, axis=0)
         rounded = mix.astype(BF16)
         mixtures[chunk, 0] = rounded
@@ -247,23 +260,30 @@
     def lot(group):
         return shape((len(group) * CAP, wide), BF16)
 
-    *pieces, info, mixtures = call(
-        functools.partial(route_kernel, owned, low, high_steps),
-        [piece] * high
-        + [shape((8, 128), jnp.int32), shape((chunks, 2, lines, tok_rows), BF16)],
+    first_steps, rest_steps = high_steps[: high // 2], high_steps[high // 2 :]
+    experts = owners * owned
+    *pieces, info, place, weight, tokens_here = call(
+        functools.partial(route_kernel, owned, low, first_steps),
+        [piece] * len(first_steps)
+        + [shape((8, 128), jnp.int32)]
+        + [shape((experts, tok_rows), kind) for kind in (jnp.int32, F32)]
+        + [shape(tokens.shape, BF16)],
         replica_plan, expert_ids.T, gate_weights.T, tokens,
         specs=[HBM] * 4,
         scratch=[
             pltpu.SMEM((owners,), jnp.int32),
             pltpu.VMEM((choices, tok_rows), jnp.int32),
             pltpu.VMEM((choices, tok_rows), F32),
-            pltpu.VMEM((tok_rows, share), BF16),
-            pltpu.VMEM((owners * owned, tok_rows), jnp.int32),
-            pltpu.VMEM((owners * owned, tok_rows), F32),
             pltpu.SemaphoreType.DMA((4,)),
         ],
         flops=10**10,
     )
+    *others, mixtures = call(
+        functools.partial(rest_kernel, owned, low, rest_steps, high_steps),
+        [piece] * len(rest_steps) + [shape((chunks, 2, lines, tok_rows), BF16)],
+        place, weight, tokens_here,
+    )
+    pieces += others
     arrived = {k: swapped(p, "expert", k * low) if k else p for k, p in zip(high_steps, pieces)}
 
     top = parts // 2
@@ -280,17 +300,17 @@
         here += [turned(value, m, 0) if m else value for m, value in enumerate(lots)]
         rows += [(k, m) for m in range(low) for k in group]
     moves = [(n, b) for n, value in enumerate(here) for b in range(value.shape[0] // CAP)]
-    here, there = (
+    there, here = (
         call(functools.partial(regroup_kernel, len(lots), [moves]), [whole], *lots)[0]
-        for lots in (here, there)
-    )
-    blocks = {0: here, top: there}
+        for lots in (there, here)
+    )
+    blocks = {top: there, 0: here}
     mask = top // 2
     while mask:
         for n in list(blocks):
             blocks[n ^ mask] = swapped(blocks[n], "dp", mask)
         mask //= 2
-    first = list(range(top + 1))
+    first = [0, *range(top, parts)]
     second = [n for n in range(parts) if n not in first]
     sums = [shape((chunks * lines, hidden_share), F32)] * 2
     gate_sum, up_sum = call(

time: 47 us -> 46.8 us (level)
    pallas_call x14 -> x15, Pallas kernels: 5.6 us -> 5.81 us  [call(): pl.pallas_call(kernel, out_shape=outs, in_specs=specs or [VMEM] * len(arg...]
  transfers between devices with their start and end apart: 22 -> 22, of which waited for: 10 -> 12; matrix products, arithmetic and copies ran while one was open for 0% -> 0% of each run, Pallas kernels for 5% -> 6%
where the time goes in v8:
time: 46.8 us; the launch traced here: 46.7 us
  starting transfers between devices  26.7 us (57%)
  waiting for transfers between devices  14 us (30%)
  Pallas kernels  5.81 us (12%)
    ppermute x22, starting transfers between devices, swapped(): lax.ppermute(value, axis, [(source, source ^ mask) for source in range(co...  26.7 us
    ppermute x22, waiting for transfers between devices, swapped(): lax.ppermute(value, axis, [(source, source ^ mask) for source in range(co...  14 us
    pallas_call x15, Pallas kernels, call(): pl.pallas_call(kernel, out_shape=outs, in_specs=specs or [VMEM] * len(arg...  5.81 us
  transfers between devices with their start and end apart: 22, of which 12 were waited for; matrix products, arithmetic and copies ran while one was open for 0% of the time, Pallas kernels for 6%

profile of v8, /device:TPU:0, one launch (start us, length us, event | category | flops | bytes accessed | tf_op | source)
XLA Modules:
  0.0 46.7 jit_solution(15853588532373775782)
XLA Ops:
  0.0 1.4 %shard_map.73 = (bf16[16,2688]{1,0:T(8,128)(2,1)S(1)}, bf16[16,2688]{1,0:T(8,128)(2,1)S(1)}, s32[8,128]{1,0:T(8,128)S(1)}, s32[16,128]{1,0:T(8,128)S(1)}, f32[16...) custom-call(s32[8]{0:T(128)} %plan_hbm.1, s32[8,128]{1,0:T(8,128)} %bitcast.2, f32[8,128]{1,0:T(8,128)} %bitcast.3, ...), custom_call_target="tpu_custom_call" | custom-call | flops 10000001024 | bytes 1000 | tf_op jit(solution)/shard_map/pallas_call | solution.py:218
  1.4 5.1 %collective-permute-start = (bf16[16,2688]{1,0:T(8,128)(2,1)S(1)}, bf16[16,2688]{1,0:T(8,128)(2,1)S(1)}, u32[]{:S(2)}, u32[]{:S(2)}) collective-permute-start(bf16[16,2688]{1,0:T(8,128)(2,1)S(1)} %get-tuple-element.41), channel_id=1, source_target_pairs={{0,24},{4,28},{8,16},{12,20},{16,8},{20,12},{24,0},{28,4},{1,25},{... | collective-permute-start | bytes 258056 | tf_op jit(solution)/shard_map/ppermute | solution.py:231
  7.5 2.3 %collective-permute-done.refs_0_ = bf16[16,2688]{1,0:T(8,128)(2,1)S(1)} collective-permute-done((bf16[16,2688]{1,0:T(8,128)(2,1)S(1)}, bf16[16,2688]{1,0:T(8,128)(2,1)S(1)}, u32[]{:S(2)}, u32[]{:S(2)}) %collective-permute-start) | collective-permute-done | bytes 86048 | tf_op jit(solution)/shard_map/ppermute | solution.py:231
  9.8 1.7 %collective-permute-start.5 = (bf16[16,2688]{1,0:T(8,128)(2,1)S(1)}, bf16[16,2688]{1,0:T(8,128)(2,1)S(1)}, u32[]{:S(2)}, u32[]{:S(2)}) collective-permute-start(bf16[16,2688]{1,0:T(8,128)(2,1)S(1)} %get-tuple-element.43.refs_0_), channel_id=1, source_target_pairs={{0,2},{1,3},{2,0},{3,1},{4,6},{5,7},{6,4},{7,5},{8,10},{9,11},{10,... | collective-permute-start | bytes 258056 | tf_op jit(solution)/shard_map/ppermute | solution.py:231
  11.5 1.5 %collective-permute-start.6 = (bf16[16,2688]{1,0:T(8,128)(2,1)S(1)}, bf16[16,2688]{1,0:T(8,128)(2,1)S(1)}, u32[]{:S(2)}, u32[]{:S(2)}) collective-permute-start(bf16[16,2688]{1,0:T(8,128)(2,1)S(1)} %get-tuple-element.44), channel_id=1, source_target_pairs={{0,6},{1,7},{2,4},{3,5},{4,2},{5,3},{6,0},{7,1},{8,14},{9,15},{10,... | collective-permute-start | bytes 258056 | tf_op jit(solution)/shard_map/ppermute | solution.py:231
  13.8 1.6 %collective-permute-start.7 = (bf16[16,2688]{1,0:T(8,128)(2,1)S(1)}, bf16[16,2688]{1,0:T(8,128)(2,1)S(1)}, u32[]{:S(2)}, u32[]{:S(2)}) collective-permute-start(bf16[16,2688]{1,0:T(8,128)(2,1)S(1)} %get-tuple-element.47.refs_2_), channel_id=1, source_target_pairs={{0,2},{1,3},{2,0},{3,1},{4,6},{5,7},{6,4},{7,5},{8,10},{9,11},{10,... | collective-permute-start | bytes 258056 | tf_op jit(solution)/shard_map/ppermute | solution.py:231
  15.3 1.5 %collective-permute-start.8 = (bf16[16,2688]{1,0:T(8,128)(2,1)S(1)}, bf16[16,2688]{1,0:T(8,128)(2,1)S(1)}, u32[]{:S(2)}, u32[]{:S(2)}) collective-permute-start(bf16[16,2688]{1,0:T(8,128)(2,1)S(1)} %get-tuple-element.48), channel_id=1, source_target_pairs={{0,6},{1,7},{2,4},{3,5},{4,2},{5,3},{6,0},{7,1},{8,14},{9,15},{10,... | collective-permute-start | bytes 258056 | tf_op jit(solution)/shard_map/ppermute | solution.py:231
  17.3 1.5 %collective-permute-start.4 = (bf16[16,2688]{1,0:T(8,128)(2,1)S(1)}, bf16[16,2688]{1,0:T(8,128)(2,1)S(1)}, u32[]{:S(2)}, u32[]{:S(2)}) collective-permute-start(bf16[16,2688]{1,0:T(8,128)(2,1)S(1)} %get-tuple-element.48), channel_id=1, source_target_pairs={{0,4},{4,0},{8,12},{12,8},{16,20},{20,16},{24,28},{28,24},{1,5},{5... | collective-permute-start | bytes 258056 | tf_op jit(solution)/shard_map/ppermute | solution.py:231
  18.8 2.0 %collective-permute-done.8.refs_3_ = bf16[16,2688]{1,0:T(8,128)(2,1)S(1)} collective-permute-done((bf16[16,2688]{1,0:T(8,128)(2,1)S(1)}, bf16[16,2688]{1,0:T(8,128)(2,1)S(1)}, u32[]{:S(2)}, u32[]{:S(2)}) %collective-permute-start.8) | collective-permute-done | bytes 86048 | tf_op jit(solution)/shard_map/ppermute | solution.py:231
  20.9 1.5 %collective-permute-done.1.refs_1_ = bf16[16,2688]{1,0:T(8,128)(2,1)S(1)} collective-permute-done((bf16[16,2688]{1,0:T(8,128)(2,1)S(1)}, bf16[16,2688]{1,0:T(8,128)(2,1)S(1)}, u32[]{:S(2)}, u32[]{:S(2)}) %collective-permute-start.1) | collective-permute-done | bytes 86048 | tf_op jit(solution)/shard_map/ppermute | solution.py:231
  22.4 0.9 %collective-permute-done.4.refs_3_ = bf16[16,2688]{1,0:T(8,128)(2,1)S(1)} collective-permute-done((bf16[16,2688]{1,0:T(8,128)(2,1)S(1)}, bf16[16,2688]{1,0:T(8,128)(2,1)S(1)}, u32[]{:S(2)}, u32[]{:S(2)}) %collective-permute-start.4) | collective-permute-done | bytes 86048 | tf_op jit(solution)/shard_map/ppermute | solution.py:231
  23.5 1.1 %shard_map.79 = (f32[192,256]{1,0:T(8,128)S(1)}, f32[192,256]{1,0:T(8,128)S(1)}) custom-call(s32[8,128]{1,0:T(8,128)S(1)} %get-tuple-element.40.info, bf16[2,3584,256]{2,1,0:T(8,128)(2,1)S(1)} %copy-done.1, bf16[2,3584,256]{2,1,0:T(8,128)(2,1)S(1)} %copy-done.2, bf16[2,256,3584]{2,1,0:T(8,128)(2,1)S(1)} %copy-done, bf16[64,2688]{1,0:T(8,128)(2,1)S(1)} %shard_map.77.refs_0_, ...), custom_call_target="tpu_custom_call" | custom-call | flops 1000 | bytes 1000 | tf_op jit(solution)/shard_map/pallas_call | solution.py:218
  27.6 1.3 %collective-permute-start.13 = (bf16[16,2688]{1,0:T(8,128)(2,1)S(1)}, bf16[16,2688]{1,0:T(8,128)(2,1)S(1)}, u32[]{:S(2)}, u32[]{:S(2)}) collective-permute-start(bf16[16,2688]{1,0:T(8,128)(2,1)S(1)} %get-tuple-element.56), channel_id=1, source_target_pairs={{0,2},{1,3},{2,0},{3,1},{4,6},{5,7},{6,4},{7,5},{8,10},{9,11},{10,... | collective-permute-start | bytes 258056 | tf_op jit(solution)/shard_map/ppermute | solution.py:231
  29.1 0.9 %collective-permute-start.14 = (bf16[16,2688]{1,0:T(8,128)(2,1)S(1)}, bf16[16,2688]{1,0:T(8,128)(2,1)S(1)}, u32[]{:S(2)}, u32[]{:S(2)}) collective-permute-start(bf16[16,2688]{1,0:T(8,128)(2,1)S(1)} %get-tuple-element.57), channel_id=1, source_target_pairs={{0,4},{4,0},{8,12},{12,8},{16,20},{20,16},{24,28},{28,24},{1,5},{5... | collective-permute-start | bytes 258056 | tf_op jit(solution)/shard_map/ppermute | solution.py:231
  30.0 1.4 %collective-permute-start.15 = (bf16[16,2688]{1,0:T(8,128)(2,1)S(1)}, bf16[16,2688]{1,0:T(8,128)(2,1)S(1)}, u32[]{:S(2)}, u32[]{:S(2)}) collective-permute-start(bf16[16,2688]{1,0:T(8,128)(2,1)S(1)} %get-tuple-element.58), channel_id=1, source_target_pairs={{0,6},{1,7},{2,4},{3,5},{4,2},{5,3},{6,0},{7,1},{8,14},{9,15},{10,... | collective-permute-start | bytes 258056 | tf_op jit(solution)/shard_map/ppermute | solution.py:231
  31.4 1.3 %collective-permute-start.18 = (bf16[16,2688]{1,0:T(8,128)(2,1)S(1)}, bf16[16,2688]{1,0:T(8,128)(2,1)S(1)}, u32[]{:S(2)}, u32[]{:S(2)}) collective-permute-start(bf16[16,2688]{1,0:T(8,128)(2,1)S(1)} %get-tuple-element.62), channel_id=1, source_target_pairs={{0,2},{1,3},{2,0},{3,1},{4,6},{5,7},{6,4},{7,5},{8,10},{9,11},{10,... | collective-permute-start | bytes 258056 | tf_op jit(solution)/shard_map/ppermute | solution.py:231
  32.7 0.8 %collective-permute-start.19 = (bf16[16,2688]{1,0:T(8,128)(2,1)S(1)}, bf16[16,2688]{1,0:T(8,128)(2,1)S(1)}, u32[]{:S(2)}, u32[]{:S(2)}) collective-permute-start(bf16[16,2688]{1,0:T(8,128)(2,1)S(1)} %get-tuple-element.63), channel_id=1, source_target_pairs={{0,4},{4,0},{8,12},{12,8},{16,20},{20,16},{24,28},{28,24},{1,5},{5... | collective-permute-start | bytes 258056 | tf_op jit(solution)/shard_map/ppermute | solution.py:231
  33.5 1.4 %collective-permute-start.20 = (bf16[16,2688]{1,0:T(8,128)(2,1)S(1)}, bf16[16,2688]{1,0:T(8,128)(2,1)S(1)}, u32[]{:S(2)}, u32[]{:S(2)}) collective-permute-start(bf16[16,2688]{1,0:T(8,128)(2,1)S(1)} %get-tuple-element.64), channel_id=1, source_target_pairs={{0,6},{1,7},{2,4},{3,5},{4,2},{5,3},{6,0},{7,1},{8,14},{9,15},{10,... | collective-permute-start | bytes 258056 | tf_op jit(solution)/shard_map/ppermute | solution.py:231
  35.2 0.9 %collective-permute-done.15.refs_3_ = bf16[16,2688]{1,0:T(8,128)(2,1)S(1)} collective-permute-done((bf16[16,2688]{1,0:T(8,128)(2,1)S(1)}, bf16[16,2688]{1,0:T(8,128)(2,1)S(1)}, u32[]{:S(2)}, u32[]{:S(2)}) %collective-permute-start.15) | collective-permute-done | bytes 86048 | tf_op jit(solution)/shard_map/ppermute | solution.py:231
  36.1 3.4 %collective-permute-start.16 = (bf16[16,2688]{1,0:T(8,128)(2,1)S(1)}, bf16[16,2688]{1,0:T(8,128)(2,1)S(1)}, u32[]{:S(2)}, u32[]{:S(2)}) collective-permute-start(bf16[16,2688]{1,0:T(8,128)(2,1)S(1)} %get-tuple-element.59), channel_id=1, source_target_pairs={{0,24},{4,28},{8,16},{12,20},{16,8},{20,12},{24,0},{28,4},{1,25},{... | collective-permute-start | bytes 258056 | tf_op jit(solution)/shard_map/ppermute | solution.py:231
  39.6 1.3 %collective-permute-start.21 = (bf16[16,2688]{1,0:T(8,128)(2,1)S(1)}, bf16[16,2688]{1,0:T(8,128)(2,1)S(1)}, u32[]{:S(2)}, u32[]{:S(2)}) collective-permute-start(bf16[16,2688]{1,0:T(8,128)(2,1)S(1)} %get-tuple-element.65), channel_id=1, source_target_pairs={{0,8},{4,12},{8,0},{12,4},{16,24},{20,28},{24,16},{28,20},{1,9},{5... | collective-permute-start | bytes 258056 | tf_op jit(solution)/shard_map/ppermute | solution.py:231
  40.8 1.7 %collective-permute-done.16.refs_0_ = bf16[16,2688]{1,0:T(8,128)(2,1)S(1)} collective-permute-done((bf16[16,2688]{1,0:T(8,128)(2,1)S(1)}, bf16[16,2688]{1,0:T(8,128)(2,1)S(1)}, u32[]{:S(2)}, u32[]{:S(2)}) %collective-permute-start.16) | collective-permute-done | bytes 86048 | tf_op jit(solution)/shard_map/ppermute | solution.py:231
  42.6 2.9 %collective-permute-done.17.refs_1_ = bf16[16,2688]{1,0:T(8,128)(2,1)S(1)} collective-permute-done((bf16[16,2688]{1,0:T(8,128)(2,1)S(1)}, bf16[16,2688]{1,0:T(8,128)(2,1)S(1)}, u32[]{:S(2)}, u32[]{:S(2)}) %collective-permute-start.17) | collective-permute-done | bytes 86048 | tf_op jit(solution)/shard_map/ppermute | solution.py:231
  45.7 1.0 %shard_map.87 = bf16[128,896]{1,0:T(8,128)(2,1)} custom-call(bf16[3,2,64,128]{3,2,1,0:T(8,128)(2,1)S(1)} %get-tuple-element.39.mixtures, bf16[16,2688]{1,0:T(8,128)(2,1)S(1)} %collective-permute-done.16.refs_0_, bf16[16,2688]{1,0:T(8,128)(2,1)S(1)} %collective-permute-done.17.refs_1_, bf16[16,2688]{1,0:T(8,128)(2,1)S(1)} %collective-permute-done.21.refs_2_, ...), custom_call_target="tpu_custom_call" | custom-call | flops 1000 | bytes 1000 | tf_op jit(solution)/shard_map/pallas_call | solution.py:218
  (41 shorter events, 6.1 us)
Async XLA Ops:
  0.0 23.5 %copy-start.1 = (bf16[2,3584,256]{2,1,0:T(8,128)(2,1)S(1)}, bf16[2,3584,256]{2,1,0:T(8,128)(2,1)}, u32[]{:S(2)}) copy-start(bf16[2,3584,256]{2,1,0:T(8,128)(2,1)} %gate.3) | copy-start | bytes 11010052
  0.0 23.5 %copy-start.2 = (bf16[2,3584,256]{2,1,0:T(8,128)(2,1)S(1)}, bf16[2,3584,256]{2,1,0:T(8,128)(2,1)}, u32[]{:S(2)}) copy-start(bf16[2,3584,256]{2,1,0:T(8,128)(2,1)} %up.3) | copy-start | bytes 11010052
  1.4 8.3 %collective-permute-start = (bf16[16,2688]{1,0:T(8,128)(2,1)S(1)}, bf16[16,2688]{1,0:T(8,128)(2,1)S(1)}, u32[]{:S(2)}, u32[]{:S(2)}) collective-permute-start(bf16[16,2688]{1,0:T(8,128)(2,1)S(1)} %get-tuple-element.41), channel_id=1, source_target_pairs={{0,24},{4,28},{8,16},{12,20},{16,8},{20,12},{24,0},{28,4},{1,25},{... | collective-permute-start | bytes 258056 | tf_op jit(solution)/shard_map/ppermute | solution.py:231
  6.5 7.2 %collective-permute-start.2 = (bf16[16,2688]{1,0:T(8,128)(2,1)S(1)}, bf16[16,2688]{1,0:T(8,128)(2,1)S(1)}, u32[]{:S(2)}, u32[]{:S(2)}) collective-permute-start(bf16[16,2688]{1,0:T(8,128)(2,1)S(1)} %get-tuple-element.45), channel_id=1, source_target_pairs={{0,16},{4,20},{8,24},{12,28},{16,0},{20,4},{24,8},{28,12},{1,17},{... | collective-permute-start | bytes 258056 | tf_op jit(solution)/shard_map/ppermute | solution.py:231
  6.7 7.0 %collective-permute-start.3 = (bf16[16,2688]{1,0:T(8,128)(2,1)S(1)}, bf16[16,2688]{1,0:T(8,128)(2,1)S(1)}, u32[]{:S(2)}, u32[]{:S(2)}) collective-permute-start(bf16[16,2688]{1,0:T(8,128)(2,1)S(1)} %get-tuple-element.46), channel_id=1, source_target_pairs={{0,8},{4,12},{8,0},{12,4},{16,24},{20,28},{24,16},{28,20},{1,9},{5... | collective-permute-start | bytes 258056 | tf_op jit(solution)/shard_map/ppermute | solution.py:231
  9.8 7.5 %collective-permute-start.5 = (bf16[16,2688]{1,0:T(8,128)(2,1)S(1)}, bf16[16,2688]{1,0:T(8,128)(2,1)S(1)}, u32[]{:S(2)}, u32[]{:S(2)}) collective-permute-start(bf16[16,2688]{1,0:T(8,128)(2,1)S(1)} %get-tuple-element.43.refs_0_), channel_id=1, source_target_pairs={{0,2},{1,3},{2,0},{3,1},{4,6},{5,7},{6,4},{7,5},{8,10},{9,11},{10,... | collective-permute-start | bytes 258056 | tf_op jit(solution)/shard_map/ppermute | solution.py:231
  11.5 7.4 %collective-permute-start.6 = (bf16[16,2688]{1,0:T(8,128)(2,1)S(1)}, bf16[16,2688]{1,0:T(8,128)(2,1)S(1)}, u32[]{:S(2)}, u32[]{:S(2)}) collective-permute-start(bf16[16,2688]{1,0:T(8,128)(2,1)S(1)} %get-tuple-element.44), channel_id=1, source_target_pairs={{0,6},{1,7},{2,4},{3,5},{4,2},{5,3},{6,0},{7,1},{8,14},{9,15},{10,... | collective-permute-start | bytes 258056 | tf_op jit(solution)/shard_map/ppermute | solution.py:231
  13.8 5.1 %collective-permute-start.7 = (bf16[16,2688]{1,0:T(8,128)(2,1)S(1)}, bf16[16,2688]{1,0:T(8,128)(2,1)S(1)}, u32[]{:S(2)}, u32[]{:S(2)}) collective-permute-start(bf16[16,2688]{1,0:T(8,128)(2,1)S(1)} %get-tuple-element.47.refs_2_), channel_id=1, source_target_pairs={{0,2},{1,3},{2,0},{3,1},{4,6},{5,7},{6,4},{7,5},{8,10},{9,11},{10,... | collective-permute-start | bytes 258056 | tf_op jit(solution)/shard_map/ppermute | solution.py:231
  15.3 5.5 %collective-permute-start.8 = (bf16[16,2688]{1,0:T(8,128)(2,1)S(1)}, bf16[16,2688]{1,0:T(8,128)(2,1)S(1)}, u32[]{:S(2)}, u32[]{:S(2)}) collective-permute-start(bf16[16,2688]{1,0:T(8,128)(2,1)S(1)} %get-tuple-element.48), channel_id=1, source_target_pairs={{0,6},{1,7},{2,4},{3,5},{4,2},{5,3},{6,0},{7,1},{8,14},{9,15},{10,... | collective-permute-start | bytes 258056 | tf_op jit(solution)/shard_map/ppermute | solution.py:231
  16.8 5.6 %collective-permute-start.1 = (bf16[16,2688]{1,0:T(8,128)(2,1)S(1)}, bf16[16,2688]{1,0:T(8,128)(2,1)S(1)}, u32[]{:S(2)}, u32[]{:S(2)}) collective-permute-start(bf16[16,2688]{1,0:T(8,128)(2,1)S(1)} %get-tuple-element.44), channel_id=1, source_target_pairs={{0,4},{4,0},{8,12},{12,8},{16,20},{20,16},{24,28},{28,24},{1,5},{5... | collective-permute-start | bytes 258056 | tf_op jit(solution)/shard_map/ppermute | solution.py:231
  17.3 6.1 %collective-permute-start.4 = (bf16[16,2688]{1,0:T(8,128)(2,1)S(1)}, bf16[16,2688]{1,0:T(8,128)(2,1)S(1)}, u32[]{:S(2)}, u32[]{:S(2)}) collective-permute-start(bf16[16,2688]{1,0:T(8,128)(2,1)S(1)} %get-tuple-element.48), channel_id=1, source_target_pairs={{0,4},{4,0},{8,12},{12,8},{16,20},{20,16},{24,28},{28,24},{1,5},{5... | collective-permute-start | bytes 258056 | tf_op jit(solution)/shard_map/ppermute | solution.py:231
  20.8 2.6 %collective-permute-start.9 = (bf16[64,2688]{1,0:T(8,128)(2,1)S(1)}, bf16[64,2688]{1,0:T(8,128)(2,1)S(1)}, u32[]{:S(2)}, u32[]{:S(2)}) collective-permute-start(bf16[64,2688]{1,0:T(8,128)(2,1)S(1)} %shard_map.78.refs_1_), channel_id=1, source_target_pairs={{0,1},{1,0},{2,3},{3,2},{4,5},{5,4},{6,7},{7,6},{8,9},{9,8},{10,11... | collective-permute-start | bytes 1032200 | tf_op jit(solution)/shard_map/ppermute | solution.py:231
  23.4 1.7 %collective-permute-start.10 = (bf16[64,2688]{1,0:T(8,128)(2,1)S(1)}, bf16[64,2688]{1,0:T(8,128)(2,1)S(1)}, u32[]{:S(2)}, u32[]{:S(2)}) collective-permute-start(bf16[64,2688]{1,0:T(8,128)(2,1)S(1)} %shard_map.77.refs_0_), channel_id=1, source_target_pairs={{0,1},{1,0},{2,3},{3,2},{4,5},{5,4},{6,7},{7,6},{8,9},{9,8},{10,11... | collective-permute-start | bytes 1032200 | tf_op jit(solution)/shard_map/ppermute | solution.py:231
  25.9 1.7 %collective-permute-start.12 = (bf16[64,2688]{1,0:T(8,128)(2,1)S(1)}, bf16[64,2688]{1,0:T(8,128)(2,1)S(1)}, u32[]{:S(2)}, u32[]{:S(2)}) collective-permute-start(bf16[64,2688]{1,0:T(8,128)(2,1)S(1)} %get-tuple-element.54), channel_id=1, source_target_pairs={{0,1},{1,0},{2,3},{3,2},{4,5},{5,4},{6,7},{7,6},{8,9},{9,8},{10,11... | collective-permute-start | bytes 1032200 | tf_op jit(solution)/shard_map/ppermute | solution.py:231
  26.6 2.3 %collective-permute-start.11 = (bf16[64,2688]{1,0:T(8,128)(2,1)S(1)}, bf16[64,2688]{1,0:T(8,128)(2,1)S(1)}, u32[]{:S(2)}, u32[]{:S(2)}) collective-permute-start(bf16[64,2688]{1,0:T(8,128)(2,1)S(1)} %get-tuple-element.53), channel_id=1, source_target_pairs={{0,1},{1,0},{2,3},{3,2},{4,5},{5,4},{6,7},{7,6},{8,9},{9,8},{10,11... | collective-permute-start | bytes 1032200 | tf_op jit(solution)/shard_map/ppermute | solution.py:231
  27.6 5.8 %collective-permute-start.13 = (bf16[16,2688]{1,0:T(8,128)(2,1)S(1)}, bf16[16,2688]{1,0:T(8,128)(2,1)S(1)}, u32[]{:S(2)}, u32[]{:S(2)}) collective-permute-start(bf16[16,2688]{1,0:T(8,128)(2,1)S(1)} %get-tuple-element.56), channel_id=1, source_target_pairs={{0,2},{1,3},{2,0},{3,1},{4,6},{5,7},{6,4},{7,5},{8,10},{9,11},{10,... | collective-permute-start | bytes 258056 | tf_op jit(solution)/shard_map/ppermute | solution.py:231
  29.1 6.1 %collective-permute-start.14 = (bf16[16,2688]{1,0:T(8,128)(2,1)S(1)}, bf16[16,2688]{1,0:T(8,128)(2,1)S(1)}, u32[]{:S(2)}, u32[]{:S(2)}) collective-permute-start(bf16[16,2688]{1,0:T(8,128)(2,1)S(1)} %get-tuple-element.57), channel_id=1, source_target_pairs={{0,4},{4,0},{8,12},{12,8},{16,20},{20,16},{24,28},{28,24},{1,5},{5... | collective-permute-start | bytes 258056 | tf_op jit(solution)/shard_map/ppermute | solution.py:231
  30.0 6.1 %collective-permute-start.15 = (bf16[16,2688]{1,0:T(8,128)(2,1)S(1)}, bf16[16,2688]{1,0:T(8,128)(2,1)S(1)}, u32[]{:S(2)}, u32[]{:S(2)}) collective-permute-start(bf16[16,2688]{1,0:T(8,128)(2,1)S(1)} %get-tuple-element.58), channel_id=1, source_target_pairs={{0,6},{1,7},{2,4},{3,5},{4,2},{5,3},{6,0},{7,1},{8,14},{9,15},{10,... | collective-permute-start | bytes 258056 | tf_op jit(solution)/shard_map/ppermute | solution.py:231
  31.4 8.1 %collective-permute-start.18 = (bf16[16,2688]{1,0:T(8,128)(2,1)S(1)}, bf16[16,2688]{1,0:T(8,128)(2,1)S(1)}, u32[]{:S(2)}, u32[]{:S(2)}) collective-permute-start(bf16[16,2688]{1,0:T(8,128)(2,1)S(1)} %get-tuple-element.62), channel_id=1, source_target_pairs={{0,2},{1,3},{2,0},{3,1},{4,6},{5,7},{6,4},{7,5},{8,10},{9,11},{10,... | collective-permute-start | bytes 258056 | tf_op jit(solution)/shard_map/ppermute | solution.py:231
  32.7 6.8 %collective-permute-start.19 = (bf16[16,2688]{1,0:T(8,128)(2,1)S(1)}, bf16[16,2688]{1,0:T(8,128)(2,1)S(1)}, u32[]{:S(2)}, u32[]{:S(2)}) collective-permute-start(bf16[16,2688]{1,0:T(8,128)(2,1)S(1)} %get-tuple-element.63), channel_id=1, source_target_pairs={{0,4},{4,0},{8,12},{12,8},{16,20},{20,16},{24,28},{28,24},{1,5},{5... | collective-permute-start | bytes 258056 | tf_op jit(solution)/shard_map/ppermute | solution.py:231
  33.5 6.0 %collective-permute-start.20 = (bf16[16,2688]{1,0:T(8,128)(2,1)S(1)}, bf16[16,2688]{1,0:T(8,128)(2,1)S(1)}, u32[]{:S(2)}, u32[]{:S(2)}) collective-permute-start(bf16[16,2688]{1,0:T(8,128)(2,1)S(1)} %get-tuple-element.64), channel_id=1, source_target_pairs={{0,6},{1,7},{2,4},{3,5},{4,2},{5,3},{6,0},{7,1},{8,14},{9,15},{10,... | collective-permute-start | bytes 258056 | tf_op jit(solution)/shard_map/ppermute | solution.py:231
  36.1 6.5 %collective-permute-start.16 = (bf16[16,2688]{1,0:T(8,128)(2,1)S(1)}, bf16[16,2688]{1,0:T(8,128)(2,1)S(1)}, u32[]{:S(2)}, u32[]{:S(2)}) collective-permute-start(bf16[16,2688]{1,0:T(8,128)(2,1)S(1)} %get-tuple-element.59), channel_id=1, source_target_pairs={{0,24},{4,28},{8,16},{12,20},{16,8},{20,12},{24,0},{28,4},{1,25},{... | collective-permute-start | bytes 258056 | tf_op jit(solution)/shard_map/ppermute | solution.py:231
  39.5 6.0 %collective-permute-start.17 = (bf16[16,2688]{1,0:T(8,128)(2,1)S(1)}, bf16[16,2688]{1,0:T(8,128)(2,1)S(1)}, u32[]{:S(2)}, u32[]{:S(2)}) collective-permute-start(bf16[16,2688]{1,0:T(8,128)(2,1)S(1)} %get-tuple-element.60), channel_id=1, source_target_pairs={{0,16},{4,20},{8,24},{12,28},{16,0},{20,4},{24,8},{28,12},{1,17},{... | collective-permute-start | bytes 258056 | tf_op jit(solution)/shard_map/ppermute | solution.py:231
  39.6 6.1 %collective-permute-start.21 = (bf16[16,2688]{1,0:T(8,128)(2,1)S(1)}, bf16[16,2688]{1,0:T(8,128)(2,1)S(1)}, u32[]{:S(2)}, u32[]{:S(2)}) collective-permute-start(bf16[16,2688]{1,0:T(8,128)(2,1)S(1)} %get-tuple-element.65), channel_id=1, source_target_pairs={{0,8},{4,12},{8,0},{12,4},{16,24},{20,28},{24,16},{28,20},{1,9},{5... | collective-permute-start | bytes 258056 | tf_op jit(solution)/shard_map/ppermute | solution.py:231
  (1 other events, 23.5 us)

commit v9 on v8

--- a/solution.py
+++ b/solution.py
@@ -28,17 +28,19 @@
     own_index = lax.axis_index("expert")
     slot = lax.broadcasted_iota(jnp.int32, (CAP, tok_rows), 0)
     size = low * CAP
+    picks = []
     for chunk in range(owned + 1):
-        picks = []
         for k, m in [(k, m) for k in high_steps for m in range(low)]:
             pick = jnp.zeros((CAP, tok_rows), F32)
             for number in range(owned):
                 line = pl.ds((own_index ^ (k * low + m)) * owned + number, 1)
                 pick = pick + (place[line, :] == slot + chunk * CAP).astype(F32)
             picks.append(pick)
-        values = dot(jnp.concatenate(picks, axis=0).astype(BF16), tokens[...]).astype(BF16)
+    values = dot(jnp.concatenate(picks, axis=0).astype(BF16), tokens[...]).astype(BF16)
+    for chunk in range(owned + 1):
         for n, piece in enumerate(pieces):
-            piece[:, chunk * share : (chunk + 1) * share] = values[n * size : (n + 1) * size]
+            begin = (chunk * len(pieces) + n) * size
+            piece[:, chunk * share : (chunk + 1) * share] = values[begin : begin + size]
 
 
 def route_kernel(owned, low, high_steps, plan_hbm, ids_hbm, gates_hbm, tokens_hbm, *refs):

time: 46.8 us -> 46.8 us (level)
  no operation moved by 1% of the time
where the time goes in v9:
time: 46.8 us; the launch traced here: 46.7 us
  starting transfers between devices  26.7 us (57%)
  waiting for transfers between devices  14.1 us (30%)
  Pallas kernels  5.75 us (12%)
    ppermute x22, starting transfers between devices, swapped(): lax.ppermute(value, axis, [(source, source ^ mask) for source in range(co...  26.7 us
    ppermute x22, waiting for transfers between devices, swapped(): lax.ppermute(value, axis, [(source, source ^ mask) for source in range(co...  14.1 us
    pallas_call x15, Pallas kernels, call(): pl.pallas_call(kernel, out_shape=outs, in_specs=specs or [VMEM] * len(arg...  5.75 us
  transfers between devices with their start and end apart: 22, of which 12 were waited for; matrix products, arithmetic and copies ran while one was open for 0% of the time, Pallas kernels for 6%

profile of v9, /device:TPU:0, one launch (start us, length us, event | category | flops | bytes accessed | tf_op | source)
XLA Modules:
  0.0 46.7 jit_solution(15639461119256186398)
XLA Ops:
  0.0 1.4 %shard_map.73 = (bf16[16,2688]{1,0:T(8,128)(2,1)S(1)}, bf16[16,2688]{1,0:T(8,128)(2,1)S(1)}, s32[8,128]{1,0:T(8,128)S(1)}, s32[16,128]{1,0:T(8,128)S(1)}, f32[16...) custom-call(s32[8]{0:T(128)} %plan_hbm.1, s32[8,128]{1,0:T(8,128)} %bitcast.2, f32[8,128]{1,0:T(8,128)} %bitcast.3, ...), custom_call_target="tpu_custom_call" | custom-call | flops 10000001024 | bytes 1000 | tf_op jit(solution)/shard_map/pallas_call | solution.py:220
  1.4 5.1 %collective-permute-start = (bf16[16,2688]{1,0:T(8,128)(2,1)S(1)}, bf16[16,2688]{1,0:T(8,128)(2,1)S(1)}, u32[]{:S(2)}, u32[]{:S(2)}) collective-permute-start(bf16[16,2688]{1,0:T(8,128)(2,1)S(1)} %get-tuple-element.41), channel_id=1, source_target_pairs={{0,24},{4,28},{8,16},{12,20},{16,8},{20,12},{24,0},{28,4},{1,25},{... | collective-permute-start | bytes 258056 | tf_op jit(solution)/shard_map/ppermute | solution.py:233
  7.4 2.3 %collective-permute-done.refs_0_ = bf16[16,2688]{1,0:T(8,128)(2,1)S(1)} collective-permute-done((bf16[16,2688]{1,0:T(8,128)(2,1)S(1)}, bf16[16,2688]{1,0:T(8,128)(2,1)S(1)}, u32[]{:S(2)}, u32[]{:S(2)}) %collective-permute-start) | collective-permute-done | bytes 86048 | tf_op jit(solution)/shard_map/ppermute | solution.py:233
  9.7 1.7 %collective-permute-start.5 = (bf16[16,2688]{1,0:T(8,128)(2,1)S(1)}, bf16[16,2688]{1,0:T(8,128)(2,1)S(1)}, u32[]{:S(2)}, u32[]{:S(2)}) collective-permute-start(bf16[16,2688]{1,0:T(8,128)(2,1)S(1)} %get-tuple-element.43.refs_0_), channel_id=1, source_target_pairs={{0,2},{1,3},{2,0},{3,1},{4,6},{5,7},{6,4},{7,5},{8,10},{9,11},{10,... | collective-permute-start | bytes 258056 | tf_op jit(solution)/shard_map/ppermute | solution.py:233
  11.4 1.5 %collective-permute-start.6 = (bf16[16,2688]{1,0:T(8,128)(2,1)S(1)}, bf16[16,2688]{1,0:T(8,128)(2,1)S(1)}, u32[]{:S(2)}, u32[]{:S(2)}) collective-permute-start(bf16[16,2688]{1,0:T(8,128)(2,1)S(1)} %get-tuple-element.44), channel_id=1, source_target_pairs={{0,6},{1,7},{2,4},{3,5},{4,2},{5,3},{6,0},{7,1},{8,14},{9,15},{10,... | collective-permute-start | bytes 258056 | tf_op jit(solution)/shard_map/ppermute | solution.py:233
  13.7 1.6 %collective-permute-start.7 = (bf16[16,2688]{1,0:T(8,128)(2,1)S(1)}, bf16[16,2688]{1,0:T(8,128)(2,1)S(1)}, u32[]{:S(2)}, u32[]{:S(2)}) collective-permute-start(bf16[16,2688]{1,0:T(8,128)(2,1)S(1)} %get-tuple-element.47.refs_2_), channel_id=1, source_target_pairs={{0,2},{1,3},{2,0},{3,1},{4,6},{5,7},{6,4},{7,5},{8,10},{9,11},{10,... | collective-permute-start | bytes 258056 | tf_op jit(solution)/shard_map/ppermute | solution.py:233
  15.3 1.5 %collective-permute-start.8 = (bf16[16,2688]{1,0:T(8,128)(2,1)S(1)}, bf16[16,2688]{1,0:T(8,128)(2,1)S(1)}, u32[]{:S(2)}, u32[]{:S(2)}) collective-permute-start(bf16[16,2688]{1,0:T(8,128)(2,1)S(1)} %get-tuple-element.48), channel_id=1, source_target_pairs={{0,6},{1,7},{2,4},{3,5},{4,2},{5,3},{6,0},{7,1},{8,14},{9,15},{10,... | collective-permute-start | bytes 258056 | tf_op jit(solution)/shard_map/ppermute | solution.py:233
  17.3 1.5 %collective-permute-start.4 = (bf16[16,2688]{1,0:T(8,128)(2,1)S(1)}, bf16[16,2688]{1,0:T(8,128)(2,1)S(1)}, u32[]{:S(2)}, u32[]{:S(2)}) collective-permute-start(bf16[16,2688]{1,0:T(8,128)(2,1)S(1)} %get-tuple-element.48), channel_id=1, source_target_pairs={{0,4},{4,0},{8,12},{12,8},{16,20},{20,16},{24,28},{28,24},{1,5},{5... | collective-permute-start | bytes 258056 | tf_op jit(solution)/shard_map/ppermute | solution.py:233
  18.8 2.0 %collective-permute-done.8.refs_3_ = bf16[16,2688]{1,0:T(8,128)(2,1)S(1)} collective-permute-done((bf16[16,2688]{1,0:T(8,128)(2,1)S(1)}, bf16[16,2688]{1,0:T(8,128)(2,1)S(1)}, u32[]{:S(2)}, u32[]{:S(2)}) %collective-permute-start.8) | collective-permute-done | bytes 86048 | tf_op jit(solution)/shard_map/ppermute | solution.py:233
  20.9 1.5 %collective-permute-done.1.refs_1_ = bf16[16,2688]{1,0:T(8,128)(2,1)S(1)} collective-permute-done((bf16[16,2688]{1,0:T(8,128)(2,1)S(1)}, bf16[16,2688]{1,0:T(8,128)(2,1)S(1)}, u32[]{:S(2)}, u32[]{:S(2)}) %collective-permute-start.1) | collective-permute-done | bytes 86048 | tf_op jit(solution)/shard_map/ppermute | solution.py:233
  22.4 0.9 %collective-permute-done.4.refs_3_ = bf16[16,2688]{1,0:T(8,128)(2,1)S(1)} collective-permute-done((bf16[16,2688]{1,0:T(8,128)(2,1)S(1)}, bf16[16,2688]{1,0:T(8,128)(2,1)S(1)}, u32[]{:S(2)}, u32[]{:S(2)}) %collective-permute-start.4) | collective-permute-done | bytes 86048 | tf_op jit(solution)/shard_map/ppermute | solution.py:233
  23.5 1.2 %shard_map.79 = (f32[192,256]{1,0:T(8,128)S(1)}, f32[192,256]{1,0:T(8,128)S(1)}) custom-call(s32[8,128]{1,0:T(8,128)S(1)} %get-tuple-element.40.info, bf16[2,3584,256]{2,1,0:T(8,128)(2,1)S(1)} %copy-done.1, bf16[2,3584,256]{2,1,0:T(8,128)(2,1)S(1)} %copy-done.2, bf16[2,256,3584]{2,1,0:T(8,128)(2,1)S(1)} %copy-done, bf16[64,2688]{1,0:T(8,128)(2,1)S(1)} %shard_map.77.refs_0_, ...), custom_call_target="tpu_custom_call" | custom-call | flops 1000 | bytes 1000 | tf_op jit(solution)/shard_map/pallas_call | solution.py:220
  27.6 1.3 %collective-permute-start.13 = (bf16[16,2688]{1,0:T(8,128)(2,1)S(1)}, bf16[16,2688]{1,0:T(8,128)(2,1)S(1)}, u32[]{:S(2)}, u32[]{:S(2)}) collective-permute-start(bf16[16,2688]{1,0:T(8,128)(2,1)S(1)} %get-tuple-element.56), channel_id=1, source_target_pairs={{0,2},{1,3},{2,0},{3,1},{4,6},{5,7},{6,4},{7,5},{8,10},{9,11},{10,... | collective-permute-start | bytes 258056 | tf_op jit(solution)/shard_map/ppermute | solution.py:233
  29.1 0.9 %collective-permute-start.14 = (bf16[16,2688]{1,0:T(8,128)(2,1)S(1)}, bf16[16,2688]{1,0:T(8,128)(2,1)S(1)}, u32[]{:S(2)}, u32[]{:S(2)}) collective-permute-start(bf16[16,2688]{1,0:T(8,128)(2,1)S(1)} %get-tuple-element.57), channel_id=1, source_target_pairs={{0,4},{4,0},{8,12},{12,8},{16,20},{20,16},{24,28},{28,24},{1,5},{5... | collective-permute-start | bytes 258056 | tf_op jit(solution)/shard_map/ppermute | solution.py:233
  29.9 1.4 %collective-permute-start.15 = (bf16[16,2688]{1,0:T(8,128)(2,1)S(1)}, bf16[16,2688]{1,0:T(8,128)(2,1)S(1)}, u32[]{:S(2)}, u32[]{:S(2)}) collective-permute-start(bf16[16,2688]{1,0:T(8,128)(2,1)S(1)} %get-tuple-element.58), channel_id=1, source_target_pairs={{0,6},{1,7},{2,4},{3,5},{4,2},{5,3},{6,0},{7,1},{8,14},{9,15},{10,... | collective-permute-start | bytes 258056 | tf_op jit(solution)/shard_map/ppermute | solution.py:233
  31.4 1.3 %collective-permute-start.18 = (bf16[16,2688]{1,0:T(8,128)(2,1)S(1)}, bf16[16,2688]{1,0:T(8,128)(2,1)S(1)}, u32[]{:S(2)}, u32[]{:S(2)}) collective-permute-start(bf16[16,2688]{1,0:T(8,128)(2,1)S(1)} %get-tuple-element.62), channel_id=1, source_target_pairs={{0,2},{1,3},{2,0},{3,1},{4,6},{5,7},{6,4},{7,5},{8,10},{9,11},{10,... | collective-permute-start | bytes 258056 | tf_op jit(solution)/shard_map/ppermute | solution.py:233
  32.6 0.8 %collective-permute-start.19 = (bf16[16,2688]{1,0:T(8,128)(2,1)S(1)}, bf16[16,2688]{1,0:T(8,128)(2,1)S(1)}, u32[]{:S(2)}, u32[]{:S(2)}) collective-permute-start(bf16[16,2688]{1,0:T(8,128)(2,1)S(1)} %get-tuple-element.63), channel_id=1, source_target_pairs={{0,4},{4,0},{8,12},{12,8},{16,20},{20,16},{24,28},{28,24},{1,5},{5... | collective-permute-start | bytes 258056 | tf_op jit(solution)/shard_map/ppermute | solution.py:233
  33.4 1.4 %collective-permute-start.20 = (bf16[16,2688]{1,0:T(8,128)(2,1)S(1)}, bf16[16,2688]{1,0:T(8,128)(2,1)S(1)}, u32[]{:S(2)}, u32[]{:S(2)}) collective-permute-start(bf16[16,2688]{1,0:T(8,128)(2,1)S(1)} %get-tuple-element.64), channel_id=1, source_target_pairs={{0,6},{1,7},{2,4},{3,5},{4,2},{5,3},{6,0},{7,1},{8,14},{9,15},{10,... | collective-permute-start | bytes 258056 | tf_op jit(solution)/shard_map/ppermute | solution.py:233
  35.1 0.9 %collective-permute-done.15.refs_3_ = bf16[16,2688]{1,0:T(8,128)(2,1)S(1)} collective-permute-done((bf16[16,2688]{1,0:T(8,128)(2,1)S(1)}, bf16[16,2688]{1,0:T(8,128)(2,1)S(1)}, u32[]{:S(2)}, u32[]{:S(2)}) %collective-permute-start.15) | collective-permute-done | bytes 86048 | tf_op jit(solution)/shard_map/ppermute | solution.py:233
  36.1 3.4 %collective-permute-start.16 = (bf16[16,2688]{1,0:T(8,128)(2,1)S(1)}, bf16[16,2688]{1,0:T(8,128)(2,1)S(1)}, u32[]{:S(2)}, u32[]{:S(2)}) collective-permute-start(bf16[16,2688]{1,0:T(8,128)(2,1)S(1)} %get-tuple-element.59), channel_id=1, source_target_pairs={{0,24},{4,28},{8,16},{12,20},{16,8},{20,12},{24,0},{28,4},{1,25},{... | collective-permute-start | bytes 258056 | tf_op jit(solution)/shard_map/ppermute | solution.py:233
  39.5 1.3 %collective-permute-start.21 = (bf16[16,2688]{1,0:T(8,128)(2,1)S(1)}, bf16[16,2688]{1,0:T(8,128)(2,1)S(1)}, u32[]{:S(2)}, u32[]{:S(2)}) collective-permute-start(bf16[16,2688]{1,0:T(8,128)(2,1)S(1)} %get-tuple-element.65), channel_id=1, source_target_pairs={{0,8},{4,12},{8,0},{12,4},{16,24},{20,28},{24,16},{28,20},{1,9},{5... | collective-permute-start | bytes 258056 | tf_op jit(solution)/shard_map/ppermute | solution.py:233
  40.8 1.7 %collective-permute-done.16.refs_0_ = bf16[16,2688]{1,0:T(8,128)(2,1)S(1)} collective-permute-done((bf16[16,2688]{1,0:T(8,128)(2,1)S(1)}, bf16[16,2688]{1,0:T(8,128)(2,1)S(1)}, u32[]{:S(2)}, u32[]{:S(2)}) %collective-permute-start.16) | collective-permute-done | bytes 86048 | tf_op jit(solution)/shard_map/ppermute | solution.py:233
  42.6 2.9 %collective-permute-done.17.refs_1_ = bf16[16,2688]{1,0:T(8,128)(2,1)S(1)} collective-permute-done((bf16[16,2688]{1,0:T(8,128)(2,1)S(1)}, bf16[16,2688]{1,0:T(8,128)(2,1)S(1)}, u32[]{:S(2)}, u32[]{:S(2)}) %collective-permute-start.17) | collective-permute-done | bytes 86048 | tf_op jit(solution)/shard_map/ppermute | solution.py:233
  45.6 1.0 %shard_map.87 = bf16[128,896]{1,0:T(8,128)(2,1)} custom-call(bf16[3,2,64,128]{3,2,1,0:T(8,128)(2,1)S(1)} %get-tuple-element.39.mixtures, bf16[16,2688]{1,0:T(8,128)(2,1)S(1)} %collective-permute-done.16.refs_0_, bf16[16,2688]{1,0:T(8,128)(2,1)S(1)} %collective-permute-done.17.refs_1_, bf16[16,2688]{1,0:T(8,128)(2,1)S(1)} %collective-permute-done.21.refs_2_, ...), custom_call_target="tpu_custom_call" | custom-call | flops 1000 | bytes 1000 | tf_op jit(solution)/shard_map/pallas_call | solution.py:220
  (41 shorter events, 6.1 us)
Async XLA Ops:
  0.0 23.5 %copy-start.1 = (bf16[2,3584,256]{2,1,0:T(8,128)(2,1)S(1)}, bf16[2,3584,256]{2,1,0:T(8,128)(2,1)}, u32[]{:S(2)}) copy-start(bf16[2,3584,256]{2,1,0:T(8,128)(2,1)} %gate.3) | copy-start | bytes 11010052
  0.0 23.5 %copy-start.2 = (bf16[2,3584,256]{2,1,0:T(8,128)(2,1)S(1)}, bf16[2,3584,256]{2,1,0:T(8,128)(2,1)}, u32[]{:S(2)}) copy-start(bf16[2,3584,256]{2,1,0:T(8,128)(2,1)} %up.3) | copy-start | bytes 11010052
  1.4 8.3 %collective-permute-start = (bf16[16,2688]{1,0:T(8,128)(2,1)S(1)}, bf16[16,2688]{1,0:T(8,128)(2,1)S(1)}, u32[]{:S(2)}, u32[]{:S(2)}) collective-permute-start(bf16[16,2688]{1,0:T(8,128)(2,1)S(1)} %get-tuple-element.41), channel_id=1, source_target_pairs={{0,24},{4,28},{8,16},{12,20},{16,8},{20,12},{24,0},{28,4},{1,25},{... | collective-permute-start | bytes 258056 | tf_op jit(solution)/shard_map/ppermute | solution.py:233
  6.5 7.2 %collective-permute-start.2 = (bf16[16,2688]{1,0:T(8,128)(2,1)S(1)}, bf16[16,2688]{1,0:T(8,128)(2,1)S(1)}, u32[]{:S(2)}, u32[]{:S(2)}) collective-permute-start(bf16[16,2688]{1,0:T(8,128)(2,1)S(1)} %get-tuple-element.45), channel_id=1, source_target_pairs={{0,16},{4,20},{8,24},{12,28},{16,0},{20,4},{24,8},{28,12},{1,17},{... | collective-permute-start | bytes 258056 | tf_op jit(solution)/shard_map/ppermute | solution.py:233
  6.7 7.0 %collective-permute-start.3 = (bf16[16,2688]{1,0:T(8,128)(2,1)S(1)}, bf16[16,2688]{1,0:T(8,128)(2,1)S(1)}, u32[]{:S(2)}, u32[]{:S(2)}) collective-permute-start(bf16[16,2688]{1,0:T(8,128)(2,1)S(1)} %get-tuple-element.46), channel_id=1, source_target_pairs={{0,8},{4,12},{8,0},{12,4},{16,24},{20,28},{24,16},{28,20},{1,9},{5... | collective-permute-start | bytes 258056 | tf_op jit(solution)/shard_map/ppermute | solution.py:233
  9.7 7.5 %collective-permute-start.5 = (bf16[16,2688]{1,0:T(8,128)(2,1)S(1)}, bf16[16,2688]{1,0:T(8,128)(2,1)S(1)}, u32[]{:S(2)}, u32[]{:S(2)}) collective-permute-start(bf16[16,2688]{1,0:T(8,128)(2,1)S(1)} %get-tuple-element.43.refs_0_), channel_id=1, source_target_pairs={{0,2},{1,3},{2,0},{3,1},{4,6},{5,7},{6,4},{7,5},{8,10},{9,11},{10,... | collective-permute-start | bytes 258056 | tf_op jit(solution)/shard_map/ppermute | solution.py:233
  11.4 7.4 %collective-permute-start.6 = (bf16[16,2688]{1,0:T(8,128)(2,1)S(1)}, bf16[16,2688]{1,0:T(8,128)(2,1)S(1)}, u32[]{:S(2)}, u32[]{:S(2)}) collective-permute-start(bf16[16,2688]{1,0:T(8,128)(2,1)S(1)} %get-tuple-element.44), channel_id=1, source_target_pairs={{0,6},{1,7},{2,4},{3,5},{4,2},{5,3},{6,0},{7,1},{8,14},{9,15},{10,... | collective-permute-start | bytes 258056 | tf_op jit(solution)/shard_map/ppermute | solution.py:233
  13.7 5.1 %collective-permute-start.7 = (bf16[16,2688]{1,0:T(8,128)(2,1)S(1)}, bf16[16,2688]{1,0:T(8,128)(2,1)S(1)}, u32[]{:S(2)}, u32[]{:S(2)}) collective-permute-start(bf16[16,2688]{1,0:T(8,128)(2,1)S(1)} %get-tuple-element.47.refs_2_), channel_id=1, source_target_pairs={{0,2},{1,3},{2,0},{3,1},{4,6},{5,7},{6,4},{7,5},{8,10},{9,11},{10,... | collective-permute-start | bytes 258056 | tf_op jit(solution)/shard_map/ppermute | solution.py:233
  15.3 5.5 %collective-permute-start.8 = (bf16[16,2688]{1,0:T(8,128)(2,1)S(1)}, bf16[16,2688]{1,0:T(8,128)(2,1)S(1)}, u32[]{:S(2)}, u32[]{:S(2)}) collective-permute-start(bf16[16,2688]{1,0:T(8,128)(2,1)S(1)} %get-tuple-element.48), channel_id=1, source_target_pairs={{0,6},{1,7},{2,4},{3,5},{4,2},{5,3},{6,0},{7,1},{8,14},{9,15},{10,... | collective-permute-start | bytes 258056 | tf_op jit(solution)/shard_map/ppermute | solution.py:233
  16.8 5.6 %collective-permute-start.1 = (bf16[16,2688]{1,0:T(8,128)(2,1)S(1)}, bf16[16,2688]{1,0:T(8,128)(2,1)S(1)}, u32[]{:S(2)}, u32[]{:S(2)}) collective-permute-start(bf16[16,2688]{1,0:T(8,128)(2,1)S(1)} %get-tuple-element.44), channel_id=1, source_target_pairs={{0,4},{4,0},{8,12},{12,8},{16,20},{20,16},{24,28},{28,24},{1,5},{5... | collective-permute-start | bytes 258056 | tf_op jit(solution)/shard_map/ppermute | solution.py:233
  17.3 6.1 %collective-permute-start.4 = (bf16[16,2688]{1,0:T(8,128)(2,1)S(1)}, bf16[16,2688]{1,0:T(8,128)(2,1)S(1)}, u32[]{:S(2)}, u32[]{:S(2)}) collective-permute-start(bf16[16,2688]{1,0:T(8,128)(2,1)S(1)} %get-tuple-element.48), channel_id=1, source_target_pairs={{0,4},{4,0},{8,12},{12,8},{16,20},{20,16},{24,28},{28,24},{1,5},{5... | collective-permute-start | bytes 258056 | tf_op jit(solution)/shard_map/ppermute | solution.py:233
  20.8 2.7 %collective-permute-start.9 = (bf16[64,2688]{1,0:T(8,128)(2,1)S(1)}, bf16[64,2688]{1,0:T(8,128)(2,1)S(1)}, u32[]{:S(2)}, u32[]{:S(2)}) collective-permute-start(bf16[64,2688]{1,0:T(8,128)(2,1)S(1)} %shard_map.78.refs_1_), channel_id=1, source_target_pairs={{0,1},{1,0},{2,3},{3,2},{4,5},{5,4},{6,7},{7,6},{8,9},{9,8},{10,11... | collective-permute-start | bytes 1032200 | tf_op jit(solution)/shard_map/ppermute | solution.py:233
  23.4 1.7 %collective-permute-start.10 = (bf16[64,2688]{1,0:T(8,128)(2,1)S(1)}, bf16[64,2688]{1,0:T(8,128)(2,1)S(1)}, u32[]{:S(2)}, u32[]{:S(2)}) collective-permute-start(bf16[64,2688]{1,0:T(8,128)(2,1)S(1)} %shard_map.77.refs_0_), channel_id=1, source_target_pairs={{0,1},{1,0},{2,3},{3,2},{4,5},{5,4},{6,7},{7,6},{8,9},{9,8},{10,11... | collective-permute-start | bytes 1032200 | tf_op jit(solution)/shard_map/ppermute | solution.py:233
  25.8 1.7 %collective-permute-start.12 = (bf16[64,2688]{1,0:T(8,128)(2,1)S(1)}, bf16[64,2688]{1,0:T(8,128)(2,1)S(1)}, u32[]{:S(2)}, u32[]{:S(2)}) collective-permute-start(bf16[64,2688]{1,0:T(8,128)(2,1)S(1)} %get-tuple-element.54), channel_id=1, source_target_pairs={{0,1},{1,0},{2,3},{3,2},{4,5},{5,4},{6,7},{7,6},{8,9},{9,8},{10,11... | collective-permute-start | bytes 1032200 | tf_op jit(solution)/shard_map/ppermute | solution.py:233
  26.6 2.3 %collective-permute-start.11 = (bf16[64,2688]{1,0:T(8,128)(2,1)S(1)}, bf16[64,2688]{1,0:T(8,128)(2,1)S(1)}, u32[]{:S(2)}, u32[]{:S(2)}) collective-permute-start(bf16[64,2688]{1,0:T(8,128)(2,1)S(1)} %get-tuple-element.53), channel_id=1, source_target_pairs={{0,1},{1,0},{2,3},{3,2},{4,5},{5,4},{6,7},{7,6},{8,9},{9,8},{10,11... | collective-permute-start | bytes 1032200 | tf_op jit(solution)/shard_map/ppermute | solution.py:233
  27.6 5.8 %collective-permute-start.13 = (bf16[16,2688]{1,0:T(8,128)(2,1)S(1)}, bf16[16,2688]{1,0:T(8,128)(2,1)S(1)}, u32[]{:S(2)}, u32[]{:S(2)}) collective-permute-start(bf16[16,2688]{1,0:T(8,128)(2,1)S(1)} %get-tuple-element.56), channel_id=1, source_target_pairs={{0,2},{1,3},{2,0},{3,1},{4,6},{5,7},{6,4},{7,5},{8,10},{9,11},{10,... | collective-permute-start | bytes 258056 | tf_op jit(solution)/shard_map/ppermute | solution.py:233
  29.1 6.0 %collective-permute-start.14 = (bf16[16,2688]{1,0:T(8,128)(2,1)S(1)}, bf16[16,2688]{1,0:T(8,128)(2,1)S(1)}, u32[]{:S(2)}, u32[]{:S(2)}) collective-permute-start(bf16[16,2688]{1,0:T(8,128)(2,1)S(1)} %get-tuple-element.57), channel_id=1, source_target_pairs={{0,4},{4,0},{8,12},{12,8},{16,20},{20,16},{24,28},{28,24},{1,5},{5... | collective-permute-start | bytes 258056 | tf_op jit(solution)/shard_map/ppermute | solution.py:233
  29.9 6.1 %collective-permute-start.15 = (bf16[16,2688]{1,0:T(8,128)(2,1)S(1)}, bf16[16,2688]{1,0:T(8,128)(2,1)S(1)}, u32[]{:S(2)}, u32[]{:S(2)}) collective-permute-start(bf16[16,2688]{1,0:T(8,128)(2,1)S(1)} %get-tuple-element.58), channel_id=1, source_target_pairs={{0,6},{1,7},{2,4},{3,5},{4,2},{5,3},{6,0},{7,1},{8,14},{9,15},{10,... | collective-permute-start | bytes 258056 | tf_op jit(solution)/shard_map/ppermute | solution.py:233
  31.4 8.1 %collective-permute-start.18 = (bf16[16,2688]{1,0:T(8,128)(2,1)S(1)}, bf16[16,2688]{1,0:T(8,128)(2,1)S(1)}, u32[]{:S(2)}, u32[]{:S(2)}) collective-permute-start(bf16[16,2688]{1,0:T(8,128)(2,1)S(1)} %get-tuple-element.62), channel_id=1, source_target_pairs={{0,2},{1,3},{2,0},{3,1},{4,6},{5,7},{6,4},{7,5},{8,10},{9,11},{10,... | collective-permute-start | bytes 258056 | tf_op jit(solution)/shard_map/ppermute | solution.py:233
  32.6 6.8 %collective-permute-start.19 = (bf16[16,2688]{1,0:T(8,128)(2,1)S(1)}, bf16[16,2688]{1,0:T(8,128)(2,1)S(1)}, u32[]{:S(2)}, u32[]{:S(2)}) collective-permute-start(bf16[16,2688]{1,0:T(8,128)(2,1)S(1)} %get-tuple-element.63), channel_id=1, source_target_pairs={{0,4},{4,0},{8,12},{12,8},{16,20},{20,16},{24,28},{28,24},{1,5},{5... | collective-permute-start | bytes 258056 | tf_op jit(solution)/shard_map/ppermute | solution.py:233
  33.4 6.0 %collective-permute-start.20 = (bf16[16,2688]{1,0:T(8,128)(2,1)S(1)}, bf16[16,2688]{1,0:T(8,128)(2,1)S(1)}, u32[]{:S(2)}, u32[]{:S(2)}) collective-permute-start(bf16[16,2688]{1,0:T(8,128)(2,1)S(1)} %get-tuple-element.64), channel_id=1, source_target_pairs={{0,6},{1,7},{2,4},{3,5},{4,2},{5,3},{6,0},{7,1},{8,14},{9,15},{10,... | collective-permute-start | bytes 258056 | tf_op jit(solution)/shard_map/ppermute | solution.py:233
  36.1 6.5 %collective-permute-start.16 = (bf16[16,2688]{1,0:T(8,128)(2,1)S(1)}, bf16[16,2688]{1,0:T(8,128)(2,1)S(1)}, u32[]{:S(2)}, u32[]{:S(2)}) collective-permute-start(bf16[16,2688]{1,0:T(8,128)(2,1)S(1)} %get-tuple-element.59), channel_id=1, source_target_pairs={{0,24},{4,28},{8,16},{12,20},{16,8},{20,12},{24,0},{28,4},{1,25},{... | collective-permute-start | bytes 258056 | tf_op jit(solution)/shard_map/ppermute | solution.py:233
  39.4 6.0 %collective-permute-start.17 = (bf16[16,2688]{1,0:T(8,128)(2,1)S(1)}, bf16[16,2688]{1,0:T(8,128)(2,1)S(1)}, u32[]{:S(2)}, u32[]{:S(2)}) collective-permute-start(bf16[16,2688]{1,0:T(8,128)(2,1)S(1)} %get-tuple-element.60), channel_id=1, source_target_pairs={{0,16},{4,20},{8,24},{12,28},{16,0},{20,4},{24,8},{28,12},{1,17},{... | collective-permute-start | bytes 258056 | tf_op jit(solution)/shard_map/ppermute | solution.py:233
  39.5 6.1 %collective-permute-start.21 = (bf16[16,2688]{1,0:T(8,128)(2,1)S(1)}, bf16[16,2688]{1,0:T(8,128)(2,1)S(1)}, u32[]{:S(2)}, u32[]{:S(2)}) collective-permute-start(bf16[16,2688]{1,0:T(8,128)(2,1)S(1)} %get-tuple-element.65), channel_id=1, source_target_pairs={{0,8},{4,12},{8,0},{12,4},{16,24},{20,28},{24,16},{28,20},{1,9},{5... | collective-permute-start | bytes 258056 | tf_op jit(solution)/shard_map/ppermute | solution.py:233
  (1 other events, 23.5 us)
